TPU v7x, 32 devices: a whole 2x2x4 slice. The times are simulated.
32 devices in a mesh: hst: 8 (over z, x), doc: 4 (over y, core).
Axes of the slice: x: 2, y: 2, z: 4, core: 2. Of those that a mesh axis runs over, the one named last changes fastest.
Arguments:
- docs: bfloat16 [262144, 768], P(('hst', 'doc')), may hold values from -400 to 400, as said below
- w_in: bfloat16 [768, 256], replicated, may hold values from -0.21875 to 0.21875
- w_out: bfloat16 [256, 64], replicated, may hold values from -0.375 to 0.375
- doc_host: int32 [262144], P(('hst', 'doc')), may hold values from 0 to 2047
- tiles: bfloat16 [2048, 128, 128], P(('hst', 'doc')), may hold values from 0 to 10, as said below
- dst_block: int32 [2048], P(('hst', 'doc')), may hold values from 0 to 15
- src_block: int32 [2048], P(('hst', 'doc')), may hold values from 0 to 127
- tile_count: int32 [32], P(('hst', 'doc')), may hold values from 1 to 64, as said below
- teleport: int32 [16384], P('hst'), may hold values 0 or 1
Outputs:
- scores: float32 [16384, 64], P(('hst', 'doc'))
Inputs may be any that keep to these rules, and one draw needn't show every extreme that they name: `docs`: embeddings stay in the stated range. `tiles`: link weights are nonnegative. `tile_count`: some device uses all 64 slots.
All inputs are finite; a program needn't handle non-finite values. No bound on the sum of `teleport` on one device may be relied on, other than what follows from the above.
Results may differ from a plain program's by a relative error of at most 0.00066.
Values may be sent and summed in bfloat16 or wider, within the bound.
No kernel may reach another device: no remote copies, remote signals or barrier semaphores. Data moves between devices by JAX's collectives and lax.ppermute only.
A program may use at most 128 MiB of HBM per device.

v0:
```python
import functools

import jax
import jax.numpy as jnp
from jax import lax
from jax.experimental import pallas as pl
from jax.experimental.pallas import tpu as pltpu
from jax.sharding import PartitionSpec as P

HOPS = 3
LABELS = 3
DIGITS = 4
DOC_BLOCK = 1024
TILE_GROUP = 16
LIFT = 2.0**64
NT = (((1,), (1,)), ((), ()))
MIB = 1 << 20


def xor_send(value, axis, step):
    size = lax.axis_size(axis)
    return lax.ppermute(value, axis, [(i, i ^ step) for i in range(size)])


def column_sum_kernel(source, count, tiles, out, total):
    step = pl.program_id(0)
    parts, rows, _ = out.shape

    @pl.when(step == 0)
    def _():
        total[...] = jnp.zeros_like(total)

    for i in range(TILE_GROUP):
        k = step * TILE_GROUP + i
        row = jnp.where(k < count[0], source[k], parts * rows)
        part = jnp.sum(tiles[i].astype(jnp.float32), axis=0, keepdims=True)
        total[pl.ds(row, 1), :] += part

    @pl.when(step == pl.num_programs(0) - 1)
    def _():
        for j in range(parts):
            out[j] = total[j * rows : (j + 1) * rows, :]


def column_sums(source, count, tiles, parts, rows):
    slots, block, _ = tiles.shape
    shape = (parts, rows, block)
    return pl.pallas_call(
        column_sum_kernel,
        grid_spec=pltpu.PrefetchScalarGridSpec(
            num_scalar_prefetch=2,
            grid=(slots // TILE_GROUP,),
            in_specs=[pl.BlockSpec((TILE_GROUP, block, block), lambda i, s, c: (i, 0, 0))],
            out_specs=pl.BlockSpec(shape, lambda i, s, c: (0, 0, 0)),
            scratch_shapes=[pltpu.VMEM((parts * rows + 8, block), jnp.float32)],
        ),
        out_shape=jax.ShapeDtypeStruct(shape, jnp.float32),
        compiler_params=pltpu.CompilerParams(vmem_limit_bytes=16 * MIB),
        cost_estimate=pl.CostEstimate(
            flops=tiles.size, bytes_accessed=tiles.size * 2, transcendentals=0
        ),
        name="column_sums",
    )(source, count, tiles)


def block_topics(docs, w_in, w_out_t, host, width):
    hidden = jax.nn.gelu(
        jnp.dot(docs[...], w_in[...], preferred_element_type=jnp.float32), approximate=True
    ).astype(jnp.bfloat16)
    logits = lax.dot_general(w_out_t[...], hidden, NT, preferred_element_type=jnp.float32)
    powers = jnp.exp(logits - jnp.max(logits, axis=0, keepdims=True))
    probs = powers * (1.0 / jnp.sum(powers, axis=0, keepdims=True))
    high = probs.astype(jnp.bfloat16)
    low = (probs - high.astype(jnp.float32)).astype(jnp.bfloat16)
    index = host[0]
    digit = index // width
    within = index - digit * width
    picks = [jnp.where(digit == j, 1.0, 0.0).astype(jnp.bfloat16) for j in range(DIGITS)]
    left = jnp.concatenate([high * p for p in picks] + [low * p for p in picks], axis=0)
    places = lax.broadcasted_iota(jnp.int32, (width, index.shape[1]), 0)
    right = jnp.where(places == within, 1.0, 0.0).astype(jnp.bfloat16)
    return lax.dot_general(left, right, NT, preferred_element_type=jnp.float32)


def documents_kernel(place, docs, w_in, w_out_t, host, degrees, *rest):
    labels, outs, total = rest[:LABELS], rest[LABELS:-1], rest[-1]
    step = pl.program_id(0)
    topics = w_out_t.shape[0]
    width = total.shape[1]
    added = block_topics(docs, w_in, w_out_t, host, width)

    @pl.when(step == 0)
    def _():
        total[...] = added

    @pl.when(step > 0)
    def _():
        total[...] += added

    @pl.when(step == pl.num_programs(0) - 1)
    def _():
        per = outs[0].shape[0]
        hosts = DIGITS * width
        degree = sum(degrees[j] for j in range(1, degrees.shape[0])) + degrees[0]
        blocks, block = degree.shape
        wide = hosts + blocks // per * block
        for j, out in enumerate(outs):
            chunk = (place[0] ^ j) * per
            for d in range(DIGITS):
                first = pl.ds(pl.multiple_of(d * topics + chunk, 8), per)
                second = pl.ds(pl.multiple_of((DIGITS + d) * topics + chunk, 8), per)
                out[:, d * width : (d + 1) * width] = total[first, :] + total[second, :]
            for c in range(blocks // per):
                cols = slice(hosts + c * block, hosts + (c + 1) * block)
                out[:, cols] = degree[c * per : (c + 1) * per, :]
            out[:, wide:] = jnp.zeros((per, block), jnp.float32)
            for r, label in enumerate(labels):
                out[r : r + 1, wide : wide + label.shape[1]] = label[...].astype(jnp.float32)


def documents(docs, w_in, w_out, doc_host, hosts, split, place, degrees, labels):
    count, depth = docs.shape
    hid, topics = w_out.shape
    per = topics // split
    width = hosts // DIGITS
    steps = count // DOC_BLOCK
    shape = (per, hosts + hosts // per + degrees.shape[2])
    return pl.pallas_call(
        documents_kernel,
        grid_spec=pltpu.PrefetchScalarGridSpec(
            num_scalar_prefetch=1,
            grid=(steps,),
            in_specs=[
                pl.BlockSpec((DOC_BLOCK, depth), lambda i, p: (i, 0)),
                pl.BlockSpec((depth, hid), lambda i, p: (0, 0)),
                pl.BlockSpec((topics, hid), lambda i, p: (0, 0)),
                pl.BlockSpec((1, 1, DOC_BLOCK), lambda i, p: (i, 0, 0)),
                pl.BlockSpec(degrees.shape, lambda i, p: (0, 0, 0)),
            ]
            + [pl.BlockSpec(label.shape, lambda i, p: (0, 0)) for label in labels],
            out_specs=[pl.BlockSpec(shape, lambda i, p: (0, 0))] * split,
            scratch_shapes=[pltpu.VMEM((2 * DIGITS * topics, width), jnp.float32)],
        ),
        out_shape=[jax.ShapeDtypeStruct(shape, jnp.float32)] * split,
        compiler_params=pltpu.CompilerParams(vmem_limit_bytes=48 * MIB),
        cost_estimate=pl.CostEstimate(
            flops=2 * count * (depth * hid + hid * topics + 2 * topics * hosts),
            bytes_accessed=docs.size * 2,
            transcendentals=count * (hid + topics),
        ),
        name="documents",
    )(place, docs, w_in, w_out.T, doc_host.reshape(steps, 1, DOC_BLOCK), degrees, *labels)


def start_kernel(held, teleport, *rest):
    sums, rest = rest[: len(rest) - 2 * held - 4], rest[len(rest) - held - 4 :]
    sent, start, inverse, meta = rest[:4]
    per, hosts = start.shape
    blocks, block = teleport.shape
    member = teleport[...].astype(jnp.float32) * LIFT
    mass = jnp.zeros((per, 1), jnp.float32)
    tail = slice(hosts, hosts + hosts // per)
    packed = 1.0 / jnp.maximum(sum(s[:, tail] for s in sums[1:]) + sums[0][:, tail], 1.0)
    for c in range(blocks // per):
        inverse[c * per : (c + 1) * per, :] = packed[:, c * block : (c + 1) * block]
    for j, s in enumerate(sums):
        meta[j * LABELS : (j + 1) * LABELS, :] = s[:LABELS, tail.stop :].astype(jnp.int32)
    for b in range(blocks):
        cols = slice(b * block, (b + 1) * block)
        value = sum(s[:, cols] for s in sums[1:]) + sums[0][:, cols]
        value = value * member[b : b + 1, :]
        start[:, cols] = value
        sent[:, cols] = (value * inverse[b : b + 1, :]).astype(jnp.bfloat16)
        mass = mass + jnp.sum(value, axis=1, keepdims=True)
    lane = lax.broadcasted_iota(jnp.int32, (per, block), 1)
    first = mass.astype(jnp.bfloat16).astype(jnp.float32)
    second = (mass - first).astype(jnp.bfloat16).astype(jnp.float32)
    third = mass - first - second
    pieces = jnp.where(
        lane == 0, first, jnp.where(lane == 1, second, jnp.where(lane == 2, third, 0.0))
    )
    sent[:, blocks * block :] = pieces.astype(jnp.bfloat16)


def start_values(teleport, sums, block, held):
    per, _ = sums[0].shape
    hosts = teleport.shape[0]
    vmem = pl.BlockSpec(memory_space=pltpu.VMEM)
    keep = pl.BlockSpec(memory_space=pl.ANY)
    return pl.pallas_call(
        functools.partial(start_kernel, len(held)),
        in_specs=[vmem] * (1 + len(sums)) + [keep] * len(held),
        out_specs=[vmem] * 4 + [keep] * len(held),
        out_shape=[
            jax.ShapeDtypeStruct((per, hosts + block), jnp.bfloat16),
            jax.ShapeDtypeStruct((per, hosts), jnp.float32),
            jax.ShapeDtypeStruct((hosts // block, block), jnp.float32),
            jax.ShapeDtypeStruct((len(sums) * LABELS, block), jnp.int32),
        ]
        + [jax.ShapeDtypeStruct(array.shape, array.dtype) for array in held],
        input_output_aliases={1 + len(sums) + i: 4 + i for i in range(len(held))},
        compiler_params=pltpu.CompilerParams(vmem_limit_bytes=16 * MIB),
        name="start_values",
    )(teleport.reshape(hosts // block, block), *sums, *held)


def after_kernel(*refs):
    del refs


def after(value, ready):
    keep = pl.BlockSpec(memory_space=pl.ANY)
    return pl.pallas_call(
        after_kernel,
        in_specs=[keep] * (1 + len(ready)),
        out_specs=keep,
        out_shape=jax.ShapeDtypeStruct(value.shape, value.dtype),
        input_output_aliases={0: 0},
        name="after",
    )(value, *ready)


def hop_kernel(first, last, parts, spans, scale, meta, here, *rest):
    shards, rest = rest[:parts][::-1], rest[parts:]
    chunks, rest = rest[: len(spans)], rest[len(spans) :]
    (tele, inverse), outs, (slabs, inflow) = rest[:2], rest[2:-2], rest[-2:]
    blocks, per, block = inflow.shape
    step = pl.program_id(0)

    @pl.when(step == 0)
    def _():
        inflow[...] = jnp.zeros_like(inflow)
        slabs[parts * blocks] = jnp.zeros(slabs.shape[1:], slabs.dtype)
        for j, shard in enumerate(shards):
            for b in range(blocks):
                slabs[j * blocks + b] = shard[:, b * block : (b + 1) * block]

    empty = jnp.zeros((per, block), jnp.bfloat16)
    for tiles, (q, begin, end) in zip(chunks, spans):
        count = meta[q * LABELS + 2, 0]
        within = jnp.logical_and(step >= begin, step < end)

        @pl.when(jnp.logical_and(within, step * TILE_GROUP < count))
        def _():
            products = []
            for c in range(0, TILE_GROUP, 4):
                held = []
                for i in range(4):
                    k = step * TILE_GROUP + c + i
                    source = meta[q * LABELS, k] ^ here[0]
                    held.append(slabs[jnp.where(k < count, source, parts * blocks)])
                left = jnp.concatenate(
                    [
                        jnp.concatenate([held[0], held[1], empty, empty], axis=0),
                        jnp.concatenate([empty, empty, held[2], held[3]], axis=0),
                    ],
                    axis=1,
                )
                right = jnp.concatenate(
                    [
                        tiles[c : c + 2].reshape(2 * block, block),
                        tiles[c + 2 : c + 4].reshape(2 * block, block),
                    ],
                    axis=1,
                )
                both = lax.dot_general(left, right, NT, preferred_element_type=jnp.float32)
                for i in range(4):
                    side = (i % 2) * block
                    products.append(both[i * per : (i + 1) * per, side : side + block])
            for i in range(TILE_GROUP):
                inflow[meta[q * LABELS + 1, step * TILE_GROUP + i]] += products[i]

    @pl.when(step == pl.num_programs(0) - 1)
    def _():
        if first:
            tail = sum(s[:, blocks * block :].astype(jnp.float32) for s in shards)
            mass = jnp.sum(tail, axis=1, keepdims=True)
        for b in range(blocks):
            cols = slice(b * block, (b + 1) * block)
            own = tele[:, cols]
            state = 0.85 * inflow[b] + 0.15 * own
            if first:
                state = state / mass
                outs[1][:, cols] = own / mass
            if last:
                inflow[b] = state * scale
            else:
                outs[0][:, cols] = (state * inverse[b : b + 1, :]).astype(jnp.bfloat16)
        if last:
            count = outs[0].shape[1] // block
            for j, out in enumerate(outs):
                begin = (here[1] ^ j) * count
                for i in range(count):
                    out[:, i * block : (i + 1) * block] = inflow[begin + i]


def hop(first, last, meta, here, shards, sets, tele, inverse):
    per, hosts = tele.shape
    slots = sum(chunk.shape[0] for chunk in sets[0])
    block = sets[0][0].shape[1]
    blocks = hosts // block
    parts, split = len(shards), len(sets)
    chunks, spans = [], []
    for q, held in enumerate(sets):
        begin = 0
        for chunk in held:
            end = begin + chunk.shape[0] // TILE_GROUP
            chunks.append(chunk)
            spans.append((q, begin, end))
            begin = end

    def stream(span):
        _, begin, end = span
        return pl.BlockSpec(
            (TILE_GROUP, block, block),
            lambda i, m, p: (jnp.clip(i - begin, 0, end - begin - 1), 0, 0),
        )

    if last:
        out_shape = [jax.ShapeDtypeStruct((per, hosts // split), jnp.float32)] * split
    else:
        out_shape = [jax.ShapeDtypeStruct((per, hosts), jnp.bfloat16)]
        if first:
            out_shape.append(jax.ShapeDtypeStruct((per, hosts), jnp.float32))

    def whole(array):
        return pl.BlockSpec(array.shape, lambda i, m, p: (0,) * len(array.shape))

    return pl.pallas_call(
        functools.partial(hop_kernel, first, last, parts, spans, float(parts * hosts)),
        grid_spec=pltpu.PrefetchScalarGridSpec(
            num_scalar_prefetch=2,
            grid=(slots // TILE_GROUP,),
            in_specs=[whole(s) for s in reversed(shards)]
            + [stream(span) for span in spans]
            + [whole(tele), whole(inverse)],
            out_specs=[whole(s) for s in out_shape],
            scratch_shapes=[
                pltpu.VMEM((parts * blocks + 1, per, block), jnp.bfloat16),
                pltpu.VMEM((blocks, per, block), jnp.float32),
            ],
        ),
        out_shape=out_shape,
        compiler_params=pltpu.CompilerParams(vmem_limit_bytes=16 * MIB),
        cost_estimate=pl.CostEstimate(
            flops=2 * split * slots * block * block * per,
            bytes_accessed=split * slots * block * block * 2,
            transcendentals=0,
        ),
        name="hop",
    )(meta, here, *reversed(shards), *chunks, tele, inverse)


def finish_kernel(here, *rest):
    chunks, out = rest[:-1], rest[-1]
    per = chunks[0].shape[0]
    for j, chunk in enumerate(chunks):
        out[pl.ds(pl.multiple_of((here[1] ^ j) * per, 8), per), :] = chunk[...]


def finish(here, chunks):
    per, rows = chunks[0].shape
    topics = per * len(chunks)
    return pl.pallas_call(
        finish_kernel,
        in_specs=[pl.BlockSpec(memory_space=pltpu.SMEM)]
        + [pl.BlockSpec(memory_space=pltpu.VMEM)] * len(chunks),
        out_shape=jax.ShapeDtypeStruct((topics, rows), jnp.float32),
        compiler_params=pltpu.CompilerParams(vmem_limit_bytes=16 * MIB),
        name="finish",
    )(here, *chunks)


def spread(sent, axis):
    size = lax.axis_size(axis)
    held = {0: sent}
    for j in range(size - 2, 2, -2):
        held[j] = xor_send(sent, axis, j)
    held[1] = xor_send(sent, axis, 1)
    held[2] = xor_send(sent, axis, 2)
    for j in range(size - 2, 0, -2):
        held[j + 1] = xor_send(held[j], axis, 1)
    return [held[j] for j in range(size)]


def body(docs, w_in, w_out, doc_host, tiles, dst_block, src_block, tile_count, teleport):
    hosts = teleport.shape[0]
    slots, block, _ = tiles.shape
    parts, split = lax.axis_size("hst"), lax.axis_size("doc")
    blocks = hosts // block
    place = lax.axis_index("doc").astype(jnp.int32)
    here = jnp.stack([lax.axis_index("hst").astype(jnp.int32) * blocks, place])
    labels = [label.reshape(1, -1) for label in (src_block, dst_block, tile_count)]

    near = xor_send(tiles, "doc", 1)
    cut = 3 * slots // 4
    early, late = tiles[:cut], tiles[cut:]
    far = {j: [xor_send(early, "doc", j)] for j in range(2, split, 2)}
    degrees = column_sums(src_block, tile_count, tiles, parts, blocks)
    degrees = lax.all_to_all(degrees, "hst", split_axis=0, concat_axis=0, tiled=True)
    sums = documents(docs, w_in, w_out, doc_host, hosts, split, place.reshape(1), degrees, labels)
    sums = [sums[0]] + [xor_send(sums[j], "doc", j) for j in range(1, split)]
    crossed = [far[j][0] for j in range(2, split, 2)]
    sent, tele, inverse, meta, late, *crossed = start_values(
        teleport, sums, block, [late] + crossed
    )
    for j in range(2, split, 2):
        far[j] = [crossed[j // 2 - 1], xor_send(late, "doc", j)]
        far[j + 1] = [xor_send(far[j][0], "doc", 1)]
    for step in range(HOPS):
        first, last = step == 0, step == HOPS - 1
        shards = spread(sent, "hst")
        if first:
            for j in range(2, split, 2):
                far[j][1] = after(far[j][1], shards[1:-1])
                far[j + 1].append(xor_send(far[j][1], "doc", 1))
            sets = [[tiles], [near]] + [far[j] for j in range(2, split)]
        outs = hop(first, last, meta, here, shards, sets, tele, inverse)
        sent = outs[0]
        if first:
            tele = outs[1]
    chunks = [outs[0]] + [xor_send(outs[j], "doc", j) for j in range(1, split)]
    return finish(here, chunks).T


def solution(mesh):
    placed = (
        P(("hst", "doc"), None),
        P(),
        P(),
        P(("hst", "doc")),
        P(("hst", "doc"), None, None),
        P(("hst", "doc")),
        P(("hst", "doc")),
        P(("hst", "doc")),
        P("hst"),
    )
    return jax.shard_map(
        body, mesh=mesh, in_specs=placed, out_specs=P(("hst", "doc"), None), check_vma=False
    )
```

profile of v0, /device:TPU:0, one launch (start us, length us, event | category | flops | bytes accessed | tf_op | source)
XLA Modules:
  0.0 130.3 jit_solution(9492862163445217084)
XLA Ops:
  0.0 2.9 %slice.7 = bf16[48,128,128]{2,1,0:T(8,128)(2,1)} slice(bf16[64,128,128]{2,1,0:T(8,128)(2,1)} %rest_8_.5), slice={[0:48], [0:128], [0:128]} | slice | bytes 3145728 | tf_op jit(solution)/shard_map/slice | solution.py:397
  2.9 3.0 %collective-permute-start.3 = (bf16[48,128,128]{2,1,0:T(8,128)(2,1)}, bf16[48,128,128]{2,1,0:T(8,128)(2,1)}, u32[]{:S(2)}, u32[]{:S(2)}) collective-permute-start(bf16[48,128,128]{2,1,0:T(8,128)(2,1)} %slice.7), channel_id=1, source_target_pairs={{0,2},{1,3},{2,0},{3,1},{4,6},{5,7},{6,4},{7,5},{8,10},{9,11},{10,... | collective-permute-start | bytes 4718600 | tf_op jit(solution)/shard_map/ppermute | solution.py:22
  6.6 1.7 %column_sums.1 = f32[8,16,128]{2,1,0:T(8,128)} custom-call(s32[64]{0:T(128)S(1)} %copy-done.16, s32[1]{0:T(128)} %copy.16.count, bf16[64,128,128]{2,1,0:T(8,128)(2,1)S(1)} %copy-done), custom_call_target="tpu_custom_call" | custom-call | flops 1048576 | bytes 2097152 | tf_op jit(solution)/shard_map/column_sums/pallas_call | solution.py:48
  8.3 5.8 %all-to-all-start = ((f32[8,16,128]{2,1,0:T(8,128)}), f32[8,16,128]{2,1,0:T(8,128)S(1)}, u32[]{:S(2)}, u32[]{:S(2)}) async-start(f32[8,16,128]{2,1,0:T(8,128)} %column_sums.1), calls=%async_computation | async-start | bytes 131072 | tf_op jit(solution)/shard_map/all_to_all | solution.py:400
  14.1 6.9 %all-to-all-done.degrees = f32[8,16,128]{2,1,0:T(8,128)S(1)} async-done(((f32[8,16,128]{2,1,0:T(8,128)}), f32[8,16,128]{2,1,0:T(8,128)S(1)}, u32[]{:S(2)}, u32[]{:S(2)}) %all-to-all-start) | async-done | bytes 65568 | tf_op jit(solution)/shard_map/all_to_all | solution.py:400
  21.0 15.1 %documents.1 = (f32[16,2304]{1,0:T(8,128)S(1)}, f32[16,2304]{1,0:T(8,128)S(1)}, f32[16,2304]{1,0:T(8,128)S(1)}, f32[16,2304]{1,0:T(8,128)S(1)}) custom-call(s32[1]{0:T(128)} %bitcast.1.place, bf16[8192,768]{1,0:T(8,128)(2,1)} %docs.1, bf16[768,256]{1,0:T(8,128)(2,1)S(1)} %copy-done.17, bf16[64,256]{1,0:T(8,128)(2,1)S(1)} %bitcast.12, ...), custom_call_target="tpu_custom_call" | custom-call | flops 7784628224 | bytes 12582912 | tf_op jit(solution)/shard_map/documents/pallas_call | solution.py:128
  36.2 0.1 collective-permute-start
  36.2 0.6 collective-permute-start.1
  36.8 1.3 collective-permute-start.2
  38.2 6.4 %collective-permute-done.1.rest_2_ = f32[16,2304]{1,0:T(8,128)S(1)} collective-permute-done((f32[16,2304]{1,0:T(8,128)S(1)}, f32[16,2304]{1,0:T(8,128)S(1)}, u32[]{:S(2)}, u32[]{:S(2)}) %collective-permute-start.1) | collective-permute-done | bytes 147488 | tf_op jit(solution)/shard_map/ppermute | solution.py:22
  44.5 1.6 %collective-permute-done.2.rest_3_ = f32[16,2304]{1,0:T(8,128)S(1)} collective-permute-done((f32[16,2304]{1,0:T(8,128)S(1)}, f32[16,2304]{1,0:T(8,128)S(1)}, u32[]{:S(2)}, u32[]{:S(2)}) %collective-permute-start.2) | collective-permute-done | bytes 147488 | tf_op jit(solution)/shard_map/ppermute | solution.py:22
  46.1 0.1 start_values.1
  46.2 0.6 collective-permute-start.13
  46.9 1.7 %collective-permute-start.12 = (bf16[16,128,128]{2,1,0:T(8,128)(2,1)S(1)}, bf16[16,128,128]{2,1,0:T(8,128)(2,1)S(1)}, u32[]{:S(2)}, u32[]{:S(2)}) collective-permute-start(bf16[16,128,128]{2,1,0:T(8,128)(2,1)S(1)} %get-tuple-element.28), channel_id=1, source_target_pairs={{0,2},{1,3},{2,0},{3,1},{4,6},{5,7},{6,4},{7,5},{8,10},{9,11},{10,... | collective-permute-start | bytes 1572872 | tf_op jit(solution)/shard_map/ppermute | solution.py:22
  48.6 1.5 %collective-permute-start.10 = (bf16[16,2176]{1,0:T(8,128)(2,1)S(1)}, bf16[16,2176]{1,0:T(8,128)(2,1)S(1)}, u32[]{:S(2)}, u32[]{:S(2)}) collective-permute-start(bf16[16,2176]{1,0:T(8,128)(2,1)S(1)} %get-tuple-element.26.rest_7_), channel_id=1, source_target_pairs={{0,4},{4,0},{8,12},{12,8},{16,20},{20,16},{24,28},{28,24},{1,5},{5... | collective-permute-start | bytes 208904 | tf_op jit(solution)/shard_map/ppermute | solution.py:22
  50.1 1.6 %collective-permute-start.8 = (bf16[16,2176]{1,0:T(8,128)(2,1)S(1)}, bf16[16,2176]{1,0:T(8,128)(2,1)S(1)}, u32[]{:S(2)}, u32[]{:S(2)}) collective-permute-start(bf16[16,2176]{1,0:T(8,128)(2,1)S(1)} %get-tuple-element.26.rest_7_), channel_id=1, source_target_pairs={{0,8},{4,12},{8,0},{12,4},{16,24},{20,28},{24,16},{28,20},{1,9},{5... | collective-permute-start | bytes 208904 | tf_op jit(solution)/shard_map/ppermute | solution.py:22
  51.7 1.2 collective-permute-done.10.refs_1_.rest_6_
  52.9 2.6 %collective-permute-start.6 = (bf16[16,2176]{1,0:T(8,128)(2,1)S(1)}, bf16[16,2176]{1,0:T(8,128)(2,1)S(1)}, u32[]{:S(2)}, u32[]{:S(2)}) collective-permute-start(bf16[16,2176]{1,0:T(8,128)(2,1)S(1)} %get-tuple-element.26.rest_7_), channel_id=1, source_target_pairs={{0,16},{4,20},{8,24},{12,28},{16,0},{20,4},{24,8},{28,12},{1,17},{... | collective-permute-start | bytes 208904 | tf_op jit(solution)/shard_map/ppermute | solution.py:22
  55.5 2.5 %collective-permute-start.4 = (bf16[16,2176]{1,0:T(8,128)(2,1)S(1)}, bf16[16,2176]{1,0:T(8,128)(2,1)S(1)}, u32[]{:S(2)}, u32[]{:S(2)}) collective-permute-start(bf16[16,2176]{1,0:T(8,128)(2,1)S(1)} %get-tuple-element.26.rest_7_), channel_id=1, source_target_pairs={{0,24},{4,28},{8,16},{12,20},{16,8},{20,12},{24,0},{28,4},{1,25},{... | collective-permute-start | bytes 208904 | tf_op jit(solution)/shard_map/ppermute | solution.py:22
  58.0 2.0 %collective-permute-done.6.refs_4_.rest_3_ = bf16[16,2176]{1,0:T(8,128)(2,1)S(1)} collective-permute-done((bf16[16,2176]{1,0:T(8,128)(2,1)S(1)}, bf16[16,2176]{1,0:T(8,128)(2,1)S(1)}, u32[]{:S(2)}, u32[]{:S(2)}) %collective-permute-start.6) | collective-permute-done | bytes 69664 | tf_op jit(solution)/shard_map/ppermute | solution.py:22
  60.1 1.5 %collective-permute-start.9 = (bf16[16,2176]{1,0:T(8,128)(2,1)S(1)}, bf16[16,2176]{1,0:T(8,128)(2,1)S(1)}, u32[]{:S(2)}, u32[]{:S(2)}) collective-permute-start(bf16[16,2176]{1,0:T(8,128)(2,1)S(1)} %collective-permute-done.8.refs_2_.rest_5_), channel_id=1, source_target_pairs={{0,4},{4,0},{8,12},{12,8},{16,20},{20,16},{24,28},{28,24},{1,5},{5... | collective-permute-start | bytes 208904 | tf_op jit(solution)/shard_map/ppermute | solution.py:22
  61.5 0.2 collective-permute-done.4.refs_6_.rest_1_
  61.7 1.5 %collective-permute-start.7 = (bf16[16,2176]{1,0:T(8,128)(2,1)S(1)}, bf16[16,2176]{1,0:T(8,128)(2,1)S(1)}, u32[]{:S(2)}, u32[]{:S(2)}) collective-permute-start(bf16[16,2176]{1,0:T(8,128)(2,1)S(1)} %collective-permute-done.6.refs_4_.rest_3_), channel_id=1, source_target_pairs={{0,4},{4,0},{8,12},{12,8},{16,20},{20,16},{24,28},{28,24},{1,5},{5... | collective-permute-start | bytes 208904 | tf_op jit(solution)/shard_map/ppermute | solution.py:22
  63.2 1.1 collective-permute-done.9.refs_3_.rest_4_
  64.4 1.7 %collective-permute-done.7.refs_5_.rest_2_ = bf16[16,2176]{1,0:T(8,128)(2,1)S(1)} collective-permute-done((bf16[16,2176]{1,0:T(8,128)(2,1)S(1)}, bf16[16,2176]{1,0:T(8,128)(2,1)S(1)}, u32[]{:S(2)}, u32[]{:S(2)}) %collective-permute-start.7) | collective-permute-done | bytes 69664 | tf_op jit(solution)/shard_map/ppermute | solution.py:22
  66.1 0.6 copy-done.13
  66.7 0.8 copy-done.1
  67.5 1.5 %collective-permute-start.5 = (bf16[16,2176]{1,0:T(8,128)(2,1)}, bf16[16,2176]{1,0:T(8,128)(2,1)S(1)}, u32[]{:S(2)}, u32[]{:S(2)}) collective-permute-start(bf16[16,2176]{1,0:T(8,128)(2,1)} %copy-done.9), channel_id=1, source_target_pairs={{0,4},{4,0},{8,12},{12,8},{16,20},{20,16},{24,28},{28,24},{1,5},{5... | collective-permute-start | bytes 208904 | tf_op jit(solution)/shard_map/ppermute | solution.py:22
  69.0 0.1 pad_add_fusion.here
  69.1 3.2 %collective-permute-done.5.rest_0_ = bf16[16,2176]{1,0:T(8,128)(2,1)S(1)} collective-permute-done((bf16[16,2176]{1,0:T(8,128)(2,1)}, bf16[16,2176]{1,0:T(8,128)(2,1)S(1)}, u32[]{:S(2)}, u32[]{:S(2)}) %collective-permute-start.5) | collective-permute-done | bytes 69664 | tf_op jit(solution)/shard_map/ppermute | solution.py:22
  72.3 1.0 copy-done.2
  73.3 0.9 copy-done.4
  74.2 0.9 copy-done.6
  75.1 0.9 copy-done.8
  76.0 0.9 copy-done.10
  76.9 0.9 copy-done.12
  77.8 0.9 copy-done.14
  78.6 5.9 %hop.3 = (bf16[16,2048]{1,0:T(8,128)(2,1)S(1)}, f32[16,2048]{1,0:T(8,128)S(1)}) custom-call(s32[12,128]{1,0:T(8,128)S(1)} %get-tuple-element.25.meta, s32[2]{0:T(128)S(1)} %pad_add_fusion.here, bf16[16,2176]{1,0:T(8,128)(2,1)S(1)} %collective-permute-done.5.rest_0_, bf16[16,2176]{1,0:T(8,128)(2,1)S(1)} %copy-done.10, bf16[16,2176]{1,0:T(8,128)(2,1)S(1)} %copy-done.14, ...), custom_call_target="tpu_custom_call" | custom-call | flops 134217728 | bytes 8388608 | tf_op jit(solution)/shard_map/hop/pallas_call | solution.py:329
  84.6 0.3 collective-permute-start.19
  84.9 4.3 %collective-permute-start.17 = (bf16[16,2048]{1,0:T(8,128)(2,1)S(1)}, bf16[16,2048]{1,0:T(8,128)(2,1)S(1)}, u32[]{:S(2)}, u32[]{:S(2)}) collective-permute-start(bf16[16,2048]{1,0:T(8,128)(2,1)S(1)} %get-tuple-element.31.rest_7_), channel_id=1, source_target_pairs={{0,16},{4,20},{8,24},{12,28},{16,0},{20,4},{24,8},{28,12},{1,17},{... | collective-permute-start | bytes 196616 | tf_op jit(solution)/shard_map/ppermute | solution.py:22
  89.2 1.1 collective-permute-start.21
  90.3 1.0 collective-permute-start.20
  91.2 2.5 %collective-permute-done.17.rest_3_ = bf16[16,2048]{1,0:T(8,128)(2,1)S(1)} collective-permute-done((bf16[16,2048]{1,0:T(8,128)(2,1)S(1)}, bf16[16,2048]{1,0:T(8,128)(2,1)S(1)}, u32[]{:S(2)}, u32[]{:S(2)}) %collective-permute-start.17) | collective-permute-done | bytes 65568 | tf_op jit(solution)/shard_map/ppermute | solution.py:22
  93.7 0.5 collective-permute-start.18
  94.2 1.1 collective-permute-done.15.rest_1_
  95.3 0.5 collective-permute-start.16
  95.8 2.2 %collective-permute-done.18.rest_2_ = bf16[16,2048]{1,0:T(8,128)(2,1)S(1)} collective-permute-done((bf16[16,2048]{1,0:T(8,128)(2,1)S(1)}, bf16[16,2048]{1,0:T(8,128)(2,1)S(1)}, u32[]{:S(2)}, u32[]{:S(2)}) %collective-permute-start.18) | collective-permute-done | bytes 65568 | tf_op jit(solution)/shard_map/ppermute | solution.py:22
  98.0 1.6 %collective-permute-done.16.rest_0_ = bf16[16,2048]{1,0:T(8,128)(2,1)S(1)} collective-permute-done((bf16[16,2048]{1,0:T(8,128)(2,1)S(1)}, bf16[16,2048]{1,0:T(8,128)(2,1)S(1)}, u32[]{:S(2)}, u32[]{:S(2)}) %collective-permute-start.16) | collective-permute-done | bytes 65568 | tf_op jit(solution)/shard_map/ppermute | solution.py:22
  99.5 5.9 %hop.4.rest_7_ = bf16[16,2048]{1,0:T(8,128)(2,1)S(1)} custom-call(s32[12,128]{1,0:T(8,128)S(1)} %get-tuple-element.25.meta, s32[2]{0:T(128)S(1)} %pad_add_fusion.here, bf16[16,2048]{1,0:T(8,128)(2,1)S(1)} %collective-permute-done.16.rest_0_, bf16[16,2048]{1,0:T(8,128)(2,1)S(1)} %collective-permute-done.15.rest_1_, ...), custom_call_target="tpu_custom_call" | custom-call | flops 134217728 | bytes 8388608 | tf_op jit(solution)/shard_map/hop/pallas_call | solution.py:329
  105.5 3.1 %collective-permute-start.24 = (bf16[16,2048]{1,0:T(8,128)(2,1)S(1)}, bf16[16,2048]{1,0:T(8,128)(2,1)S(1)}, u32[]{:S(2)}, u32[]{:S(2)}) collective-permute-start(bf16[16,2048]{1,0:T(8,128)(2,1)S(1)} %hop.4.rest_7_), channel_id=1, source_target_pairs={{0,16},{4,20},{8,24},{12,28},{16,0},{20,4},{24,8},{28,12},{1,17},{... | collective-permute-start | bytes 196616 | tf_op jit(solution)/shard_map/ppermute | solution.py:22
  108.6 1.2 collective-permute-start.22
  109.9 0.2 collective-permute-start.28
  110.0 1.1 collective-permute-done.26.rest_5_
  111.2 0.7 collective-permute-start.27
  111.9 1.3 collective-permute-start.25
  113.2 1.5 %collective-permute-done.22.rest_1_ = bf16[16,2048]{1,0:T(8,128)(2,1)S(1)} collective-permute-done((bf16[16,2048]{1,0:T(8,128)(2,1)S(1)}, bf16[16,2048]{1,0:T(8,128)(2,1)S(1)}, u32[]{:S(2)}, u32[]{:S(2)}) %collective-permute-start.22) | collective-permute-done | bytes 65568 | tf_op jit(solution)/shard_map/ppermute | solution.py:22
  114.7 1.0 collective-permute-start.23
  115.7 0.5 collective-permute-done.25.rest_2_
  116.2 2.8 %collective-permute-done.23.rest_0_ = bf16[16,2048]{1,0:T(8,128)(2,1)S(1)} collective-permute-done((bf16[16,2048]{1,0:T(8,128)(2,1)S(1)}, bf16[16,2048]{1,0:T(8,128)(2,1)S(1)}, u32[]{:S(2)}, u32[]{:S(2)}) %collective-permute-start.23) | collective-permute-done | bytes 65568 | tf_op jit(solution)/shard_map/ppermute | solution.py:22
  119.0 5.9 %hop.5 = (f32[16,512]{1,0:T(8,128)S(1)}, f32[16,512]{1,0:T(8,128)S(1)}, f32[16,512]{1,0:T(8,128)S(1)}, f32[16,512]{1,0:T(8,128)S(1)}) custom-call(s32[12,128]{1,0:T(8,128)S(1)} %get-tuple-element.25.meta, s32[2]{0:T(128)S(1)} %pad_add_fusion.here, bf16[16,2048]{1,0:T(8,128)(2,1)S(1)} %collective-permute-done.23.rest_0_, ...), custom_call_target="tpu_custom_call" | custom-call | flops 134217728 | bytes 8388608 | tf_op jit(solution)/shard_map/hop/pallas_call | solution.py:329
  124.9 0.5 collective-permute-start.30
  125.4 1.3 %collective-permute-start.31 = (f32[16,512]{1,0:T(8,128)S(1)}, f32[16,512]{1,0:T(8,128)S(1)}, u32[]{:S(2)}, u32[]{:S(2)}) collective-permute-start(f32[16,512]{1,0:T(8,128)S(1)} %get-tuple-element.36), channel_id=1, source_target_pairs={{0,3},{1,2},{2,1},{3,0},{4,7},{5,6},{6,5},{7,4},{8,11},{9,10},{10,... | collective-permute-start | bytes 98312 | tf_op jit(solution)/shard_map/ppermute | solution.py:22
  126.8 2.3 %collective-permute-done.30.rest_2_ = f32[16,512]{1,0:T(8,128)S(1)} collective-permute-done((f32[16,512]{1,0:T(8,128)S(1)}, f32[16,512]{1,0:T(8,128)S(1)}, u32[]{:S(2)}, u32[]{:S(2)}) %collective-permute-start.30) | collective-permute-done | bytes 32800 | tf_op jit(solution)/shard_map/ppermute | solution.py:22
  129.1 1.2 finish.1
  (55 shorter events, 0.3 us)
Async XLA Ops:
  0.0 6.6 %copy-start = (bf16[64,128,128]{2,1,0:T(8,128)(2,1)S(1)}, bf16[64,128,128]{2,1,0:T(8,128)(2,1)}, u32[]{:S(2)}) copy-start(bf16[64,128,128]{2,1,0:T(8,128)(2,1)} %rest_8_.5) | copy-start | bytes 6291460
  0.0 6.6 %copy-start.16 = (s32[64]{0:T(128)S(1)}, s32[64]{0:T(128)}, u32[]{:S(2)}) copy-start(s32[64]{0:T(128)} %source.1) | copy-start | bytes 772
  2.9 18.1 %copy-start.17 = (bf16[768,256]{1,0:T(8,128)(2,1)S(1)}, bf16[768,256]{1,0:T(8,128)(2,1)}, u32[]{:S(2)}) copy-start(bf16[768,256]{1,0:T(8,128)(2,1)} %w_in.1) | copy-start | bytes 1179652
  2.9 18.1 %copy-start.18 = (bf16[256,64]{0,1:T(8,128)(2,1)S(1)}, bf16[256,64]{0,1:T(8,128)(2,1)}, u32[]{:S(2)}) copy-start(bf16[256,64]{0,1:T(8,128)(2,1)} %param.11) | copy-start | bytes 98308
  2.9 18.1 %copy-start.19 = (s32[8192]{0:T(1024)S(1)}, s32[8192]{0:T(1024)}, u32[]{:S(2)}) copy-start(s32[8192]{0:T(1024)} %param.12) | copy-start | bytes 98308
  2.9 18.1 %copy-start.20 = (s32[64]{0:T(128)S(1)}, s32[64]{0:T(128)}, u32[]{:S(2)}) copy-start(s32[64]{0:T(128)} %param.14) | copy-start | bytes 772
  2.9 43.2 %collective-permute-start.3 = (bf16[48,128,128]{2,1,0:T(8,128)(2,1)}, bf16[48,128,128]{2,1,0:T(8,128)(2,1)}, u32[]{:S(2)}, u32[]{:S(2)}) collective-permute-start(bf16[48,128,128]{2,1,0:T(8,128)(2,1)} %slice.7), channel_id=1, source_target_pairs={{0,2},{1,3},{2,0},{3,1},{4,6},{5,7},{6,4},{7,5},{8,10},{9,11},{10,... | collective-permute-start | bytes 4718600 | tf_op jit(solution)/shard_map/ppermute | solution.py:22
  8.3 12.7 %all-to-all-start = ((f32[8,16,128]{2,1,0:T(8,128)}), f32[8,16,128]{2,1,0:T(8,128)S(1)}, u32[]{:S(2)}, u32[]{:S(2)}) async-start(f32[8,16,128]{2,1,0:T(8,128)} %column_sums.1), calls=%async_computation | async-start | bytes 131072 | tf_op jit(solution)/shard_map/all_to_all | solution.py:400
  14.1 58.2 %collective-permute-start.11 = (bf16[64,128,128]{2,1,0:T(8,128)(2,1)S(1)}, bf16[64,128,128]{2,1,0:T(8,128)(2,1)}, u32[]{:S(2)}, u32[]{:S(2)}) collective-permute-start(bf16[64,128,128]{2,1,0:T(8,128)(2,1)S(1)} %copy-done), channel_id=1, source_target_pairs={{0,1},{1,0},{2,3},{3,2},{4,5},{5,4},{6,7},{7,6},{8,9},{9,8},{10,11... | collective-permute-start | bytes 6291464 | tf_op jit(solution)/shard_map/ppermute | solution.py:22
  21.0 25.1 %copy-start.15 = (s32[2048]{0:T(1024)S(1)}, s32[2048]{0:T(1024)}, u32[]{:S(2)}) copy-start(s32[2048]{0:T(1024)} %param.17) | copy-start | bytes 24580
  36.2 2.0 %collective-permute-start = (f32[16,2304]{1,0:T(8,128)S(1)}, f32[16,2304]{1,0:T(8,128)S(1)}, u32[]{:S(2)}, u32[]{:S(2)}) collective-permute-start(f32[16,2304]{1,0:T(8,128)S(1)} %get-tuple-element.22), channel_id=1, source_target_pairs={{0,1},{1,0},{2,3},{3,2},{4,5},{5,4},{6,7},{7,6},{8,9},{9,8},{10,11... | collective-permute-start | bytes 442376 | tf_op jit(solution)/shard_map/ppermute | solution.py:22
  36.2 8.3 %collective-permute-start.1 = (f32[16,2304]{1,0:T(8,128)S(1)}, f32[16,2304]{1,0:T(8,128)S(1)}, u32[]{:S(2)}, u32[]{:S(2)}) collective-permute-start(f32[16,2304]{1,0:T(8,128)S(1)} %get-tuple-element.23), channel_id=1, source_target_pairs={{0,2},{1,3},{2,0},{3,1},{4,6},{5,7},{6,4},{7,5},{8,10},{9,11},{10,... | collective-permute-start | bytes 442376 | tf_op jit(solution)/shard_map/ppermute | solution.py:22
  36.8 9.3 %collective-permute-start.2 = (f32[16,2304]{1,0:T(8,128)S(1)}, f32[16,2304]{1,0:T(8,128)S(1)}, u32[]{:S(2)}, u32[]{:S(2)}) collective-permute-start(f32[16,2304]{1,0:T(8,128)S(1)} %get-tuple-element.24), channel_id=1, source_target_pairs={{0,3},{1,2},{2,1},{3,0},{4,7},{5,6},{6,5},{7,4},{8,11},{9,10},{10,... | collective-permute-start | bytes 442376 | tf_op jit(solution)/shard_map/ppermute | solution.py:22
  46.2 26.1 %collective-permute-start.13 = (bf16[48,128,128]{2,1,0:T(8,128)(2,1)}, bf16[48,128,128]{2,1,0:T(8,128)(2,1)}, u32[]{:S(2)}, u32[]{:S(2)}) collective-permute-start(bf16[48,128,128]{2,1,0:T(8,128)(2,1)} %get-tuple-element.27.rest_10_), channel_id=1, source_target_pairs={{0,1},{1,0},{2,3},{3,2},{4,5},{5,4},{6,7},{7,6},{8,9},{9,8},{10,11... | collective-permute-start | bytes 4718600 | tf_op jit(solution)/shard_map/ppermute | solution.py:22
  46.9 19.2 %collective-permute-start.12 = (bf16[16,128,128]{2,1,0:T(8,128)(2,1)S(1)}, bf16[16,128,128]{2,1,0:T(8,128)(2,1)S(1)}, u32[]{:S(2)}, u32[]{:S(2)}) collective-permute-start(bf16[16,128,128]{2,1,0:T(8,128)(2,1)S(1)} %get-tuple-element.28), channel_id=1, source_target_pairs={{0,2},{1,3},{2,0},{3,1},{4,6},{5,7},{6,4},{7,5},{8,10},{9,11},{10,... | collective-permute-start | bytes 1572872 | tf_op jit(solution)/shard_map/ppermute | solution.py:22
  48.6 4.3 %collective-permute-start.10 = (bf16[16,2176]{1,0:T(8,128)(2,1)S(1)}, bf16[16,2176]{1,0:T(8,128)(2,1)S(1)}, u32[]{:S(2)}, u32[]{:S(2)}) collective-permute-start(bf16[16,2176]{1,0:T(8,128)(2,1)S(1)} %get-tuple-element.26.rest_7_), channel_id=1, source_target_pairs={{0,4},{4,0},{8,12},{12,8},{16,20},{20,16},{24,28},{28,24},{1,5},{5... | collective-permute-start | bytes 208904 | tf_op jit(solution)/shard_map/ppermute | solution.py:22
  50.1 5.4 %collective-permute-start.8 = (bf16[16,2176]{1,0:T(8,128)(2,1)S(1)}, bf16[16,2176]{1,0:T(8,128)(2,1)S(1)}, u32[]{:S(2)}, u32[]{:S(2)}) collective-permute-start(bf16[16,2176]{1,0:T(8,128)(2,1)S(1)} %get-tuple-element.26.rest_7_), channel_id=1, source_target_pairs={{0,8},{4,12},{8,0},{12,4},{16,24},{20,28},{24,16},{28,20},{1,9},{5... | collective-permute-start | bytes 208904 | tf_op jit(solution)/shard_map/ppermute | solution.py:22
  52.9 13.1 %copy-start.3 = (bf16[16,2176]{1,0:T(8,128)(2,1)}, bf16[16,2176]{1,0:T(8,128)(2,1)S(1)}, u32[]{:S(2)}) copy-start(bf16[16,2176]{1,0:T(8,128)(2,1)S(1)} %collective-permute-done.10.refs_1_.rest_6_) | copy-start | bytes 208900
  52.9 7.1 %collective-permute-start.6 = (bf16[16,2176]{1,0:T(8,128)(2,1)S(1)}, bf16[16,2176]{1,0:T(8,128)(2,1)S(1)}, u32[]{:S(2)}, u32[]{:S(2)}) collective-permute-start(bf16[16,2176]{1,0:T(8,128)(2,1)S(1)} %get-tuple-element.26.rest_7_), channel_id=1, source_target_pairs={{0,16},{4,20},{8,24},{12,28},{16,0},{20,4},{24,8},{28,12},{1,17},{... | collective-permute-start | bytes 208904 | tf_op jit(solution)/shard_map/ppermute | solution.py:22
  55.5 10.5 %copy-start.5 = (bf16[16,2176]{1,0:T(8,128)(2,1)}, bf16[16,2176]{1,0:T(8,128)(2,1)S(1)}, u32[]{:S(2)}) copy-start(bf16[16,2176]{1,0:T(8,128)(2,1)S(1)} %collective-permute-done.8.refs_2_.rest_5_) | copy-start | bytes 208900
  55.5 6.2 %collective-permute-start.4 = (bf16[16,2176]{1,0:T(8,128)(2,1)S(1)}, bf16[16,2176]{1,0:T(8,128)(2,1)S(1)}, u32[]{:S(2)}, u32[]{:S(2)}) collective-permute-start(bf16[16,2176]{1,0:T(8,128)(2,1)S(1)} %get-tuple-element.26.rest_7_), channel_id=1, source_target_pairs={{0,24},{4,28},{8,16},{12,20},{16,8},{20,12},{24,0},{28,4},{1,25},{... | collective-permute-start | bytes 208904 | tf_op jit(solution)/shard_map/ppermute | solution.py:22
  60.1 6.0 %copy-start.7 = (bf16[16,2176]{1,0:T(8,128)(2,1)}, bf16[16,2176]{1,0:T(8,128)(2,1)S(1)}, u32[]{:S(2)}) copy-start(bf16[16,2176]{1,0:T(8,128)(2,1)S(1)} %collective-permute-done.6.refs_4_.rest_3_) | copy-start | bytes 208900
  60.1 4.3 %collective-permute-start.9 = (bf16[16,2176]{1,0:T(8,128)(2,1)S(1)}, bf16[16,2176]{1,0:T(8,128)(2,1)S(1)}, u32[]{:S(2)}, u32[]{:S(2)}) collective-permute-start(bf16[16,2176]{1,0:T(8,128)(2,1)S(1)} %collective-permute-done.8.refs_2_.rest_5_), channel_id=1, source_target_pairs={{0,4},{4,0},{8,12},{12,8},{16,20},{20,16},{24,28},{28,24},{1,5},{5... | collective-permute-start | bytes 208904 | tf_op jit(solution)/shard_map/ppermute | solution.py:22
  61.7 4.3 %copy-start.9 = (bf16[16,2176]{1,0:T(8,128)(2,1)}, bf16[16,2176]{1,0:T(8,128)(2,1)S(1)}, u32[]{:S(2)}) copy-start(bf16[16,2176]{1,0:T(8,128)(2,1)S(1)} %collective-permute-done.4.refs_6_.rest_1_) | copy-start | bytes 208900
  61.7 4.3 %collective-permute-start.7 = (bf16[16,2176]{1,0:T(8,128)(2,1)S(1)}, bf16[16,2176]{1,0:T(8,128)(2,1)S(1)}, u32[]{:S(2)}, u32[]{:S(2)}) collective-permute-start(bf16[16,2176]{1,0:T(8,128)(2,1)S(1)} %collective-permute-done.6.refs_4_.rest_3_), channel_id=1, source_target_pairs={{0,4},{4,0},{8,12},{12,8},{16,20},{20,16},{24,28},{28,24},{1,5},{5... | collective-permute-start | bytes 208904 | tf_op jit(solution)/shard_map/ppermute | solution.py:22
  64.4 1.7 %copy-start.11 = (bf16[16,2176]{1,0:T(8,128)(2,1)}, bf16[16,2176]{1,0:T(8,128)(2,1)S(1)}, u32[]{:S(2)}) copy-start(bf16[16,2176]{1,0:T(8,128)(2,1)S(1)} %collective-permute-done.9.refs_3_.rest_4_) | copy-start | bytes 208900
  66.0 0.6 copy-start.13
  66.7 0.8 copy-start.1
  67.5 4.8 %collective-permute-start.14 = (bf16[16,128,128]{2,1,0:T(8,128)(2,1)}, bf16[16,128,128]{2,1,0:T(8,128)(2,1)S(1)}, u32[]{:S(2)}, u32[]{:S(2)}) collective-permute-start(bf16[16,128,128]{2,1,0:T(8,128)(2,1)} %after.1.rest_11_), channel_id=1, source_target_pairs={{0,1},{1,0},{2,3},{3,2},{4,5},{5,4},{6,7},{7,6},{8,9},{9,8},{10,11... | collective-permute-start | bytes 1572872 | tf_op jit(solution)/shard_map/ppermute | solution.py:22
  67.5 4.8 %collective-permute-start.5 = (bf16[16,2176]{1,0:T(8,128)(2,1)}, bf16[16,2176]{1,0:T(8,128)(2,1)S(1)}, u32[]{:S(2)}, u32[]{:S(2)}) collective-permute-start(bf16[16,2176]{1,0:T(8,128)(2,1)} %copy-done.9), channel_id=1, source_target_pairs={{0,4},{4,0},{8,12},{12,8},{16,20},{20,16},{24,28},{28,24},{1,5},{5... | collective-permute-start | bytes 208904 | tf_op jit(solution)/shard_map/ppermute | solution.py:22
  72.3 1.0 copy-start.2
  73.3 0.9 copy-start.4
  74.2 0.9 copy-start.6
  75.1 0.9 copy-start.8
  76.0 0.9 copy-start.10
  76.9 0.9 copy-start.12
  77.8 0.9 copy-start.14
  84.6 5.7 %collective-permute-start.19 = (bf16[16,2048]{1,0:T(8,128)(2,1)S(1)}, bf16[16,2048]{1,0:T(8,128)(2,1)S(1)}, u32[]{:S(2)}, u32[]{:S(2)}) collective-permute-start(bf16[16,2048]{1,0:T(8,128)(2,1)S(1)} %get-tuple-element.31.rest_7_), channel_id=1, source_target_pairs={{0,8},{4,12},{8,0},{12,4},{16,24},{20,28},{24,16},{28,20},{1,9},{5... | collective-permute-start | bytes 196616 | tf_op jit(solution)/shard_map/ppermute | solution.py:22
  84.9 8.8 %collective-permute-start.17 = (bf16[16,2048]{1,0:T(8,128)(2,1)S(1)}, bf16[16,2048]{1,0:T(8,128)(2,1)S(1)}, u32[]{:S(2)}, u32[]{:S(2)}) collective-permute-start(bf16[16,2048]{1,0:T(8,128)(2,1)S(1)} %get-tuple-element.31.rest_7_), channel_id=1, source_target_pairs={{0,16},{4,20},{8,24},{12,28},{16,0},{20,4},{24,8},{28,12},{1,17},{... | collective-permute-start | bytes 196616 | tf_op jit(solution)/shard_map/ppermute | solution.py:22
  89.2 6.1 %collective-permute-start.15 = (bf16[16,2048]{1,0:T(8,128)(2,1)S(1)}, bf16[16,2048]{1,0:T(8,128)(2,1)S(1)}, u32[]{:S(2)}, u32[]{:S(2)}) collective-permute-start(bf16[16,2048]{1,0:T(8,128)(2,1)S(1)} %get-tuple-element.31.rest_7_), channel_id=1, source_target_pairs={{0,24},{4,28},{8,16},{12,20},{16,8},{20,12},{24,0},{28,4},{1,25},{... | collective-permute-start | bytes 196616 | tf_op jit(solution)/shard_map/ppermute | solution.py:22
  89.2 6.5 %collective-permute-start.21 = (bf16[16,2048]{1,0:T(8,128)(2,1)S(1)}, bf16[16,2048]{1,0:T(8,128)(2,1)S(1)}, u32[]{:S(2)}, u32[]{:S(2)}) collective-permute-start(bf16[16,2048]{1,0:T(8,128)(2,1)S(1)} %get-tuple-element.31.rest_7_), channel_id=1, source_target_pairs={{0,4},{4,0},{8,12},{12,8},{16,20},{20,16},{24,28},{28,24},{1,5},{5... | collective-permute-start | bytes 196616 | tf_op jit(solution)/shard_map/ppermute | solution.py:22
  90.3 5.5 %collective-permute-start.20 = (bf16[16,2048]{1,0:T(8,128)(2,1)S(1)}, bf16[16,2048]{1,0:T(8,128)(2,1)S(1)}, u32[]{:S(2)}, u32[]{:S(2)}) collective-permute-start(bf16[16,2048]{1,0:T(8,128)(2,1)S(1)} %collective-permute-done.19.rest_5_), channel_id=1, source_target_pairs={{0,4},{4,0},{8,12},{12,8},{16,20},{20,16},{24,28},{28,24},{1,5},{5... | collective-permute-start | bytes 196616 | tf_op jit(solution)/shard_map/ppermute | solution.py:22
  93.7 4.3 %collective-permute-start.18 = (bf16[16,2048]{1,0:T(8,128)(2,1)S(1)}, bf16[16,2048]{1,0:T(8,128)(2,1)S(1)}, u32[]{:S(2)}, u32[]{:S(2)}) collective-permute-start(bf16[16,2048]{1,0:T(8,128)(2,1)S(1)} %collective-permute-done.17.rest_3_), channel_id=1, source_target_pairs={{0,4},{4,0},{8,12},{12,8},{16,20},{20,16},{24,28},{28,24},{1,5},{5... | collective-permute-start | bytes 196616 | tf_op jit(solution)/shard_map/ppermute | solution.py:22
  95.3 4.3 %collective-permute-start.16 = (bf16[16,2048]{1,0:T(8,128)(2,1)S(1)}, bf16[16,2048]{1,0:T(8,128)(2,1)S(1)}, u32[]{:S(2)}, u32[]{:S(2)}) collective-permute-start(bf16[16,2048]{1,0:T(8,128)(2,1)S(1)} %collective-permute-done.15.rest_1_), channel_id=1, source_target_pairs={{0,4},{4,0},{8,12},{12,8},{16,20},{20,16},{24,28},{28,24},{1,5},{5... | collective-permute-start | bytes 196616 | tf_op jit(solution)/shard_map/ppermute | solution.py:22
  105.4 5.7 %collective-permute-start.26 = (bf16[16,2048]{1,0:T(8,128)(2,1)S(1)}, bf16[16,2048]{1,0:T(8,128)(2,1)S(1)}, u32[]{:S(2)}, u32[]{:S(2)}) collective-permute-start(bf16[16,2048]{1,0:T(8,128)(2,1)S(1)} %hop.4.rest_7_), channel_id=1, source_target_pairs={{0,8},{4,12},{8,0},{12,4},{16,24},{20,28},{24,16},{28,20},{1,9},{5... | collective-permute-start | bytes 196616 | tf_op jit(solution)/shard_map/ppermute | solution.py:22
  105.5 6.4 %collective-permute-start.24 = (bf16[16,2048]{1,0:T(8,128)(2,1)S(1)}, bf16[16,2048]{1,0:T(8,128)(2,1)S(1)}, u32[]{:S(2)}, u32[]{:S(2)}) collective-permute-start(bf16[16,2048]{1,0:T(8,128)(2,1)S(1)} %hop.4.rest_7_), channel_id=1, source_target_pairs={{0,16},{4,20},{8,24},{12,28},{16,0},{20,4},{24,8},{28,12},{1,17},{... | collective-permute-start | bytes 196616 | tf_op jit(solution)/shard_map/ppermute | solution.py:22
  108.6 6.1 %collective-permute-start.22 = (bf16[16,2048]{1,0:T(8,128)(2,1)S(1)}, bf16[16,2048]{1,0:T(8,128)(2,1)S(1)}, u32[]{:S(2)}, u32[]{:S(2)}) collective-permute-start(bf16[16,2048]{1,0:T(8,128)(2,1)S(1)} %hop.4.rest_7_), channel_id=1, source_target_pairs={{0,24},{4,28},{8,16},{12,20},{16,8},{20,12},{24,0},{28,4},{1,25},{... | collective-permute-start | bytes 196616 | tf_op jit(solution)/shard_map/ppermute | solution.py:22
  109.9 5.8 %collective-permute-start.28 = (bf16[16,2048]{1,0:T(8,128)(2,1)S(1)}, bf16[16,2048]{1,0:T(8,128)(2,1)S(1)}, u32[]{:S(2)}, u32[]{:S(2)}) collective-permute-start(bf16[16,2048]{1,0:T(8,128)(2,1)S(1)} %hop.4.rest_7_), channel_id=1, source_target_pairs={{0,4},{4,0},{8,12},{12,8},{16,20},{20,16},{24,28},{28,24},{1,5},{5... | collective-permute-start | bytes 196616 | tf_op jit(solution)/shard_map/ppermute | solution.py:22
  111.2 4.5 %collective-permute-start.27 = (bf16[16,2048]{1,0:T(8,128)(2,1)S(1)}, bf16[16,2048]{1,0:T(8,128)(2,1)S(1)}, u32[]{:S(2)}, u32[]{:S(2)}) collective-permute-start(bf16[16,2048]{1,0:T(8,128)(2,1)S(1)} %collective-permute-done.26.rest_5_), channel_id=1, source_target_pairs={{0,4},{4,0},{8,12},{12,8},{16,20},{20,16},{24,28},{28,24},{1,5},{5... | collective-permute-start | bytes 196616 | tf_op jit(solution)/shard_map/ppermute | solution.py:22
  111.9 4.3 %collective-permute-start.25 = (bf16[16,2048]{1,0:T(8,128)(2,1)S(1)}, bf16[16,2048]{1,0:T(8,128)(2,1)S(1)}, u32[]{:S(2)}, u32[]{:S(2)}) collective-permute-start(bf16[16,2048]{1,0:T(8,128)(2,1)S(1)} %collective-permute-done.24.rest_3_), channel_id=1, source_target_pairs={{0,4},{4,0},{8,12},{12,8},{16,20},{20,16},{24,28},{28,24},{1,5},{5... | collective-permute-start | bytes 196616 | tf_op jit(solution)/shard_map/ppermute | solution.py:22
  114.7 4.3 %collective-permute-start.23 = (bf16[16,2048]{1,0:T(8,128)(2,1)S(1)}, bf16[16,2048]{1,0:T(8,128)(2,1)S(1)}, u32[]{:S(2)}, u32[]{:S(2)}) collective-permute-start(bf16[16,2048]{1,0:T(8,128)(2,1)S(1)} %collective-permute-done.22.rest_1_), channel_id=1, source_target_pairs={{0,4},{4,0},{8,12},{12,8},{16,20},{20,16},{24,28},{28,24},{1,5},{5... | collective-permute-start | bytes 196616 | tf_op jit(solution)/shard_map/ppermute | solution.py:22
  124.8 1.9 %collective-permute-start.29 = (f32[16,512]{1,0:T(8,128)S(1)}, f32[16,512]{1,0:T(8,128)S(1)}, u32[]{:S(2)}, u32[]{:S(2)}) collective-permute-start(f32[16,512]{1,0:T(8,128)S(1)} %get-tuple-element.34), channel_id=1, source_target_pairs={{0,1},{1,0},{2,3},{3,2},{4,5},{5,4},{6,7},{7,6},{8,9},{9,8},{10,11... | collective-permute-start | bytes 98312 | tf_op jit(solution)/shard_map/ppermute | solution.py:22
  124.9 4.2 %collective-permute-start.30 = (f32[16,512]{1,0:T(8,128)S(1)}, f32[16,512]{1,0:T(8,128)S(1)}, u32[]{:S(2)}, u32[]{:S(2)}) collective-permute-start(f32[16,512]{1,0:T(8,128)S(1)} %get-tuple-element.35), channel_id=1, source_target_pairs={{0,2},{1,3},{2,0},{3,1},{4,6},{5,7},{6,4},{7,5},{8,10},{9,11},{10,... | collective-permute-start | bytes 98312 | tf_op jit(solution)/shard_map/ppermute | solution.py:22
  125.4 3.7 %collective-permute-start.31 = (f32[16,512]{1,0:T(8,128)S(1)}, f32[16,512]{1,0:T(8,128)S(1)}, u32[]{:S(2)}, u32[]{:S(2)}) collective-permute-start(f32[16,512]{1,0:T(8,128)S(1)} %get-tuple-element.36), channel_id=1, source_target_pairs={{0,3},{1,2},{2,1},{3,0},{4,7},{5,6},{6,5},{7,4},{8,11},{9,10},{10,... | collective-permute-start | bytes 98312 | tf_op jit(solution)/shard_map/ppermute | solution.py:22
where the time goes:
time: 131 us; the launch traced here: 130 us
  starting transfers between devices  42.9 us (33%)
  waiting for transfers between devices  40 us (31%)
  Pallas kernels  35.8 us (27%)
  local copies, waits for them, and re-layouts  10.7 us (8%)
    ppermute x32, starting transfers between devices, xor_send(): return lax.ppermute(value, axis, [(i, i ^ step) for i in range(size)])  37.1 us
    ppermute x32, waiting for transfers between devices, xor_send(): return lax.ppermute(value, axis, [(i, i ^ step) for i in range(size)])  33.1 us
    pallas_call x3, Pallas kernels, hop(): pl.pallas_call(functools.partial(hop_kernel, first, last, parts, spans, f...  17.7 us
    pallas_call x1, Pallas kernels, documents(): pl.pallas_call(documents_kernel, grid_spec=pltpu.PrefetchScalarGridSpec(n...  15.1 us
    unnamed x42, local copies, waits for them, and re-layouts  7.76 us
    all_to_all x1, waiting for transfers between devices, body(): lax.all_to_all(degrees, 'hst', split_axis=0, concat_axis=0, tiled=True)  6.89 us
    all_to_all x1, starting transfers between devices, body(): lax.all_to_all(degrees, 'hst', split_axis=0, concat_axis=0, tiled=True)  5.78 us
    slice x2, local copies, waits for them, and re-layouts, body(): early, late = (tiles[:cut], tiles[cut:])  2.92 us
  transfers between devices with their start and end apart: 33, of which 18 were waited for; matrix products, arithmetic and copies ran while one was open for 0% of the time, Pallas kernels for 13%

commit v1 on v0

--- a/solution.py
+++ b/solution.py
@@ -12,6 +12,7 @@
 DIGITS = 4
 DOC_BLOCK = 1024
 TILE_GROUP = 16
+HOP_MIB = 16
 LIFT = 2.0**64
 NT = (((1,), (1,)), ((), ()))
 MIB = 1 << 20
@@ -216,6 +217,7 @@
         out_specs=keep,
         out_shape=jax.ShapeDtypeStruct(value.shape, value.dtype),
         input_output_aliases={0: 0},
+        compiler_params=pltpu.CompilerParams(vmem_limit_bytes=MIB),
         name="after",
     )(value, *ready)
 
@@ -225,30 +227,28 @@
     chunks, rest = rest[: len(spans)], rest[len(spans) :]
     (tele, inverse), outs, (slabs, inflow) = rest[:2], rest[2:-2], rest[-2:]
     blocks, per, block = inflow.shape
-    step = pl.program_id(0)
-
-    @pl.when(step == 0)
-    def _():
-        inflow[...] = jnp.zeros_like(inflow)
-        slabs[parts * blocks] = jnp.zeros(slabs.shape[1:], slabs.dtype)
-        for j, shard in enumerate(shards):
-            for b in range(blocks):
-                slabs[j * blocks + b] = shard[:, b * block : (b + 1) * block]
+
+    inflow[...] = jnp.zeros_like(inflow)
+    slabs[parts * blocks] = jnp.zeros(slabs.shape[1:], slabs.dtype)
+    for j, shard in enumerate(shards):
+        for b in range(blocks):
+            slabs[j * blocks + b] = shard[:, b * block : (b + 1) * block]
 
     empty = jnp.zeros((per, block), jnp.bfloat16)
-    for tiles, (q, begin, end) in zip(chunks, spans):
+    for tiles, (q, begin) in zip(chunks, spans):
         count = meta[q * LABELS + 2, 0]
-        within = jnp.logical_and(step >= begin, step < end)
-
-        @pl.when(jnp.logical_and(within, step * TILE_GROUP < count))
-        def _():
+        size = tiles.shape[0]
+        groups = (jnp.clip(count - begin, 0, size) + (TILE_GROUP - 1)) // TILE_GROUP
+
+        def group(step, carry):
             products = []
             for c in range(0, TILE_GROUP, 4):
-                held = []
+                held, quad = [], []
                 for i in range(4):
-                    k = step * TILE_GROUP + c + i
-                    source = meta[q * LABELS, k] ^ here[0]
-                    held.append(slabs[jnp.where(k < count, source, parts * blocks)])
+                    at = step * TILE_GROUP + c + i
+                    source = meta[q * LABELS, begin + at] ^ here[0]
+                    held.append(slabs[jnp.where(begin + at < count, source, parts * blocks)])
+                    quad.append(tiles[at])
                 left = jnp.concatenate(
                     [
                         jnp.concatenate([held[0], held[1], empty, empty], axis=0),
@@ -258,8 +258,8 @@
                 )
                 right = jnp.concatenate(
                     [
-                        tiles[c : c + 2].reshape(2 * block, block),
-                        tiles[c + 2 : c + 4].reshape(2 * block, block),
+                        jnp.concatenate(quad[:2], axis=0),
+                        jnp.concatenate(quad[2:], axis=0),
                     ],
                     axis=1,
                 )
@@ -268,30 +268,31 @@
                     side = (i % 2) * block
                     products.append(both[i * per : (i + 1) * per, side : side + block])
             for i in range(TILE_GROUP):
-                inflow[meta[q * LABELS + 1, step * TILE_GROUP + i]] += products[i]
-
-    @pl.when(step == pl.num_programs(0) - 1)
-    def _():
+                inflow[meta[q * LABELS + 1, begin + step * TILE_GROUP + i]] += products[i]
+            return carry
+
+        lax.fori_loop(0, groups, group, 0)
+
+    if first:
+        tail = sum(s[:, blocks * block :].astype(jnp.float32) for s in shards)
+        mass = jnp.sum(tail, axis=1, keepdims=True)
+    for b in range(blocks):
+        cols = slice(b * block, (b + 1) * block)
+        own = tele[:, cols]
+        state = 0.85 * inflow[b] + 0.15 * own
         if first:
-            tail = sum(s[:, blocks * block :].astype(jnp.float32) for s in shards)
-            mass = jnp.sum(tail, axis=1, keepdims=True)
-        for b in range(blocks):
-            cols = slice(b * block, (b + 1) * block)
-            own = tele[:, cols]
-            state = 0.85 * inflow[b] + 0.15 * own
-            if first:
-                state = state / mass
-                outs[1][:, cols] = own / mass
-            if last:
-                inflow[b] = state * scale
-            else:
-                outs[0][:, cols] = (state * inverse[b : b + 1, :]).astype(jnp.bfloat16)
+            state = state / mass
+            outs[1][:, cols] = own / mass
         if last:
-            count = outs[0].shape[1] // block
-            for j, out in enumerate(outs):
-                begin = (here[1] ^ j) * count
-                for i in range(count):
-                    out[:, i * block : (i + 1) * block] = inflow[begin + i]
+            inflow[b] = state * scale
+        else:
+            outs[0][:, cols] = (state * inverse[b : b + 1, :]).astype(jnp.bfloat16)
+    if last:
+        count = outs[0].shape[1] // block
+        for j, out in enumerate(outs):
+            start = (here[1] ^ j) * count
+            for i in range(count):
+                out[:, i * block : (i + 1) * block] = inflow[start + i]
 
 
 def hop(first, last, meta, here, shards, sets, tele, inverse):
@@ -304,44 +305,27 @@
     for q, held in enumerate(sets):
         begin = 0
         for chunk in held:
-            end = begin + chunk.shape[0] // TILE_GROUP
             chunks.append(chunk)
-            spans.append((q, begin, end))
-            begin = end
-
-    def stream(span):
-        _, begin, end = span
-        return pl.BlockSpec(
-            (TILE_GROUP, block, block),
-            lambda i, m, p: (jnp.clip(i - begin, 0, end - begin - 1), 0, 0),
-        )
-
+            spans.append((q, begin))
+            begin += chunk.shape[0]
     if last:
         out_shape = [jax.ShapeDtypeStruct((per, hosts // split), jnp.float32)] * split
     else:
         out_shape = [jax.ShapeDtypeStruct((per, hosts), jnp.bfloat16)]
         if first:
             out_shape.append(jax.ShapeDtypeStruct((per, hosts), jnp.float32))
-
-    def whole(array):
-        return pl.BlockSpec(array.shape, lambda i, m, p: (0,) * len(array.shape))
-
+    smem = pl.BlockSpec(memory_space=pltpu.SMEM)
+    vmem = pl.BlockSpec(memory_space=pltpu.VMEM)
     return pl.pallas_call(
         functools.partial(hop_kernel, first, last, parts, spans, float(parts * hosts)),
-        grid_spec=pltpu.PrefetchScalarGridSpec(
-            num_scalar_prefetch=2,
-            grid=(slots // TILE_GROUP,),
-            in_specs=[whole(s) for s in reversed(shards)]
-            + [stream(span) for span in spans]
-            + [whole(tele), whole(inverse)],
-            out_specs=[whole(s) for s in out_shape],
-            scratch_shapes=[
-                pltpu.VMEM((parts * blocks + 1, per, block), jnp.bfloat16),
-                pltpu.VMEM((blocks, per, block), jnp.float32),
-            ],
-        ),
+        in_specs=[smem] * 2 + [vmem] * (parts + len(chunks) + 2),
+        out_specs=[vmem] * len(out_shape),
+        scratch_shapes=[
+            pltpu.VMEM((parts * blocks + 1, per, block), jnp.bfloat16),
+            pltpu.VMEM((blocks, per, block), jnp.float32),
+        ],
         out_shape=out_shape,
-        compiler_params=pltpu.CompilerParams(vmem_limit_bytes=16 * MIB),
+        compiler_params=pltpu.CompilerParams(vmem_limit_bytes=HOP_MIB * MIB),
         cost_estimate=pl.CostEstimate(
             flops=2 * split * slots * block * block * per,
             bytes_accessed=split * slots * block * block * 2,
@@ -412,7 +396,7 @@
         shards = spread(sent, "hst")
         if first:
             for j in range(2, split, 2):
-                far[j][1] = after(far[j][1], shards[1:-1])
+                far[j][1] = after(far[j][1], shards[1:])
                 far[j + 1].append(xor_send(far[j][1], "doc", 1))
             sets = [[tiles], [near]] + [far[j] for j in range(2, split)]
         outs = hop(first, last, meta, here, shards, sets, tele, inverse)

time: 131 us -> 129 us (0.985)
  starting transfers between devices: 42.9 us -> 46 us
  local copies, waits for them, and re-layouts: 10.7 us -> 7.76 us
  Pallas kernels: 35.8 us -> 34.3 us
    ppermute x32, starting transfers between devices: 37.1 us -> 40.2 us  [xor_send(): return lax.ppermute(value, axis, [(i, i ^ step) for i in range(size)])]
    unnamed x42 -> x30, local copies, waits for them, and re-layouts: 7.76 us -> 4.84 us
    pallas_call x3, Pallas kernels: 17.7 us -> 16.1 us  [hop(): pl.pallas_call(functools.partial(hop_kernel, first, last, parts, spans, f...]
where the time goes in v1:
time: 129 us
  starting transfers between devices  46 us (36%)
  waiting for transfers between devices  40.1 us (31%)
  Pallas kernels  34.3 us (27%)
  local copies, waits for them, and re-layouts  7.76 us (6%)
    ppermute x32, starting transfers between devices, xor_send(): return lax.ppermute(value, axis, [(i, i ^ step) for i in range(size)])  40.2 us
    ppermute x32, waiting for transfers between devices, xor_send(): return lax.ppermute(value, axis, [(i, i ^ step) for i in range(size)])  33.2 us
    pallas_call x3, Pallas kernels, hop(): pl.pallas_call(functools.partial(hop_kernel, first, last, parts, spans, f...  16.1 us
    pallas_call x1, Pallas kernels, documents(): pl.pallas_call(documents_kernel, grid_spec=pltpu.PrefetchScalarGridSpec(n...  15.1 us
    all_to_all x1, waiting for transfers between devices, body(): lax.all_to_all(degrees, 'hst', split_axis=0, concat_axis=0, tiled=True)  6.89 us
    all_to_all x1, starting transfers between devices, body(): lax.all_to_all(degrees, 'hst', split_axis=0, concat_axis=0, tiled=True)  5.82 us
    unnamed x30, local copies, waits for them, and re-layouts  4.84 us
    slice x2, local copies, waits for them, and re-layouts, body(): early, late = (tiles[:cut], tiles[cut:])  2.92 us
  transfers between devices with their start and end apart: 33, of which 18 were waited for; matrix products, arithmetic and copies ran while one was open for 0% of the time, Pallas kernels for 13%

profile of v1, /device:TPU:0, one launch (start us, length us, event | category | flops | bytes accessed | tf_op | source)
XLA Modules:
  0.0 129.0 jit_solution(7071390805069462812)
XLA Ops:
  0.0 2.9 %slice.7 = bf16[48,128,128]{2,1,0:T(8,128)(2,1)} slice(bf16[64,128,128]{2,1,0:T(8,128)(2,1)} %rest_8_.5), slice={[0:48], [0:128], [0:128]} | slice | bytes 3145728 | tf_op jit(solution)/shard_map/slice | solution.py:381
  2.9 3.0 %collective-permute-start.3 = (bf16[48,128,128]{2,1,0:T(8,128)(2,1)}, bf16[48,128,128]{2,1,0:T(8,128)(2,1)}, u32[]{:S(2)}, u32[]{:S(2)}) collective-permute-start(bf16[48,128,128]{2,1,0:T(8,128)(2,1)} %slice.7), channel_id=1, source_target_pairs={{0,2},{1,3},{2,0},{3,1},{4,6},{5,7},{6,4},{7,5},{8,10},{9,11},{10,... | collective-permute-start | bytes 4718600 | tf_op jit(solution)/shard_map/ppermute | solution.py:23
  6.6 1.7 %column_sums.1 = f32[8,16,128]{2,1,0:T(8,128)} custom-call(s32[64]{0:T(128)S(1)} %copy-done.10, s32[1]{0:T(128)} %copy.16.count, bf16[64,128,128]{2,1,0:T(8,128)(2,1)S(1)} %copy-done), custom_call_target="tpu_custom_call" | custom-call | flops 1048576 | bytes 2097152 | tf_op jit(solution)/shard_map/column_sums/pallas_call | solution.py:49
  8.3 5.8 %all-to-all-start = ((f32[8,16,128]{2,1,0:T(8,128)}), f32[8,16,128]{2,1,0:T(8,128)S(1)}, u32[]{:S(2)}, u32[]{:S(2)}) async-start(f32[8,16,128]{2,1,0:T(8,128)} %column_sums.1), calls=%async_computation | async-start | bytes 131072 | tf_op jit(solution)/shard_map/all_to_all | solution.py:384
  14.1 6.9 %all-to-all-done.degrees = f32[8,16,128]{2,1,0:T(8,128)S(1)} async-done(((f32[8,16,128]{2,1,0:T(8,128)}), f32[8,16,128]{2,1,0:T(8,128)S(1)}, u32[]{:S(2)}, u32[]{:S(2)}) %all-to-all-start) | async-done | bytes 65568 | tf_op jit(solution)/shard_map/all_to_all | solution.py:384
  21.0 0.0 copy-start.9
  21.0 15.1 %documents.1 = (f32[16,2304]{1,0:T(8,128)S(1)}, f32[16,2304]{1,0:T(8,128)S(1)}, f32[16,2304]{1,0:T(8,128)S(1)}, f32[16,2304]{1,0:T(8,128)S(1)}) custom-call(s32[1]{0:T(128)} %bitcast.1.place, bf16[8192,768]{1,0:T(8,128)(2,1)} %docs.1, bf16[768,256]{1,0:T(8,128)(2,1)S(1)} %copy-done.11, bf16[64,256]{1,0:T(8,128)(2,1)S(1)} %bitcast.12, ...), custom_call_target="tpu_custom_call" | custom-call | flops 7784628224 | bytes 12582912 | tf_op jit(solution)/shard_map/documents/pallas_call | solution.py:129
  36.2 0.1 collective-permute-start
  36.3 0.5 collective-permute-start.1
  36.8 1.3 %collective-permute-start.2 = (f32[16,2304]{1,0:T(8,128)S(1)}, f32[16,2304]{1,0:T(8,128)S(1)}, u32[]{:S(2)}, u32[]{:S(2)}) collective-permute-start(f32[16,2304]{1,0:T(8,128)S(1)} %get-tuple-element.24), channel_id=1, source_target_pairs={{0,3},{1,2},{2,1},{3,0},{4,7},{5,6},{6,5},{7,4},{8,11},{9,10},{10,... | collective-permute-start | bytes 442376 | tf_op jit(solution)/shard_map/ppermute | solution.py:23
  38.2 0.0 collective-permute-done.rest_1_
  38.2 6.4 %collective-permute-done.1.rest_2_ = f32[16,2304]{1,0:T(8,128)S(1)} collective-permute-done((f32[16,2304]{1,0:T(8,128)S(1)}, f32[16,2304]{1,0:T(8,128)S(1)}, u32[]{:S(2)}, u32[]{:S(2)}) %collective-permute-start.1) | collective-permute-done | bytes 147488 | tf_op jit(solution)/shard_map/ppermute | solution.py:23
  44.5 1.6 %collective-permute-done.2.rest_3_ = f32[16,2304]{1,0:T(8,128)S(1)} collective-permute-done((f32[16,2304]{1,0:T(8,128)S(1)}, f32[16,2304]{1,0:T(8,128)S(1)}, u32[]{:S(2)}, u32[]{:S(2)}) %collective-permute-start.2) | collective-permute-done | bytes 147488 | tf_op jit(solution)/shard_map/ppermute | solution.py:23
  46.1 0.1 start_values.1
  46.3 0.0 copy-start.5
  46.3 0.6 collective-permute-start.13
  46.9 1.7 %collective-permute-start.12 = (bf16[16,128,128]{2,1,0:T(8,128)(2,1)S(1)}, bf16[16,128,128]{2,1,0:T(8,128)(2,1)S(1)}, u32[]{:S(2)}, u32[]{:S(2)}) collective-permute-start(bf16[16,128,128]{2,1,0:T(8,128)(2,1)S(1)} %get-tuple-element.28), channel_id=1, source_target_pairs={{0,2},{1,3},{2,0},{3,1},{4,6},{5,7},{6,4},{7,5},{8,10},{9,11},{10,... | collective-permute-start | bytes 1572872 | tf_op jit(solution)/shard_map/ppermute | solution.py:23
  48.7 1.5 %collective-permute-start.10 = (bf16[16,2176]{1,0:T(8,128)(2,1)S(1)}, bf16[16,2176]{1,0:T(8,128)(2,1)S(1)}, u32[]{:S(2)}, u32[]{:S(2)}) collective-permute-start(bf16[16,2176]{1,0:T(8,128)(2,1)S(1)} %get-tuple-element.26.rest_7_), channel_id=1, source_target_pairs={{0,4},{4,0},{8,12},{12,8},{16,20},{20,16},{24,28},{28,24},{1,5},{5... | collective-permute-start | bytes 208904 | tf_op jit(solution)/shard_map/ppermute | solution.py:23
  50.1 1.6 %collective-permute-start.8 = (bf16[16,2176]{1,0:T(8,128)(2,1)S(1)}, bf16[16,2176]{1,0:T(8,128)(2,1)S(1)}, u32[]{:S(2)}, u32[]{:S(2)}) collective-permute-start(bf16[16,2176]{1,0:T(8,128)(2,1)S(1)} %get-tuple-element.26.rest_7_), channel_id=1, source_target_pairs={{0,8},{4,12},{8,0},{12,4},{16,24},{20,28},{24,16},{28,20},{1,9},{5... | collective-permute-start | bytes 208904 | tf_op jit(solution)/shard_map/ppermute | solution.py:23
  51.7 1.2 collective-permute-done.10.refs_1_.rest_6_
  53.0 2.6 %collective-permute-start.6 = (bf16[16,2176]{1,0:T(8,128)(2,1)S(1)}, bf16[16,2176]{1,0:T(8,128)(2,1)S(1)}, u32[]{:S(2)}, u32[]{:S(2)}) collective-permute-start(bf16[16,2176]{1,0:T(8,128)(2,1)S(1)} %get-tuple-element.26.rest_7_), channel_id=1, source_target_pairs={{0,16},{4,20},{8,24},{12,28},{16,0},{20,4},{24,8},{28,12},{1,17},{... | collective-permute-start | bytes 208904 | tf_op jit(solution)/shard_map/ppermute | solution.py:23
  55.6 2.5 %collective-permute-start.4 = (bf16[16,2176]{1,0:T(8,128)(2,1)S(1)}, bf16[16,2176]{1,0:T(8,128)(2,1)S(1)}, u32[]{:S(2)}, u32[]{:S(2)}) collective-permute-start(bf16[16,2176]{1,0:T(8,128)(2,1)S(1)} %get-tuple-element.26.rest_7_), channel_id=1, source_target_pairs={{0,24},{4,28},{8,16},{12,20},{16,8},{20,12},{24,0},{28,4},{1,25},{... | collective-permute-start | bytes 208904 | tf_op jit(solution)/shard_map/ppermute | solution.py:23
  58.1 2.0 %collective-permute-done.6.refs_4_.rest_3_ = bf16[16,2176]{1,0:T(8,128)(2,1)S(1)} collective-permute-done((bf16[16,2176]{1,0:T(8,128)(2,1)S(1)}, bf16[16,2176]{1,0:T(8,128)(2,1)S(1)}, u32[]{:S(2)}, u32[]{:S(2)}) %collective-permute-start.6) | collective-permute-done | bytes 69664 | tf_op jit(solution)/shard_map/ppermute | solution.py:23
  60.1 1.5 %collective-permute-start.9 = (bf16[16,2176]{1,0:T(8,128)(2,1)S(1)}, bf16[16,2176]{1,0:T(8,128)(2,1)S(1)}, u32[]{:S(2)}, u32[]{:S(2)}) collective-permute-start(bf16[16,2176]{1,0:T(8,128)(2,1)S(1)} %collective-permute-done.8.refs_2_.rest_5_), channel_id=1, source_target_pairs={{0,4},{4,0},{8,12},{12,8},{16,20},{20,16},{24,28},{28,24},{1,5},{5... | collective-permute-start | bytes 208904 | tf_op jit(solution)/shard_map/ppermute | solution.py:23
  61.6 0.2 collective-permute-done.4.refs_6_.rest_1_
  61.8 1.5 %collective-permute-start.7 = (bf16[16,2176]{1,0:T(8,128)(2,1)S(1)}, bf16[16,2176]{1,0:T(8,128)(2,1)S(1)}, u32[]{:S(2)}, u32[]{:S(2)}) collective-permute-start(bf16[16,2176]{1,0:T(8,128)(2,1)S(1)} %collective-permute-done.6.refs_4_.rest_3_), channel_id=1, source_target_pairs={{0,4},{4,0},{8,12},{12,8},{16,20},{20,16},{24,28},{28,24},{1,5},{5... | collective-permute-start | bytes 208904 | tf_op jit(solution)/shard_map/ppermute | solution.py:23
  63.3 1.9 %collective-permute-done.9.refs_3_.rest_4_ = bf16[16,2176]{1,0:T(8,128)(2,1)S(1)} collective-permute-done((bf16[16,2176]{1,0:T(8,128)(2,1)S(1)}, bf16[16,2176]{1,0:T(8,128)(2,1)S(1)}, u32[]{:S(2)}, u32[]{:S(2)}) %collective-permute-start.9) | collective-permute-done | bytes 69664 | tf_op jit(solution)/shard_map/ppermute | solution.py:23
  65.1 1.0 collective-permute-start.5
  66.2 3.3 %collective-permute-done.5.refs_7_.rest_0_ = bf16[16,2176]{1,0:T(8,128)(2,1)S(1)} collective-permute-done((bf16[16,2176]{1,0:T(8,128)(2,1)S(1)}, bf16[16,2176]{1,0:T(8,128)(2,1)S(1)}, u32[]{:S(2)}, u32[]{:S(2)}) %collective-permute-start.5) | collective-permute-done | bytes 69664 | tf_op jit(solution)/shard_map/ppermute | solution.py:23
  69.5 0.6 copy-done.1
  70.1 0.6 copy-done.3
  70.7 0.1 pad_add_fusion.here
  70.8 1.8 %collective-permute-done.14.rest_13_ = bf16[16,128,128]{2,1,0:T(8,128)(2,1)S(1)} collective-permute-done((bf16[16,128,128]{2,1,0:T(8,128)(2,1)S(1)}, bf16[16,128,128]{2,1,0:T(8,128)(2,1)S(1)}, u32[]{:S(2)}, u32[]{:S(2)}) %collective-permute-start.14) | collective-permute-done | bytes 524320 | tf_op jit(solution)/shard_map/ppermute | solution.py:23
  72.6 0.9 copy-done.2
  73.5 0.9 copy-done.4
  74.4 0.9 copy-done.6
  75.3 0.9 copy-done.8
  76.2 5.4 %hop.3 = (bf16[16,2048]{1,0:T(8,128)(2,1)S(1)}, f32[16,2048]{1,0:T(8,128)S(1)}) custom-call(s32[12,128]{1,0:T(8,128)S(1)} %get-tuple-element.25.meta, s32[2]{0:T(128)S(1)} %pad_add_fusion.here, bf16[16,2176]{1,0:T(8,128)(2,1)S(1)} %copy-done.4, bf16[16,2176]{1,0:T(8,128)(2,1)S(1)} %collective-permute-done.4.refs_6_.rest_1_, bf16[16,2176]{1,0:T(8,128)(2,1)S(1)} %copy-done.2, ...), custom_call_target="tpu_custom_call" | custom-call | flops 134217728 | bytes 8388608 | tf_op jit(solution)/shard_map/hop/pallas_call | solution.py:319
  81.6 2.0 %collective-permute-start.19 = (bf16[16,2048]{1,0:T(8,128)(2,1)S(1)}, bf16[16,2048]{1,0:T(8,128)(2,1)S(1)}, u32[]{:S(2)}, u32[]{:S(2)}) collective-permute-start(bf16[16,2048]{1,0:T(8,128)(2,1)S(1)} %get-tuple-element.31.rest_7_), channel_id=1, source_target_pairs={{0,8},{4,12},{8,0},{12,4},{16,24},{20,28},{24,16},{28,20},{1,9},{5... | collective-permute-start | bytes 196616 | tf_op jit(solution)/shard_map/ppermute | solution.py:23
  83.6 3.3 %collective-permute-start.17 = (bf16[16,2048]{1,0:T(8,128)(2,1)S(1)}, bf16[16,2048]{1,0:T(8,128)(2,1)S(1)}, u32[]{:S(2)}, u32[]{:S(2)}) collective-permute-start(bf16[16,2048]{1,0:T(8,128)(2,1)S(1)} %get-tuple-element.31.rest_7_), channel_id=1, source_target_pairs={{0,16},{4,20},{8,24},{12,28},{16,0},{20,4},{24,8},{28,12},{1,17},{... | collective-permute-start | bytes 196616 | tf_op jit(solution)/shard_map/ppermute | solution.py:23
  87.0 1.6 %collective-permute-start.21 = (bf16[16,2048]{1,0:T(8,128)(2,1)S(1)}, bf16[16,2048]{1,0:T(8,128)(2,1)S(1)}, u32[]{:S(2)}, u32[]{:S(2)}) collective-permute-start(bf16[16,2048]{1,0:T(8,128)(2,1)S(1)} %get-tuple-element.31.rest_7_), channel_id=1, source_target_pairs={{0,4},{4,0},{8,12},{12,8},{16,20},{20,16},{24,28},{28,24},{1,5},{5... | collective-permute-start | bytes 196616 | tf_op jit(solution)/shard_map/ppermute | solution.py:23
  88.6 0.4 collective-permute-start.20
  89.0 2.0 %collective-permute-done.17.rest_3_ = bf16[16,2048]{1,0:T(8,128)(2,1)S(1)} collective-permute-done((bf16[16,2048]{1,0:T(8,128)(2,1)S(1)}, bf16[16,2048]{1,0:T(8,128)(2,1)S(1)}, u32[]{:S(2)}, u32[]{:S(2)}) %collective-permute-start.17) | collective-permute-done | bytes 65568 | tf_op jit(solution)/shard_map/ppermute | solution.py:23
  91.0 1.1 collective-permute-start.18
  92.2 1.0 collective-permute-done.15.rest_1_
  93.1 1.1 collective-permute-start.16
  94.3 1.3 %collective-permute-done.18.rest_2_ = bf16[16,2048]{1,0:T(8,128)(2,1)S(1)} collective-permute-done((bf16[16,2048]{1,0:T(8,128)(2,1)S(1)}, bf16[16,2048]{1,0:T(8,128)(2,1)S(1)}, u32[]{:S(2)}, u32[]{:S(2)}) %collective-permute-start.18) | collective-permute-done | bytes 65568 | tf_op jit(solution)/shard_map/ppermute | solution.py:23
  95.6 1.8 %collective-permute-done.16.rest_0_ = bf16[16,2048]{1,0:T(8,128)(2,1)S(1)} collective-permute-done((bf16[16,2048]{1,0:T(8,128)(2,1)S(1)}, bf16[16,2048]{1,0:T(8,128)(2,1)S(1)}, u32[]{:S(2)}, u32[]{:S(2)}) %collective-permute-start.16) | collective-permute-done | bytes 65568 | tf_op jit(solution)/shard_map/ppermute | solution.py:23
  97.4 5.3 %hop.4.rest_7_ = bf16[16,2048]{1,0:T(8,128)(2,1)S(1)} custom-call(s32[12,128]{1,0:T(8,128)S(1)} %get-tuple-element.25.meta, s32[2]{0:T(128)S(1)} %pad_add_fusion.here, bf16[16,2048]{1,0:T(8,128)(2,1)S(1)} %collective-permute-done.16.rest_0_, bf16[16,2048]{1,0:T(8,128)(2,1)S(1)} %collective-permute-done.15.rest_1_, ...), custom_call_target="tpu_custom_call" | custom-call | flops 134217728 | bytes 8388608 | tf_op jit(solution)/shard_map/hop/pallas_call | solution.py:319
  102.8 2.3 %collective-permute-start.26 = (bf16[16,2048]{1,0:T(8,128)(2,1)S(1)}, bf16[16,2048]{1,0:T(8,128)(2,1)S(1)}, u32[]{:S(2)}, u32[]{:S(2)}) collective-permute-start(bf16[16,2048]{1,0:T(8,128)(2,1)S(1)} %hop.4.rest_7_), channel_id=1, source_target_pairs={{0,8},{4,12},{8,0},{12,4},{16,24},{20,28},{24,16},{28,20},{1,9},{5... | collective-permute-start | bytes 196616 | tf_op jit(solution)/shard_map/ppermute | solution.py:23
  105.1 2.8 %collective-permute-start.24 = (bf16[16,2048]{1,0:T(8,128)(2,1)S(1)}, bf16[16,2048]{1,0:T(8,128)(2,1)S(1)}, u32[]{:S(2)}, u32[]{:S(2)}) collective-permute-start(bf16[16,2048]{1,0:T(8,128)(2,1)S(1)} %hop.4.rest_7_), channel_id=1, source_target_pairs={{0,16},{4,20},{8,24},{12,28},{16,0},{20,4},{24,8},{28,12},{1,17},{... | collective-permute-start | bytes 196616 | tf_op jit(solution)/shard_map/ppermute | solution.py:23
  107.9 1.9 %collective-permute-start.28 = (bf16[16,2048]{1,0:T(8,128)(2,1)S(1)}, bf16[16,2048]{1,0:T(8,128)(2,1)S(1)}, u32[]{:S(2)}, u32[]{:S(2)}) collective-permute-start(bf16[16,2048]{1,0:T(8,128)(2,1)S(1)} %hop.4.rest_7_), channel_id=1, source_target_pairs={{0,4},{4,0},{8,12},{12,8},{16,20},{20,16},{24,28},{28,24},{1,5},{5... | collective-permute-start | bytes 196616 | tf_op jit(solution)/shard_map/ppermute | solution.py:23
  109.8 1.2 collective-permute-start.27
  111.0 0.9 collective-permute-start.25
  111.8 2.1 %collective-permute-done.22.rest_1_ = bf16[16,2048]{1,0:T(8,128)(2,1)S(1)} collective-permute-done((bf16[16,2048]{1,0:T(8,128)(2,1)S(1)}, bf16[16,2048]{1,0:T(8,128)(2,1)S(1)}, u32[]{:S(2)}, u32[]{:S(2)}) %collective-permute-start.22) | collective-permute-done | bytes 65568 | tf_op jit(solution)/shard_map/ppermute | solution.py:23
  114.0 0.1 collective-permute-done.27.rest_4_
  114.1 1.2 collective-permute-done.25.rest_2_
  115.2 3.0 %collective-permute-done.23.rest_0_ = bf16[16,2048]{1,0:T(8,128)(2,1)S(1)} collective-permute-done((bf16[16,2048]{1,0:T(8,128)(2,1)S(1)}, bf16[16,2048]{1,0:T(8,128)(2,1)S(1)}, u32[]{:S(2)}, u32[]{:S(2)}) %collective-permute-start.23) | collective-permute-done | bytes 65568 | tf_op jit(solution)/shard_map/ppermute | solution.py:23
  118.2 5.4 %hop.5 = (f32[16,512]{1,0:T(8,128)S(1)}, f32[16,512]{1,0:T(8,128)S(1)}, f32[16,512]{1,0:T(8,128)S(1)}, f32[16,512]{1,0:T(8,128)S(1)}) custom-call(s32[12,128]{1,0:T(8,128)S(1)} %get-tuple-element.25.meta, s32[2]{0:T(128)S(1)} %pad_add_fusion.here, bf16[16,2048]{1,0:T(8,128)(2,1)S(1)} %collective-permute-done.23.rest_0_, ...), custom_call_target="tpu_custom_call" | custom-call | flops 134217728 | bytes 8388608 | tf_op jit(solution)/shard_map/hop/pallas_call | solution.py:319
  123.6 0.1 collective-permute-start.29
  123.7 0.4 collective-permute-start.30
  124.0 1.5 %collective-permute-start.31 = (f32[16,512]{1,0:T(8,128)S(1)}, f32[16,512]{1,0:T(8,128)S(1)}, u32[]{:S(2)}, u32[]{:S(2)}) collective-permute-start(f32[16,512]{1,0:T(8,128)S(1)} %get-tuple-element.36), channel_id=1, source_target_pairs={{0,3},{1,2},{2,1},{3,0},{4,7},{5,6},{6,5},{7,4},{8,11},{9,10},{10,... | collective-permute-start | bytes 98312 | tf_op jit(solution)/shard_map/ppermute | solution.py:23
  125.5 2.3 %collective-permute-done.30.rest_2_ = f32[16,512]{1,0:T(8,128)S(1)} collective-permute-done((f32[16,512]{1,0:T(8,128)S(1)}, f32[16,512]{1,0:T(8,128)S(1)}, u32[]{:S(2)}, u32[]{:S(2)}) %collective-permute-start.30) | collective-permute-done | bytes 32800 | tf_op jit(solution)/shard_map/ppermute | solution.py:23
  127.8 1.2 finish.1
  (43 shorter events, 0.1 us)
Async XLA Ops:
  0.0 6.6 %copy-start = (bf16[64,128,128]{2,1,0:T(8,128)(2,1)S(1)}, bf16[64,128,128]{2,1,0:T(8,128)(2,1)}, u32[]{:S(2)}) copy-start(bf16[64,128,128]{2,1,0:T(8,128)(2,1)} %rest_8_.5) | copy-start | bytes 6291460
  0.0 6.6 %copy-start.10 = (s32[64]{0:T(128)S(1)}, s32[64]{0:T(128)}, u32[]{:S(2)}) copy-start(s32[64]{0:T(128)} %source.1) | copy-start | bytes 772
  2.9 18.1 %copy-start.11 = (bf16[768,256]{1,0:T(8,128)(2,1)S(1)}, bf16[768,256]{1,0:T(8,128)(2,1)}, u32[]{:S(2)}) copy-start(bf16[768,256]{1,0:T(8,128)(2,1)} %w_in.1) | copy-start | bytes 1179652
  2.9 18.1 %copy-start.12 = (bf16[256,64]{0,1:T(8,128)(2,1)S(1)}, bf16[256,64]{0,1:T(8,128)(2,1)}, u32[]{:S(2)}) copy-start(bf16[256,64]{0,1:T(8,128)(2,1)} %param.11) | copy-start | bytes 98308
  2.9 18.1 %copy-start.13 = (s32[8192]{0:T(1024)S(1)}, s32[8192]{0:T(1024)}, u32[]{:S(2)}) copy-start(s32[8192]{0:T(1024)} %param.12) | copy-start | bytes 98308
  2.9 18.1 %copy-start.14 = (s32[64]{0:T(128)S(1)}, s32[64]{0:T(128)}, u32[]{:S(2)}) copy-start(s32[64]{0:T(128)} %param.14) | copy-start | bytes 772
  2.9 43.2 %collective-permute-start.3 = (bf16[48,128,128]{2,1,0:T(8,128)(2,1)}, bf16[48,128,128]{2,1,0:T(8,128)(2,1)}, u32[]{:S(2)}, u32[]{:S(2)}) collective-permute-start(bf16[48,128,128]{2,1,0:T(8,128)(2,1)} %slice.7), channel_id=1, source_target_pairs={{0,2},{1,3},{2,0},{3,1},{4,6},{5,7},{6,4},{7,5},{8,10},{9,11},{10,... | collective-permute-start | bytes 4718600 | tf_op jit(solution)/shard_map/ppermute | solution.py:23
  8.3 12.7 %all-to-all-start = ((f32[8,16,128]{2,1,0:T(8,128)}), f32[8,16,128]{2,1,0:T(8,128)S(1)}, u32[]{:S(2)}, u32[]{:S(2)}) async-start(f32[8,16,128]{2,1,0:T(8,128)} %column_sums.1), calls=%async_computation | async-start | bytes 131072 | tf_op jit(solution)/shard_map/all_to_all | solution.py:384
  14.1 56.7 %collective-permute-start.11 = (bf16[64,128,128]{2,1,0:T(8,128)(2,1)S(1)}, bf16[64,128,128]{2,1,0:T(8,128)(2,1)}, u32[]{:S(2)}, u32[]{:S(2)}) collective-permute-start(bf16[64,128,128]{2,1,0:T(8,128)(2,1)S(1)} %copy-done), channel_id=1, source_target_pairs={{0,1},{1,0},{2,3},{3,2},{4,5},{5,4},{6,7},{7,6},{8,9},{9,8},{10,11... | collective-permute-start | bytes 6291464 | tf_op jit(solution)/shard_map/ppermute | solution.py:23
  21.0 25.1 %copy-start.9 = (s32[2048]{0:T(1024)S(1)}, s32[2048]{0:T(1024)}, u32[]{:S(2)}) copy-start(s32[2048]{0:T(1024)} %param.17) | copy-start | bytes 24580
  36.2 2.0 %collective-permute-start = (f32[16,2304]{1,0:T(8,128)S(1)}, f32[16,2304]{1,0:T(8,128)S(1)}, u32[]{:S(2)}, u32[]{:S(2)}) collective-permute-start(f32[16,2304]{1,0:T(8,128)S(1)} %get-tuple-element.22), channel_id=1, source_target_pairs={{0,1},{1,0},{2,3},{3,2},{4,5},{5,4},{6,7},{7,6},{8,9},{9,8},{10,11... | collective-permute-start | bytes 442376 | tf_op jit(solution)/shard_map/ppermute | solution.py:23
  36.3 8.3 %collective-permute-start.1 = (f32[16,2304]{1,0:T(8,128)S(1)}, f32[16,2304]{1,0:T(8,128)S(1)}, u32[]{:S(2)}, u32[]{:S(2)}) collective-permute-start(f32[16,2304]{1,0:T(8,128)S(1)} %get-tuple-element.23), channel_id=1, source_target_pairs={{0,2},{1,3},{2,0},{3,1},{4,6},{5,7},{6,4},{7,5},{8,10},{9,11},{10,... | collective-permute-start | bytes 442376 | tf_op jit(solution)/shard_map/ppermute | solution.py:23
  36.8 9.3 %collective-permute-start.2 = (f32[16,2304]{1,0:T(8,128)S(1)}, f32[16,2304]{1,0:T(8,128)S(1)}, u32[]{:S(2)}, u32[]{:S(2)}) collective-permute-start(f32[16,2304]{1,0:T(8,128)S(1)} %get-tuple-element.24), channel_id=1, source_target_pairs={{0,3},{1,2},{2,1},{3,0},{4,7},{5,6},{6,5},{7,4},{8,11},{9,10},{10,... | collective-permute-start | bytes 442376 | tf_op jit(solution)/shard_map/ppermute | solution.py:23
  46.3 23.2 %copy-start.5 = (f32[16,2048]{1,0:T(8,128)}, f32[16,2048]{1,0:T(8,128)S(1)}, u32[]{:S(2)}) copy-start(f32[16,2048]{1,0:T(8,128)S(1)} %get-tuple-element.29.rest_14_) | copy-start | bytes 393220
  46.3 23.2 %copy-start.7 = (bf16[16,2176]{1,0:T(8,128)(2,1)}, bf16[16,2176]{1,0:T(8,128)(2,1)S(1)}, u32[]{:S(2)}) copy-start(bf16[16,2176]{1,0:T(8,128)(2,1)S(1)} %get-tuple-element.26.rest_7_) | copy-start | bytes 208900
  46.3 26.3 %collective-permute-start.13 = (bf16[48,128,128]{2,1,0:T(8,128)(2,1)}, bf16[48,128,128]{2,1,0:T(8,128)(2,1)}, u32[]{:S(2)}, u32[]{:S(2)}) collective-permute-start(bf16[48,128,128]{2,1,0:T(8,128)(2,1)} %get-tuple-element.27.rest_10_), channel_id=1, source_target_pairs={{0,1},{1,0},{2,3},{3,2},{4,5},{5,4},{6,7},{7,6},{8,9},{9,8},{10,11... | collective-permute-start | bytes 4718600 | tf_op jit(solution)/shard_map/ppermute | solution.py:23
  46.9 22.5 %collective-permute-start.12 = (bf16[16,128,128]{2,1,0:T(8,128)(2,1)S(1)}, bf16[16,128,128]{2,1,0:T(8,128)(2,1)S(1)}, u32[]{:S(2)}, u32[]{:S(2)}) collective-permute-start(bf16[16,128,128]{2,1,0:T(8,128)(2,1)S(1)} %get-tuple-element.28), channel_id=1, source_target_pairs={{0,2},{1,3},{2,0},{3,1},{4,6},{5,7},{6,4},{7,5},{8,10},{9,11},{10,... | collective-permute-start | bytes 1572872 | tf_op jit(solution)/shard_map/ppermute | solution.py:23
  48.7 4.3 %collective-permute-start.10 = (bf16[16,2176]{1,0:T(8,128)(2,1)S(1)}, bf16[16,2176]{1,0:T(8,128)(2,1)S(1)}, u32[]{:S(2)}, u32[]{:S(2)}) collective-permute-start(bf16[16,2176]{1,0:T(8,128)(2,1)S(1)} %get-tuple-element.26.rest_7_), channel_id=1, source_target_pairs={{0,4},{4,0},{8,12},{12,8},{16,20},{20,16},{24,28},{28,24},{1,5},{5... | collective-permute-start | bytes 208904 | tf_op jit(solution)/shard_map/ppermute | solution.py:23
  50.1 5.4 %collective-permute-start.8 = (bf16[16,2176]{1,0:T(8,128)(2,1)S(1)}, bf16[16,2176]{1,0:T(8,128)(2,1)S(1)}, u32[]{:S(2)}, u32[]{:S(2)}) collective-permute-start(bf16[16,2176]{1,0:T(8,128)(2,1)S(1)} %get-tuple-element.26.rest_7_), channel_id=1, source_target_pairs={{0,8},{4,12},{8,0},{12,4},{16,24},{20,28},{24,16},{28,20},{1,9},{5... | collective-permute-start | bytes 208904 | tf_op jit(solution)/shard_map/ppermute | solution.py:23
  53.0 7.1 %collective-permute-start.6 = (bf16[16,2176]{1,0:T(8,128)(2,1)S(1)}, bf16[16,2176]{1,0:T(8,128)(2,1)S(1)}, u32[]{:S(2)}, u32[]{:S(2)}) collective-permute-start(bf16[16,2176]{1,0:T(8,128)(2,1)S(1)} %get-tuple-element.26.rest_7_), channel_id=1, source_target_pairs={{0,16},{4,20},{8,24},{12,28},{16,0},{20,4},{24,8},{28,12},{1,17},{... | collective-permute-start | bytes 208904 | tf_op jit(solution)/shard_map/ppermute | solution.py:23
  55.6 6.2 %collective-permute-start.4 = (bf16[16,2176]{1,0:T(8,128)(2,1)S(1)}, bf16[16,2176]{1,0:T(8,128)(2,1)S(1)}, u32[]{:S(2)}, u32[]{:S(2)}) collective-permute-start(bf16[16,2176]{1,0:T(8,128)(2,1)S(1)} %get-tuple-element.26.rest_7_), channel_id=1, source_target_pairs={{0,24},{4,28},{8,16},{12,20},{16,8},{20,12},{24,0},{28,4},{1,25},{... | collective-permute-start | bytes 208904 | tf_op jit(solution)/shard_map/ppermute | solution.py:23
  60.1 5.0 %collective-permute-start.9 = (bf16[16,2176]{1,0:T(8,128)(2,1)S(1)}, bf16[16,2176]{1,0:T(8,128)(2,1)S(1)}, u32[]{:S(2)}, u32[]{:S(2)}) collective-permute-start(bf16[16,2176]{1,0:T(8,128)(2,1)S(1)} %collective-permute-done.8.refs_2_.rest_5_), channel_id=1, source_target_pairs={{0,4},{4,0},{8,12},{12,8},{16,20},{20,16},{24,28},{28,24},{1,5},{5... | collective-permute-start | bytes 208904 | tf_op jit(solution)/shard_map/ppermute | solution.py:23
  61.8 4.4 %collective-permute-start.7 = (bf16[16,2176]{1,0:T(8,128)(2,1)S(1)}, bf16[16,2176]{1,0:T(8,128)(2,1)S(1)}, u32[]{:S(2)}, u32[]{:S(2)}) collective-permute-start(bf16[16,2176]{1,0:T(8,128)(2,1)S(1)} %collective-permute-done.6.refs_4_.rest_3_), channel_id=1, source_target_pairs={{0,4},{4,0},{8,12},{12,8},{16,20},{20,16},{24,28},{28,24},{1,5},{5... | collective-permute-start | bytes 208904 | tf_op jit(solution)/shard_map/ppermute | solution.py:23
  65.1 4.3 %collective-permute-start.5 = (bf16[16,2176]{1,0:T(8,128)(2,1)S(1)}, bf16[16,2176]{1,0:T(8,128)(2,1)S(1)}, u32[]{:S(2)}, u32[]{:S(2)}) collective-permute-start(bf16[16,2176]{1,0:T(8,128)(2,1)S(1)} %collective-permute-done.4.refs_6_.rest_1_), channel_id=1, source_target_pairs={{0,4},{4,0},{8,12},{12,8},{16,20},{20,16},{24,28},{28,24},{1,5},{5... | collective-permute-start | bytes 208904 | tf_op jit(solution)/shard_map/ppermute | solution.py:23
  69.5 0.6 copy-start.1
  70.1 0.6 copy-start.3
  70.7 1.9 %collective-permute-start.14 = (bf16[16,128,128]{2,1,0:T(8,128)(2,1)S(1)}, bf16[16,128,128]{2,1,0:T(8,128)(2,1)S(1)}, u32[]{:S(2)}, u32[]{:S(2)}) collective-permute-start(bf16[16,128,128]{2,1,0:T(8,128)(2,1)S(1)} %after.1.rest_11_), channel_id=1, source_target_pairs={{0,1},{1,0},{2,3},{3,2},{4,5},{5,4},{6,7},{7,6},{8,9},{9,8},{10,11... | collective-permute-start | bytes 1572872 | tf_op jit(solution)/shard_map/ppermute | solution.py:23
  72.6 0.9 copy-start.2
  73.5 0.9 copy-start.4
  74.4 0.9 copy-start.6
  75.3 0.9 copy-start.8
  81.6 7.0 %collective-permute-start.19 = (bf16[16,2048]{1,0:T(8,128)(2,1)S(1)}, bf16[16,2048]{1,0:T(8,128)(2,1)S(1)}, u32[]{:S(2)}, u32[]{:S(2)}) collective-permute-start(bf16[16,2048]{1,0:T(8,128)(2,1)S(1)} %get-tuple-element.31.rest_7_), channel_id=1, source_target_pairs={{0,8},{4,12},{8,0},{12,4},{16,24},{20,28},{24,16},{28,20},{1,9},{5... | collective-permute-start | bytes 196616 | tf_op jit(solution)/shard_map/ppermute | solution.py:23
  83.6 7.4 %collective-permute-start.17 = (bf16[16,2048]{1,0:T(8,128)(2,1)S(1)}, bf16[16,2048]{1,0:T(8,128)(2,1)S(1)}, u32[]{:S(2)}, u32[]{:S(2)}) collective-permute-start(bf16[16,2048]{1,0:T(8,128)(2,1)S(1)} %get-tuple-element.31.rest_7_), channel_id=1, source_target_pairs={{0,16},{4,20},{8,24},{12,28},{16,0},{20,4},{24,8},{28,12},{1,17},{... | collective-permute-start | bytes 196616 | tf_op jit(solution)/shard_map/ppermute | solution.py:23
  87.0 6.2 %collective-permute-start.15 = (bf16[16,2048]{1,0:T(8,128)(2,1)S(1)}, bf16[16,2048]{1,0:T(8,128)(2,1)S(1)}, u32[]{:S(2)}, u32[]{:S(2)}) collective-permute-start(bf16[16,2048]{1,0:T(8,128)(2,1)S(1)} %get-tuple-element.31.rest_7_), channel_id=1, source_target_pairs={{0,24},{4,28},{8,16},{12,20},{16,8},{20,12},{24,0},{28,4},{1,25},{... | collective-permute-start | bytes 196616 | tf_op jit(solution)/shard_map/ppermute | solution.py:23
  87.0 7.3 %collective-permute-start.21 = (bf16[16,2048]{1,0:T(8,128)(2,1)S(1)}, bf16[16,2048]{1,0:T(8,128)(2,1)S(1)}, u32[]{:S(2)}, u32[]{:S(2)}) collective-permute-start(bf16[16,2048]{1,0:T(8,128)(2,1)S(1)} %get-tuple-element.31.rest_7_), channel_id=1, source_target_pairs={{0,4},{4,0},{8,12},{12,8},{16,20},{20,16},{24,28},{28,24},{1,5},{5... | collective-permute-start | bytes 196616 | tf_op jit(solution)/shard_map/ppermute | solution.py:23
  88.6 5.7 %collective-permute-start.20 = (bf16[16,2048]{1,0:T(8,128)(2,1)S(1)}, bf16[16,2048]{1,0:T(8,128)(2,1)S(1)}, u32[]{:S(2)}, u32[]{:S(2)}) collective-permute-start(bf16[16,2048]{1,0:T(8,128)(2,1)S(1)} %collective-permute-done.19.rest_5_), channel_id=1, source_target_pairs={{0,4},{4,0},{8,12},{12,8},{16,20},{20,16},{24,28},{28,24},{1,5},{5... | collective-permute-start | bytes 196616 | tf_op jit(solution)/shard_map/ppermute | solution.py:23
  91.0 4.5 %collective-permute-start.18 = (bf16[16,2048]{1,0:T(8,128)(2,1)S(1)}, bf16[16,2048]{1,0:T(8,128)(2,1)S(1)}, u32[]{:S(2)}, u32[]{:S(2)}) collective-permute-start(bf16[16,2048]{1,0:T(8,128)(2,1)S(1)} %collective-permute-done.17.rest_3_), channel_id=1, source_target_pairs={{0,4},{4,0},{8,12},{12,8},{16,20},{20,16},{24,28},{28,24},{1,5},{5... | collective-permute-start | bytes 196616 | tf_op jit(solution)/shard_map/ppermute | solution.py:23
  93.1 4.3 %collective-permute-start.16 = (bf16[16,2048]{1,0:T(8,128)(2,1)S(1)}, bf16[16,2048]{1,0:T(8,128)(2,1)S(1)}, u32[]{:S(2)}, u32[]{:S(2)}) collective-permute-start(bf16[16,2048]{1,0:T(8,128)(2,1)S(1)} %collective-permute-done.15.rest_1_), channel_id=1, source_target_pairs={{0,4},{4,0},{8,12},{12,8},{16,20},{20,16},{24,28},{28,24},{1,5},{5... | collective-permute-start | bytes 196616 | tf_op jit(solution)/shard_map/ppermute | solution.py:23
  102.8 7.1 %collective-permute-start.26 = (bf16[16,2048]{1,0:T(8,128)(2,1)S(1)}, bf16[16,2048]{1,0:T(8,128)(2,1)S(1)}, u32[]{:S(2)}, u32[]{:S(2)}) collective-permute-start(bf16[16,2048]{1,0:T(8,128)(2,1)S(1)} %hop.4.rest_7_), channel_id=1, source_target_pairs={{0,8},{4,12},{8,0},{12,4},{16,24},{20,28},{24,16},{28,20},{1,9},{5... | collective-permute-start | bytes 196616 | tf_op jit(solution)/shard_map/ppermute | solution.py:23
  105.1 5.9 %collective-permute-start.24 = (bf16[16,2048]{1,0:T(8,128)(2,1)S(1)}, bf16[16,2048]{1,0:T(8,128)(2,1)S(1)}, u32[]{:S(2)}, u32[]{:S(2)}) collective-permute-start(bf16[16,2048]{1,0:T(8,128)(2,1)S(1)} %hop.4.rest_7_), channel_id=1, source_target_pairs={{0,16},{4,20},{8,24},{12,28},{16,0},{20,4},{24,8},{28,12},{1,17},{... | collective-permute-start | bytes 196616 | tf_op jit(solution)/shard_map/ppermute | solution.py:23
  107.9 6.1 %collective-permute-start.22 = (bf16[16,2048]{1,0:T(8,128)(2,1)S(1)}, bf16[16,2048]{1,0:T(8,128)(2,1)S(1)}, u32[]{:S(2)}, u32[]{:S(2)}) collective-permute-start(bf16[16,2048]{1,0:T(8,128)(2,1)S(1)} %hop.4.rest_7_), channel_id=1, source_target_pairs={{0,24},{4,28},{8,16},{12,20},{16,8},{20,12},{24,0},{28,4},{1,25},{... | collective-permute-start | bytes 196616 | tf_op jit(solution)/shard_map/ppermute | solution.py:23
  107.9 6.1 %collective-permute-start.28 = (bf16[16,2048]{1,0:T(8,128)(2,1)S(1)}, bf16[16,2048]{1,0:T(8,128)(2,1)S(1)}, u32[]{:S(2)}, u32[]{:S(2)}) collective-permute-start(bf16[16,2048]{1,0:T(8,128)(2,1)S(1)} %hop.4.rest_7_), channel_id=1, source_target_pairs={{0,4},{4,0},{8,12},{12,8},{16,20},{20,16},{24,28},{28,24},{1,5},{5... | collective-permute-start | bytes 196616 | tf_op jit(solution)/shard_map/ppermute | solution.py:23
  109.8 4.3 %collective-permute-start.27 = (bf16[16,2048]{1,0:T(8,128)(2,1)S(1)}, bf16[16,2048]{1,0:T(8,128)(2,1)S(1)}, u32[]{:S(2)}, u32[]{:S(2)}) collective-permute-start(bf16[16,2048]{1,0:T(8,128)(2,1)S(1)} %collective-permute-done.26.rest_5_), channel_id=1, source_target_pairs={{0,4},{4,0},{8,12},{12,8},{16,20},{20,16},{24,28},{28,24},{1,5},{5... | collective-permute-start | bytes 196616 | tf_op jit(solution)/shard_map/ppermute | solution.py:23
  111.0 4.3 %collective-permute-start.25 = (bf16[16,2048]{1,0:T(8,128)(2,1)S(1)}, bf16[16,2048]{1,0:T(8,128)(2,1)S(1)}, u32[]{:S(2)}, u32[]{:S(2)}) collective-permute-start(bf16[16,2048]{1,0:T(8,128)(2,1)S(1)} %collective-permute-done.24.rest_3_), channel_id=1, source_target_pairs={{0,4},{4,0},{8,12},{12,8},{16,20},{20,16},{24,28},{28,24},{1,5},{5... | collective-permute-start | bytes 196616 | tf_op jit(solution)/shard_map/ppermute | solution.py:23
  113.9 4.3 %collective-permute-start.23 = (bf16[16,2048]{1,0:T(8,128)(2,1)S(1)}, bf16[16,2048]{1,0:T(8,128)(2,1)S(1)}, u32[]{:S(2)}, u32[]{:S(2)}) collective-permute-start(bf16[16,2048]{1,0:T(8,128)(2,1)S(1)} %collective-permute-done.22.rest_1_), channel_id=1, source_target_pairs={{0,4},{4,0},{8,12},{12,8},{16,20},{20,16},{24,28},{28,24},{1,5},{5... | collective-permute-start | bytes 196616 | tf_op jit(solution)/shard_map/ppermute | solution.py:23
  123.6 1.9 %collective-permute-start.29 = (f32[16,512]{1,0:T(8,128)S(1)}, f32[16,512]{1,0:T(8,128)S(1)}, u32[]{:S(2)}, u32[]{:S(2)}) collective-permute-start(f32[16,512]{1,0:T(8,128)S(1)} %get-tuple-element.34), channel_id=1, source_target_pairs={{0,1},{1,0},{2,3},{3,2},{4,5},{5,4},{6,7},{7,6},{8,9},{9,8},{10,11... | collective-permute-start | bytes 98312 | tf_op jit(solution)/shard_map/ppermute | solution.py:23
  123.7 4.2 %collective-permute-start.30 = (f32[16,512]{1,0:T(8,128)S(1)}, f32[16,512]{1,0:T(8,128)S(1)}, u32[]{:S(2)}, u32[]{:S(2)}) collective-permute-start(f32[16,512]{1,0:T(8,128)S(1)} %get-tuple-element.35), channel_id=1, source_target_pairs={{0,2},{1,3},{2,0},{3,1},{4,6},{5,7},{6,4},{7,5},{8,10},{9,11},{10,... | collective-permute-start | bytes 98312 | tf_op jit(solution)/shard_map/ppermute | solution.py:23
  124.0 3.8 %collective-permute-start.31 = (f32[16,512]{1,0:T(8,128)S(1)}, f32[16,512]{1,0:T(8,128)S(1)}, u32[]{:S(2)}, u32[]{:S(2)}) collective-permute-start(f32[16,512]{1,0:T(8,128)S(1)} %get-tuple-element.36), channel_id=1, source_target_pairs={{0,3},{1,2},{2,1},{3,0},{4,7},{5,6},{6,5},{7,4},{8,11},{9,10},{10,... | collective-permute-start | bytes 98312 | tf_op jit(solution)/shard_map/ppermute | solution.py:23

commit v2 on v1

--- a/solution.py
+++ b/solution.py
@@ -222,7 +222,7 @@
     )(value, *ready)
 
 
-def hop_kernel(first, last, parts, spans, scale, meta, here, *rest):
+def hop_kernel(first, last, parts, spans, scale, meta, part, place, *rest):
     shards, rest = rest[:parts][::-1], rest[parts:]
     chunks, rest = rest[: len(spans)], rest[len(spans) :]
     (tele, inverse), outs, (slabs, inflow) = rest[:2], rest[2:-2], rest[-2:]
@@ -234,44 +234,48 @@
         for b in range(blocks):
             slabs[j * blocks + b] = shard[:, b * block : (b + 1) * block]
 
+    split = meta.shape[0] // LABELS
     empty = jnp.zeros((per, block), jnp.bfloat16)
-    for tiles, (q, begin) in zip(chunks, spans):
-        count = meta[q * LABELS + 2, 0]
-        size = tiles.shape[0]
-        groups = (jnp.clip(count - begin, 0, size) + (TILE_GROUP - 1)) // TILE_GROUP
+    counts = [meta[q * LABELS + 2, 0] for q in range(split)]
+    most = functools.reduce(jnp.maximum, counts)
+    edges = sorted({begin for _, begin in spans})
+    edges.append(edges[-1] + chunks[-1].shape[0])
+
+    def quads(q, tiles, begin, at):
+        for c in range(0, TILE_GROUP, 4):
+            held, quad, into = [], [], []
+            for i in range(c, c + 4):
+                k = begin + at + i
+                source = meta[q * LABELS, k] ^ (part[0] * blocks)
+                held.append(slabs[jnp.where(k < counts[q], source, parts * blocks)])
+                quad.append(tiles[at + i])
+                into.append(meta[q * LABELS + 1, k])
+            left = jnp.concatenate(
+                [
+                    jnp.concatenate([held[0], held[1], empty, empty], axis=0),
+                    jnp.concatenate([empty, empty, held[2], held[3]], axis=0),
+                ],
+                axis=1,
+            )
+            right = jnp.concatenate(
+                [jnp.concatenate(quad[:2], axis=0), jnp.concatenate(quad[2:], axis=0)], axis=1
+            )
+            both = lax.dot_general(left, right, NT, preferred_element_type=jnp.float32)
+            for i in range(4):
+                side = (i % 2) * block
+                inflow[into[i]] += both[i * per : (i + 1) * per, side : side + block]
+
+    for first_slot, end_slot in zip(edges[:-1], edges[1:]):
+        groups = jnp.clip(most - first_slot, 0, end_slot - first_slot) + (TILE_GROUP - 1)
 
         def group(step, carry):
-            products = []
-            for c in range(0, TILE_GROUP, 4):
-                held, quad = [], []
-                for i in range(4):
-                    at = step * TILE_GROUP + c + i
-                    source = meta[q * LABELS, begin + at] ^ here[0]
-                    held.append(slabs[jnp.where(begin + at < count, source, parts * blocks)])
-                    quad.append(tiles[at])
-                left = jnp.concatenate(
-                    [
-                        jnp.concatenate([held[0], held[1], empty, empty], axis=0),
-                        jnp.concatenate([empty, empty, held[2], held[3]], axis=0),
-                    ],
-                    axis=1,
-                )
-                right = jnp.concatenate(
-                    [
-                        jnp.concatenate(quad[:2], axis=0),
-                        jnp.concatenate(quad[2:], axis=0),
-                    ],
-                    axis=1,
-                )
-                both = lax.dot_general(left, right, NT, preferred_element_type=jnp.float32)
-                for i in range(4):
-                    side = (i % 2) * block
-                    products.append(both[i * per : (i + 1) * per, side : side + block])
-            for i in range(TILE_GROUP):
-                inflow[meta[q * LABELS + 1, begin + step * TILE_GROUP + i]] += products[i]
+            for q in range(split):
+                for tiles, (owner, begin) in zip(chunks, spans):
+                    if owner == q and begin <= first_slot < begin + tiles.shape[0]:
+                        quads(q, tiles, begin, first_slot - begin + step * TILE_GROUP)
             return carry
 
-        lax.fori_loop(0, groups, group, 0)
+        lax.fori_loop(0, groups // TILE_GROUP, group, 0)
 
     if first:
         tail = sum(s[:, blocks * block :].astype(jnp.float32) for s in shards)
@@ -290,12 +294,12 @@
     if last:
         count = outs[0].shape[1] // block
         for j, out in enumerate(outs):
-            start = (here[1] ^ j) * count
+            start = (place[0] ^ j) * count
             for i in range(count):
                 out[:, i * block : (i + 1) * block] = inflow[start + i]
 
 
-def hop(first, last, meta, here, shards, sets, tele, inverse):
+def hop(first, last, meta, part, place, shards, sets, tele, inverse):
     per, hosts = tele.shape
     slots = sum(chunk.shape[0] for chunk in sets[0])
     block = sets[0][0].shape[1]
@@ -318,7 +322,7 @@
     vmem = pl.BlockSpec(memory_space=pltpu.VMEM)
     return pl.pallas_call(
         functools.partial(hop_kernel, first, last, parts, spans, float(parts * hosts)),
-        in_specs=[smem] * 2 + [vmem] * (parts + len(chunks) + 2),
+        in_specs=[smem] * 3 + [vmem] * (parts + len(chunks) + 2),
         out_specs=[vmem] * len(out_shape),
         scratch_shapes=[
             pltpu.VMEM((parts * blocks + 1, per, block), jnp.bfloat16),
@@ -332,17 +336,17 @@
             transcendentals=0,
         ),
         name="hop",
-    )(meta, here, *reversed(shards), *chunks, tele, inverse)
-
-
-def finish_kernel(here, *rest):
+    )(meta, part, place, *reversed(shards), *chunks, tele, inverse)
+
+
+def finish_kernel(place, *rest):
     chunks, out = rest[:-1], rest[-1]
     per = chunks[0].shape[0]
     for j, chunk in enumerate(chunks):
-        out[pl.ds(pl.multiple_of((here[1] ^ j) * per, 8), per), :] = chunk[...]
-
-
-def finish(here, chunks):
+        out[pl.ds(pl.multiple_of((place[0] ^ j) * per, 8), per), :] = chunk[...]
+
+
+def finish(place, chunks):
     per, rows = chunks[0].shape
     topics = per * len(chunks)
     return pl.pallas_call(
@@ -352,7 +356,7 @@
         out_shape=jax.ShapeDtypeStruct((topics, rows), jnp.float32),
         compiler_params=pltpu.CompilerParams(vmem_limit_bytes=16 * MIB),
         name="finish",
-    )(here, *chunks)
+    )(place, *chunks)
 
 
 def spread(sent, axis):
@@ -372,8 +376,8 @@
     slots, block, _ = tiles.shape
     parts, split = lax.axis_size("hst"), lax.axis_size("doc")
     blocks = hosts // block
-    place = lax.axis_index("doc").astype(jnp.int32)
-    here = jnp.stack([lax.axis_index("hst").astype(jnp.int32) * blocks, place])
+    part = lax.axis_index("hst").astype(jnp.int32).reshape(1)
+    place = lax.axis_index("doc").astype(jnp.int32).reshape(1)
     labels = [label.reshape(1, -1) for label in (src_block, dst_block, tile_count)]
 
     near = xor_send(tiles, "doc", 1)
@@ -382,15 +386,14 @@
     far = {j: [xor_send(early, "doc", j)] for j in range(2, split, 2)}
     degrees = column_sums(src_block, tile_count, tiles, parts, blocks)
     degrees = lax.all_to_all(degrees, "hst", split_axis=0, concat_axis=0, tiled=True)
-    sums = documents(docs, w_in, w_out, doc_host, hosts, split, place.reshape(1), degrees, labels)
+    sums = documents(docs, w_in, w_out, doc_host, hosts, split, place, degrees, labels)
     sums = [sums[0]] + [xor_send(sums[j], "doc", j) for j in range(1, split)]
-    crossed = [far[j][0] for j in range(2, split, 2)]
-    sent, tele, inverse, meta, late, *crossed = start_values(
-        teleport, sums, block, [late] + crossed
-    )
     for j in range(2, split, 2):
-        far[j] = [crossed[j // 2 - 1], xor_send(late, "doc", j)]
+        far[j][0] = after(far[j][0], [sums[1]])
         far[j + 1] = [xor_send(far[j][0], "doc", 1)]
+    sent, tele, inverse, meta, late = start_values(teleport, sums, block, [late])
+    for j in range(2, split, 2):
+        far[j].append(xor_send(late, "doc", j))
     for step in range(HOPS):
         first, last = step == 0, step == HOPS - 1
         shards = spread(sent, "hst")
@@ -399,12 +402,12 @@
                 far[j][1] = after(far[j][1], shards[1:])
                 far[j + 1].append(xor_send(far[j][1], "doc", 1))
             sets = [[tiles], [near]] + [far[j] for j in range(2, split)]
-        outs = hop(first, last, meta, here, shards, sets, tele, inverse)
+        outs = hop(first, last, meta, part, place, shards, sets, tele, inverse)
         sent = outs[0]
         if first:
             tele = outs[1]
     chunks = [outs[0]] + [xor_send(outs[j], "doc", j) for j in range(1, split)]
-    return finish(here, chunks).T
+    return finish(place, chunks).T
 
 
 def solution(mesh):

time: 129 us -> 131 us (1.016)
  starting transfers between devices: 46 us -> 48.2 us
    ppermute x32, starting transfers between devices: 40.2 us -> 42.3 us  [xor_send(): return lax.ppermute(value, axis, [(i, i ^ step) for i in range(size)])]
  transfers between devices with their start and end apart: 33 -> 33, of which waited for: 18 -> 20; matrix products, arithmetic and copies ran while one was open for 0% -> 0% of each run, Pallas kernels for 13% -> 13%
where the time goes in v2:
time: 131 us
  starting transfers between devices  48.2 us (37%)
  waiting for transfers between devices  39.1 us (30%)
  Pallas kernels  35 us (27%)
  local copies, waits for them, and re-layouts  7.76 us (6%)
    ppermute x32, starting transfers between devices, xor_send(): return lax.ppermute(value, axis, [(i, i ^ step) for i in range(size)])  42.3 us
    ppermute x32, waiting for transfers between devices, xor_send(): return lax.ppermute(value, axis, [(i, i ^ step) for i in range(size)])  32.2 us
    pallas_call x3, Pallas kernels, hop(): pl.pallas_call(functools.partial(hop_kernel, first, last, parts, spans, f...  17.4 us
    pallas_call x1, Pallas kernels, documents(): pl.pallas_call(documents_kernel, grid_spec=pltpu.PrefetchScalarGridSpec(n...  15.1 us
    all_to_all x1, waiting for transfers between devices, body(): lax.all_to_all(degrees, 'hst', split_axis=0, concat_axis=0, tiled=True)  6.89 us
    all_to_all x1, starting transfers between devices, body(): lax.all_to_all(degrees, 'hst', split_axis=0, concat_axis=0, tiled=True)  5.82 us
    unnamed x30, local copies, waits for them, and re-layouts  4.84 us
    slice x2, local copies, waits for them, and re-layouts, body(): early, late = (tiles[:cut], tiles[cut:])  2.92 us
  transfers between devices with their start and end apart: 33, of which 20 were waited for; matrix products, arithmetic and copies ran while one was open for 0% of the time, Pallas kernels for 13%

profile of v2, /device:TPU:0, one launch (start us, length us, event | category | flops | bytes accessed | tf_op | source)
XLA Modules:
  0.0 130.8 jit_solution(357447263355059706)
XLA Ops:
  0.0 2.9 %slice.7 = bf16[48,128,128]{2,1,0:T(8,128)(2,1)} slice(bf16[64,128,128]{2,1,0:T(8,128)(2,1)} %rest_8_.5), slice={[0:48], [0:128], [0:128]} | slice | bytes 3145728 | tf_op jit(solution)/shard_map/slice | solution.py:385
  2.9 3.0 %collective-permute-start.11 = (bf16[48,128,128]{2,1,0:T(8,128)(2,1)}, bf16[48,128,128]{2,1,0:T(8,128)(2,1)}, u32[]{:S(2)}, u32[]{:S(2)}) collective-permute-start(bf16[48,128,128]{2,1,0:T(8,128)(2,1)} %slice.7), channel_id=1, source_target_pairs={{0,2},{1,3},{2,0},{3,1},{4,6},{5,7},{6,4},{7,5},{8,10},{9,11},{10,... | collective-permute-start | bytes 4718600 | tf_op jit(solution)/shard_map/ppermute | solution.py:23
  6.6 1.7 %column_sums.1 = f32[8,16,128]{2,1,0:T(8,128)} custom-call(s32[64]{0:T(128)S(1)} %copy-done.10, s32[1]{0:T(128)} %copy.16.count, bf16[64,128,128]{2,1,0:T(8,128)(2,1)S(1)} %copy-done), custom_call_target="tpu_custom_call" | custom-call | flops 1048576 | bytes 2097152 | tf_op jit(solution)/shard_map/column_sums/pallas_call | solution.py:49
  8.3 5.8 %all-to-all-start = ((f32[8,16,128]{2,1,0:T(8,128)}), f32[8,16,128]{2,1,0:T(8,128)S(1)}, u32[]{:S(2)}, u32[]{:S(2)}) async-start(f32[8,16,128]{2,1,0:T(8,128)} %column_sums.1), calls=%async_computation | async-start | bytes 131072 | tf_op jit(solution)/shard_map/all_to_all | solution.py:388
  14.1 6.9 %all-to-all-done.degrees = f32[8,16,128]{2,1,0:T(8,128)S(1)} async-done(((f32[8,16,128]{2,1,0:T(8,128)}), f32[8,16,128]{2,1,0:T(8,128)S(1)}, u32[]{:S(2)}, u32[]{:S(2)}) %all-to-all-start) | async-done | bytes 65568 | tf_op jit(solution)/shard_map/all_to_all | solution.py:388
  21.0 15.1 %documents.1 = (f32[16,2304]{1,0:T(8,128)S(1)}, f32[16,2304]{1,0:T(8,128)S(1)}, f32[16,2304]{1,0:T(8,128)S(1)}, f32[16,2304]{1,0:T(8,128)S(1)}) custom-call(s32[1]{0:T(128)} %bitcast.place, bf16[8192,768]{1,0:T(8,128)(2,1)} %docs.1, bf16[768,256]{1,0:T(8,128)(2,1)S(1)} %copy-done.11, bf16[64,256]{1,0:T(8,128)(2,1)S(1)} %bitcast.12, ...), custom_call_target="tpu_custom_call" | custom-call | flops 7784628224 | bytes 12582912 | tf_op jit(solution)/shard_map/documents/pallas_call | solution.py:129
  36.2 0.0 copy-start.9
  36.2 0.1 collective-permute-start
  36.2 1.4 %collective-permute-done.rest_1_.refs_1_ = f32[16,2304]{1,0:T(8,128)S(1)} collective-permute-done((f32[16,2304]{1,0:T(8,128)S(1)}, f32[16,2304]{1,0:T(8,128)S(1)}, u32[]{:S(2)}, u32[]{:S(2)}) %collective-permute-start) | collective-permute-done | bytes 147488 | tf_op jit(solution)/shard_map/ppermute | solution.py:23
  37.6 3.0 %collective-permute-done.11.refs_0_ = bf16[48,128,128]{2,1,0:T(8,128)(2,1)} collective-permute-done((bf16[48,128,128]{2,1,0:T(8,128)(2,1)}, bf16[48,128,128]{2,1,0:T(8,128)(2,1)}, u32[]{:S(2)}, u32[]{:S(2)}) %collective-permute-start.11) | collective-permute-done | bytes 1572896 | tf_op jit(solution)/shard_map/ppermute | solution.py:23
  40.7 1.7 %collective-permute-start.1 = (f32[16,2304]{1,0:T(8,128)S(1)}, f32[16,2304]{1,0:T(8,128)S(1)}, u32[]{:S(2)}, u32[]{:S(2)}) collective-permute-start(f32[16,2304]{1,0:T(8,128)S(1)} %get-tuple-element.22), channel_id=1, source_target_pairs={{0,2},{1,3},{2,0},{3,1},{4,6},{5,7},{6,4},{7,5},{8,10},{9,11},{10,... | collective-permute-start | bytes 442376 | tf_op jit(solution)/shard_map/ppermute | solution.py:23
  42.4 0.1 collective-permute-start.2
  42.6 4.7 %collective-permute-done.1.rest_2_ = f32[16,2304]{1,0:T(8,128)S(1)} collective-permute-done((f32[16,2304]{1,0:T(8,128)S(1)}, f32[16,2304]{1,0:T(8,128)S(1)}, u32[]{:S(2)}, u32[]{:S(2)}) %collective-permute-start.1) | collective-permute-done | bytes 147488 | tf_op jit(solution)/shard_map/ppermute | solution.py:23
  47.3 2.4 %collective-permute-done.2.rest_3_ = f32[16,2304]{1,0:T(8,128)S(1)} collective-permute-done((f32[16,2304]{1,0:T(8,128)S(1)}, f32[16,2304]{1,0:T(8,128)S(1)}, u32[]{:S(2)}, u32[]{:S(2)}) %collective-permute-start.2) | collective-permute-done | bytes 147488 | tf_op jit(solution)/shard_map/ppermute | solution.py:23
  49.7 0.1 start_values.1
  49.8 0.0 copy-start.5
  49.8 1.8 %collective-permute-start.12 = (bf16[16,128,128]{2,1,0:T(8,128)(2,1)S(1)}, bf16[16,128,128]{2,1,0:T(8,128)(2,1)S(1)}, u32[]{:S(2)}, u32[]{:S(2)}) collective-permute-start(bf16[16,128,128]{2,1,0:T(8,128)(2,1)S(1)} %get-tuple-element.26), channel_id=1, source_target_pairs={{0,2},{1,3},{2,0},{3,1},{4,6},{5,7},{6,4},{7,5},{8,10},{9,11},{10,... | collective-permute-start | bytes 1572872 | tf_op jit(solution)/shard_map/ppermute | solution.py:23
  51.7 1.5 %collective-permute-start.9 = (bf16[16,2176]{1,0:T(8,128)(2,1)S(1)}, bf16[16,2176]{1,0:T(8,128)(2,1)S(1)}, u32[]{:S(2)}, u32[]{:S(2)}) collective-permute-start(bf16[16,2176]{1,0:T(8,128)(2,1)S(1)} %get-tuple-element.25.rest_7_), channel_id=1, source_target_pairs={{0,4},{4,0},{8,12},{12,8},{16,20},{20,16},{24,28},{28,24},{1,5},{5... | collective-permute-start | bytes 208904 | tf_op jit(solution)/shard_map/ppermute | solution.py:23
  53.1 1.6 %collective-permute-start.7 = (bf16[16,2176]{1,0:T(8,128)(2,1)S(1)}, bf16[16,2176]{1,0:T(8,128)(2,1)S(1)}, u32[]{:S(2)}, u32[]{:S(2)}) collective-permute-start(bf16[16,2176]{1,0:T(8,128)(2,1)S(1)} %get-tuple-element.25.rest_7_), channel_id=1, source_target_pairs={{0,8},{4,12},{8,0},{12,4},{16,24},{20,28},{24,16},{28,20},{1,9},{5... | collective-permute-start | bytes 208904 | tf_op jit(solution)/shard_map/ppermute | solution.py:23
  54.7 1.2 collective-permute-done.9.refs_1_.rest_6_
  56.0 2.6 %collective-permute-start.5 = (bf16[16,2176]{1,0:T(8,128)(2,1)S(1)}, bf16[16,2176]{1,0:T(8,128)(2,1)S(1)}, u32[]{:S(2)}, u32[]{:S(2)}) collective-permute-start(bf16[16,2176]{1,0:T(8,128)(2,1)S(1)} %get-tuple-element.25.rest_7_), channel_id=1, source_target_pairs={{0,16},{4,20},{8,24},{12,28},{16,0},{20,4},{24,8},{28,12},{1,17},{... | collective-permute-start | bytes 208904 | tf_op jit(solution)/shard_map/ppermute | solution.py:23
  58.6 2.5 %collective-permute-start.3 = (bf16[16,2176]{1,0:T(8,128)(2,1)S(1)}, bf16[16,2176]{1,0:T(8,128)(2,1)S(1)}, u32[]{:S(2)}, u32[]{:S(2)}) collective-permute-start(bf16[16,2176]{1,0:T(8,128)(2,1)S(1)} %get-tuple-element.25.rest_7_), channel_id=1, source_target_pairs={{0,24},{4,28},{8,16},{12,20},{16,8},{20,12},{24,0},{28,4},{1,25},{... | collective-permute-start | bytes 208904 | tf_op jit(solution)/shard_map/ppermute | solution.py:23
  61.1 0.4 collective-permute-done.5.refs_4_.rest_3_
  61.5 1.5 %collective-permute-start.8 = (bf16[16,2176]{1,0:T(8,128)(2,1)S(1)}, bf16[16,2176]{1,0:T(8,128)(2,1)S(1)}, u32[]{:S(2)}, u32[]{:S(2)}) collective-permute-start(bf16[16,2176]{1,0:T(8,128)(2,1)S(1)} %collective-permute-done.7.refs_2_.rest_5_), channel_id=1, source_target_pairs={{0,4},{4,0},{8,12},{12,8},{16,20},{20,16},{24,28},{28,24},{1,5},{5... | collective-permute-start | bytes 208904 | tf_op jit(solution)/shard_map/ppermute | solution.py:23
  63.0 1.8 %collective-permute-done.3.refs_6_.rest_1_ = bf16[16,2176]{1,0:T(8,128)(2,1)S(1)} collective-permute-done((bf16[16,2176]{1,0:T(8,128)(2,1)S(1)}, bf16[16,2176]{1,0:T(8,128)(2,1)S(1)}, u32[]{:S(2)}, u32[]{:S(2)}) %collective-permute-start.3) | collective-permute-done | bytes 69664 | tf_op jit(solution)/shard_map/ppermute | solution.py:23
  64.8 1.5 %collective-permute-start.6 = (bf16[16,2176]{1,0:T(8,128)(2,1)S(1)}, bf16[16,2176]{1,0:T(8,128)(2,1)S(1)}, u32[]{:S(2)}, u32[]{:S(2)}) collective-permute-start(bf16[16,2176]{1,0:T(8,128)(2,1)S(1)} %collective-permute-done.5.refs_4_.rest_3_), channel_id=1, source_target_pairs={{0,4},{4,0},{8,12},{12,8},{16,20},{20,16},{24,28},{28,24},{1,5},{5... | collective-permute-start | bytes 208904 | tf_op jit(solution)/shard_map/ppermute | solution.py:23
  66.3 1.4 %collective-permute-start.4 = (bf16[16,2176]{1,0:T(8,128)(2,1)S(1)}, bf16[16,2176]{1,0:T(8,128)(2,1)S(1)}, u32[]{:S(2)}, u32[]{:S(2)}) collective-permute-start(bf16[16,2176]{1,0:T(8,128)(2,1)S(1)} %collective-permute-done.3.refs_6_.rest_1_), channel_id=1, source_target_pairs={{0,4},{4,0},{8,12},{12,8},{16,20},{20,16},{24,28},{28,24},{1,5},{5... | collective-permute-start | bytes 208904 | tf_op jit(solution)/shard_map/ppermute | solution.py:23
  67.7 1.4 %collective-permute-done.6.refs_5_.rest_2_ = bf16[16,2176]{1,0:T(8,128)(2,1)S(1)} collective-permute-done((bf16[16,2176]{1,0:T(8,128)(2,1)S(1)}, bf16[16,2176]{1,0:T(8,128)(2,1)S(1)}, u32[]{:S(2)}, u32[]{:S(2)}) %collective-permute-start.6) | collective-permute-done | bytes 69664 | tf_op jit(solution)/shard_map/ppermute | solution.py:23
  69.1 1.5 %collective-permute-done.4.refs_7_.rest_0_ = bf16[16,2176]{1,0:T(8,128)(2,1)S(1)} collective-permute-done((bf16[16,2176]{1,0:T(8,128)(2,1)S(1)}, bf16[16,2176]{1,0:T(8,128)(2,1)S(1)}, u32[]{:S(2)}, u32[]{:S(2)}) %collective-permute-start.4) | collective-permute-done | bytes 69664 | tf_op jit(solution)/shard_map/ppermute | solution.py:23
  70.6 0.6 copy-done.1
  71.2 0.6 copy-done.3
  71.8 1.9 %collective-permute-done.14.rest_13_ = bf16[16,128,128]{2,1,0:T(8,128)(2,1)S(1)} collective-permute-done((bf16[16,128,128]{2,1,0:T(8,128)(2,1)S(1)}, bf16[16,128,128]{2,1,0:T(8,128)(2,1)S(1)}, u32[]{:S(2)}, u32[]{:S(2)}) %collective-permute-start.14) | collective-permute-done | bytes 524320 | tf_op jit(solution)/shard_map/ppermute | solution.py:23
  73.8 0.9 copy-done.2
  74.7 0.9 copy-done.4
  75.5 0.9 copy-done.6
  76.4 0.9 copy-done.8
  77.3 5.9 %hop.3 = (bf16[16,2048]{1,0:T(8,128)(2,1)S(1)}, f32[16,2048]{1,0:T(8,128)S(1)}) custom-call(s32[12,128]{1,0:T(8,128)S(1)} %get-tuple-element.24.meta, s32[1]{0:T(128)} %bitcast.7.part, s32[1]{0:T(128)} %bitcast.place, bf16[16,2176]{1,0:T(8,128)(2,1)S(1)} %copy-done.4, bf16[16,2176]{1,0:T(8,128)(2,1)S(1)} %collective-permute-done.3.refs_6_.rest_1_, ...), custom_call_target="tpu_custom_call" | custom-call | flops 134217728 | bytes 8388608 | tf_op jit(solution)/shard_map/hop/pallas_call | solution.py:323
  83.2 2.7 %collective-permute-start.19 = (bf16[16,2048]{1,0:T(8,128)(2,1)S(1)}, bf16[16,2048]{1,0:T(8,128)(2,1)S(1)}, u32[]{:S(2)}, u32[]{:S(2)}) collective-permute-start(bf16[16,2048]{1,0:T(8,128)(2,1)S(1)} %get-tuple-element.29.rest_7_), channel_id=1, source_target_pairs={{0,8},{4,12},{8,0},{12,4},{16,24},{20,28},{24,16},{28,20},{1,9},{5... | collective-permute-start | bytes 196616 | tf_op jit(solution)/shard_map/ppermute | solution.py:23
  85.8 3.2 %collective-permute-start.17 = (bf16[16,2048]{1,0:T(8,128)(2,1)S(1)}, bf16[16,2048]{1,0:T(8,128)(2,1)S(1)}, u32[]{:S(2)}, u32[]{:S(2)}) collective-permute-start(bf16[16,2048]{1,0:T(8,128)(2,1)S(1)} %get-tuple-element.29.rest_7_), channel_id=1, source_target_pairs={{0,16},{4,20},{8,24},{12,28},{16,0},{20,4},{24,8},{28,12},{1,17},{... | collective-permute-start | bytes 196616 | tf_op jit(solution)/shard_map/ppermute | solution.py:23
  89.1 2.0 %collective-permute-start.21 = (bf16[16,2048]{1,0:T(8,128)(2,1)S(1)}, bf16[16,2048]{1,0:T(8,128)(2,1)S(1)}, u32[]{:S(2)}, u32[]{:S(2)}) collective-permute-start(bf16[16,2048]{1,0:T(8,128)(2,1)S(1)} %get-tuple-element.29.rest_7_), channel_id=1, source_target_pairs={{0,4},{4,0},{8,12},{12,8},{16,20},{20,16},{24,28},{28,24},{1,5},{5... | collective-permute-start | bytes 196616 | tf_op jit(solution)/shard_map/ppermute | solution.py:23
  91.1 0.1 collective-permute-start.20
  91.2 1.9 %collective-permute-done.17.rest_3_ = bf16[16,2048]{1,0:T(8,128)(2,1)S(1)} collective-permute-done((bf16[16,2048]{1,0:T(8,128)(2,1)S(1)}, bf16[16,2048]{1,0:T(8,128)(2,1)S(1)}, u32[]{:S(2)}, u32[]{:S(2)}) %collective-permute-start.17) | collective-permute-done | bytes 65568 | tf_op jit(solution)/shard_map/ppermute | solution.py:23
  93.1 2.0 %collective-permute-start.18 = (bf16[16,2048]{1,0:T(8,128)(2,1)S(1)}, bf16[16,2048]{1,0:T(8,128)(2,1)S(1)}, u32[]{:S(2)}, u32[]{:S(2)}) collective-permute-start(bf16[16,2048]{1,0:T(8,128)(2,1)S(1)} %collective-permute-done.17.rest_3_), channel_id=1, source_target_pairs={{0,4},{4,0},{8,12},{12,8},{16,20},{20,16},{24,28},{28,24},{1,5},{5... | collective-permute-start | bytes 196616 | tf_op jit(solution)/shard_map/ppermute | solution.py:23
  95.1 0.1 collective-permute-done.15.rest_1_
  95.2 2.0 %collective-permute-start.16 = (bf16[16,2048]{1,0:T(8,128)(2,1)S(1)}, bf16[16,2048]{1,0:T(8,128)(2,1)S(1)}, u32[]{:S(2)}, u32[]{:S(2)}) collective-permute-start(bf16[16,2048]{1,0:T(8,128)(2,1)S(1)} %collective-permute-done.15.rest_1_), channel_id=1, source_target_pairs={{0,4},{4,0},{8,12},{12,8},{16,20},{20,16},{24,28},{28,24},{1,5},{5... | collective-permute-start | bytes 196616 | tf_op jit(solution)/shard_map/ppermute | solution.py:23
  97.3 0.7 collective-permute-done.18.rest_2_
  97.9 1.6 %collective-permute-done.16.rest_0_ = bf16[16,2048]{1,0:T(8,128)(2,1)S(1)} collective-permute-done((bf16[16,2048]{1,0:T(8,128)(2,1)S(1)}, bf16[16,2048]{1,0:T(8,128)(2,1)S(1)}, u32[]{:S(2)}, u32[]{:S(2)}) %collective-permute-start.16) | collective-permute-done | bytes 65568 | tf_op jit(solution)/shard_map/ppermute | solution.py:23
  99.5 5.8 %hop.4.rest_7_ = bf16[16,2048]{1,0:T(8,128)(2,1)S(1)} custom-call(s32[12,128]{1,0:T(8,128)S(1)} %get-tuple-element.24.meta, s32[1]{0:T(128)} %bitcast.7.part, s32[1]{0:T(128)} %bitcast.place, bf16[16,2048]{1,0:T(8,128)(2,1)S(1)} %collective-permute-done.16.rest_0_, bf16[16,2048]{1,0:T(8,128)(2,1)S(1)} %collective-permute-done.15.rest_1_, ...), custom_call_target="tpu_custom_call" | custom-call | flops 134217728 | bytes 8388608 | tf_op jit(solution)/shard_map/hop/pallas_call | solution.py:323
  105.3 1.2 collective-permute-start.26
  106.4 3.4 %collective-permute-start.24 = (bf16[16,2048]{1,0:T(8,128)(2,1)S(1)}, bf16[16,2048]{1,0:T(8,128)(2,1)S(1)}, u32[]{:S(2)}, u32[]{:S(2)}) collective-permute-start(bf16[16,2048]{1,0:T(8,128)(2,1)S(1)} %hop.4.rest_7_), channel_id=1, source_target_pairs={{0,16},{4,20},{8,24},{12,28},{16,0},{20,4},{24,8},{28,12},{1,17},{... | collective-permute-start | bytes 196616 | tf_op jit(solution)/shard_map/ppermute | solution.py:23
  109.8 1.9 %collective-permute-start.28 = (bf16[16,2048]{1,0:T(8,128)(2,1)S(1)}, bf16[16,2048]{1,0:T(8,128)(2,1)S(1)}, u32[]{:S(2)}, u32[]{:S(2)}) collective-permute-start(bf16[16,2048]{1,0:T(8,128)(2,1)S(1)} %hop.4.rest_7_), channel_id=1, source_target_pairs={{0,4},{4,0},{8,12},{12,8},{16,20},{20,16},{24,28},{28,24},{1,5},{5... | collective-permute-start | bytes 196616 | tf_op jit(solution)/shard_map/ppermute | solution.py:23
  111.7 0.8 collective-permute-start.27
  112.6 0.2 collective-permute-done.24.rest_3_
  112.8 1.0 collective-permute-start.25
  113.8 2.1 %collective-permute-done.22.rest_1_ = bf16[16,2048]{1,0:T(8,128)(2,1)S(1)} collective-permute-done((bf16[16,2048]{1,0:T(8,128)(2,1)S(1)}, bf16[16,2048]{1,0:T(8,128)(2,1)S(1)}, u32[]{:S(2)}, u32[]{:S(2)}) %collective-permute-start.22) | collective-permute-done | bytes 65568 | tf_op jit(solution)/shard_map/ppermute | solution.py:23
  115.9 0.7 collective-permute-start.23
  116.6 0.4 collective-permute-done.25.rest_2_
  117.0 3.1 %collective-permute-done.23.rest_0_ = bf16[16,2048]{1,0:T(8,128)(2,1)S(1)} collective-permute-done((bf16[16,2048]{1,0:T(8,128)(2,1)S(1)}, bf16[16,2048]{1,0:T(8,128)(2,1)S(1)}, u32[]{:S(2)}, u32[]{:S(2)}) %collective-permute-start.23) | collective-permute-done | bytes 65568 | tf_op jit(solution)/shard_map/ppermute | solution.py:23
  120.1 5.8 %hop.5 = (f32[16,512]{1,0:T(8,128)S(1)}, f32[16,512]{1,0:T(8,128)S(1)}, f32[16,512]{1,0:T(8,128)S(1)}, f32[16,512]{1,0:T(8,128)S(1)}) custom-call(s32[12,128]{1,0:T(8,128)S(1)} %get-tuple-element.24.meta, s32[1]{0:T(128)} %bitcast.7.part, s32[1]{0:T(128)} %bitcast.place, bf16[16,2048]{1,0:T(8,128)(2,1)S(1)} %collective-permute-done.23.rest_0_, ...), custom_call_target="tpu_custom_call" | custom-call | flops 134217728 | bytes 8388608 | tf_op jit(solution)/shard_map/hop/pallas_call | solution.py:323
  125.9 0.1 collective-permute-start.29
  126.0 0.4 collective-permute-start.30
  126.4 1.5 %collective-permute-start.31 = (f32[16,512]{1,0:T(8,128)S(1)}, f32[16,512]{1,0:T(8,128)S(1)}, u32[]{:S(2)}, u32[]{:S(2)}) collective-permute-start(f32[16,512]{1,0:T(8,128)S(1)} %get-tuple-element.34), channel_id=1, source_target_pairs={{0,3},{1,2},{2,1},{3,0},{4,7},{5,6},{6,5},{7,4},{8,11},{9,10},{10,... | collective-permute-start | bytes 98312 | tf_op jit(solution)/shard_map/ppermute | solution.py:23
  127.9 2.3 %collective-permute-done.30.rest_2_ = f32[16,512]{1,0:T(8,128)S(1)} collective-permute-done((f32[16,512]{1,0:T(8,128)S(1)}, f32[16,512]{1,0:T(8,128)S(1)}, u32[]{:S(2)}, u32[]{:S(2)}) %collective-permute-start.30) | collective-permute-done | bytes 32800 | tf_op jit(solution)/shard_map/ppermute | solution.py:23
  130.2 0.7 finish.1
  (43 shorter events, 0.1 us)
Async XLA Ops:
  0.0 6.6 %copy-start = (bf16[64,128,128]{2,1,0:T(8,128)(2,1)S(1)}, bf16[64,128,128]{2,1,0:T(8,128)(2,1)}, u32[]{:S(2)}) copy-start(bf16[64,128,128]{2,1,0:T(8,128)(2,1)} %rest_8_.5) | copy-start | bytes 6291460
  0.0 6.6 %copy-start.10 = (s32[64]{0:T(128)S(1)}, s32[64]{0:T(128)}, u32[]{:S(2)}) copy-start(s32[64]{0:T(128)} %source.1) | copy-start | bytes 772
  2.9 18.1 %copy-start.11 = (bf16[768,256]{1,0:T(8,128)(2,1)S(1)}, bf16[768,256]{1,0:T(8,128)(2,1)}, u32[]{:S(2)}) copy-start(bf16[768,256]{1,0:T(8,128)(2,1)} %w_in.1) | copy-start | bytes 1179652
  2.9 18.1 %copy-start.12 = (bf16[256,64]{0,1:T(8,128)(2,1)S(1)}, bf16[256,64]{0,1:T(8,128)(2,1)}, u32[]{:S(2)}) copy-start(bf16[256,64]{0,1:T(8,128)(2,1)} %param.11) | copy-start | bytes 98308
  2.9 18.1 %copy-start.13 = (s32[8192]{0:T(1024)S(1)}, s32[8192]{0:T(1024)}, u32[]{:S(2)}) copy-start(s32[8192]{0:T(1024)} %param.12) | copy-start | bytes 98308
  2.9 18.1 %copy-start.14 = (s32[64]{0:T(128)S(1)}, s32[64]{0:T(128)}, u32[]{:S(2)}) copy-start(s32[64]{0:T(128)} %param.14) | copy-start | bytes 772
  2.9 37.7 %collective-permute-start.11 = (bf16[48,128,128]{2,1,0:T(8,128)(2,1)}, bf16[48,128,128]{2,1,0:T(8,128)(2,1)}, u32[]{:S(2)}, u32[]{:S(2)}) collective-permute-start(bf16[48,128,128]{2,1,0:T(8,128)(2,1)} %slice.7), channel_id=1, source_target_pairs={{0,2},{1,3},{2,0},{3,1},{4,6},{5,7},{6,4},{7,5},{8,10},{9,11},{10,... | collective-permute-start | bytes 4718600 | tf_op jit(solution)/shard_map/ppermute | solution.py:23
  8.3 12.7 %all-to-all-start = ((f32[8,16,128]{2,1,0:T(8,128)}), f32[8,16,128]{2,1,0:T(8,128)S(1)}, u32[]{:S(2)}, u32[]{:S(2)}) async-start(f32[8,16,128]{2,1,0:T(8,128)} %column_sums.1), calls=%async_computation | async-start | bytes 131072 | tf_op jit(solution)/shard_map/all_to_all | solution.py:388
  14.1 59.7 %collective-permute-start.10 = (bf16[64,128,128]{2,1,0:T(8,128)(2,1)S(1)}, bf16[64,128,128]{2,1,0:T(8,128)(2,1)}, u32[]{:S(2)}, u32[]{:S(2)}) collective-permute-start(bf16[64,128,128]{2,1,0:T(8,128)(2,1)S(1)} %copy-done), channel_id=1, source_target_pairs={{0,1},{1,0},{2,3},{3,2},{4,5},{5,4},{6,7},{7,6},{8,9},{9,8},{10,11... | collective-permute-start | bytes 6291464 | tf_op jit(solution)/shard_map/ppermute | solution.py:23
  36.2 13.5 %copy-start.9 = (s32[2048]{0:T(1024)S(1)}, s32[2048]{0:T(1024)}, u32[]{:S(2)}) copy-start(s32[2048]{0:T(1024)} %param.17) | copy-start | bytes 24580
  36.2 1.4 %collective-permute-start = (f32[16,2304]{1,0:T(8,128)S(1)}, f32[16,2304]{1,0:T(8,128)S(1)}, u32[]{:S(2)}, u32[]{:S(2)}) collective-permute-start(f32[16,2304]{1,0:T(8,128)S(1)} %get-tuple-element.21), channel_id=1, source_target_pairs={{0,1},{1,0},{2,3},{3,2},{4,5},{5,4},{6,7},{7,6},{8,9},{9,8},{10,11... | collective-permute-start | bytes 442376 | tf_op jit(solution)/shard_map/ppermute | solution.py:23
  40.6 33.1 %collective-permute-start.13 = (bf16[48,128,128]{2,1,0:T(8,128)(2,1)}, bf16[48,128,128]{2,1,0:T(8,128)(2,1)}, u32[]{:S(2)}, u32[]{:S(2)}) collective-permute-start(bf16[48,128,128]{2,1,0:T(8,128)(2,1)} %after.2.rest_10_), channel_id=1, source_target_pairs={{0,1},{1,0},{2,3},{3,2},{4,5},{5,4},{6,7},{7,6},{8,9},{9,8},{10,11... | collective-permute-start | bytes 4718600 | tf_op jit(solution)/shard_map/ppermute | solution.py:23
  40.7 6.6 %collective-permute-start.1 = (f32[16,2304]{1,0:T(8,128)S(1)}, f32[16,2304]{1,0:T(8,128)S(1)}, u32[]{:S(2)}, u32[]{:S(2)}) collective-permute-start(f32[16,2304]{1,0:T(8,128)S(1)} %get-tuple-element.22), channel_id=1, source_target_pairs={{0,2},{1,3},{2,0},{3,1},{4,6},{5,7},{6,4},{7,5},{8,10},{9,11},{10,... | collective-permute-start | bytes 442376 | tf_op jit(solution)/shard_map/ppermute | solution.py:23
  42.4 7.3 %collective-permute-start.2 = (f32[16,2304]{1,0:T(8,128)S(1)}, f32[16,2304]{1,0:T(8,128)S(1)}, u32[]{:S(2)}, u32[]{:S(2)}) collective-permute-start(f32[16,2304]{1,0:T(8,128)S(1)} %get-tuple-element.23), channel_id=1, source_target_pairs={{0,3},{1,2},{2,1},{3,0},{4,7},{5,6},{6,5},{7,4},{8,11},{9,10},{10,... | collective-permute-start | bytes 442376 | tf_op jit(solution)/shard_map/ppermute | solution.py:23
  49.8 20.8 %copy-start.5 = (f32[16,2048]{1,0:T(8,128)}, f32[16,2048]{1,0:T(8,128)S(1)}, u32[]{:S(2)}) copy-start(f32[16,2048]{1,0:T(8,128)S(1)} %get-tuple-element.27.rest_14_) | copy-start | bytes 393220
  49.8 20.7 %copy-start.7 = (bf16[16,2176]{1,0:T(8,128)(2,1)}, bf16[16,2176]{1,0:T(8,128)(2,1)S(1)}, u32[]{:S(2)}) copy-start(bf16[16,2176]{1,0:T(8,128)(2,1)S(1)} %get-tuple-element.25.rest_7_) | copy-start | bytes 208900
  49.8 20.7 %collective-permute-start.12 = (bf16[16,128,128]{2,1,0:T(8,128)(2,1)S(1)}, bf16[16,128,128]{2,1,0:T(8,128)(2,1)S(1)}, u32[]{:S(2)}, u32[]{:S(2)}) collective-permute-start(bf16[16,128,128]{2,1,0:T(8,128)(2,1)S(1)} %get-tuple-element.26), channel_id=1, source_target_pairs={{0,2},{1,3},{2,0},{3,1},{4,6},{5,7},{6,4},{7,5},{8,10},{9,11},{10,... | collective-permute-start | bytes 1572872 | tf_op jit(solution)/shard_map/ppermute | solution.py:23
  51.7 4.3 %collective-permute-start.9 = (bf16[16,2176]{1,0:T(8,128)(2,1)S(1)}, bf16[16,2176]{1,0:T(8,128)(2,1)S(1)}, u32[]{:S(2)}, u32[]{:S(2)}) collective-permute-start(bf16[16,2176]{1,0:T(8,128)(2,1)S(1)} %get-tuple-element.25.rest_7_), channel_id=1, source_target_pairs={{0,4},{4,0},{8,12},{12,8},{16,20},{20,16},{24,28},{28,24},{1,5},{5... | collective-permute-start | bytes 208904 | tf_op jit(solution)/shard_map/ppermute | solution.py:23
  53.1 5.4 %collective-permute-start.7 = (bf16[16,2176]{1,0:T(8,128)(2,1)S(1)}, bf16[16,2176]{1,0:T(8,128)(2,1)S(1)}, u32[]{:S(2)}, u32[]{:S(2)}) collective-permute-start(bf16[16,2176]{1,0:T(8,128)(2,1)S(1)} %get-tuple-element.25.rest_7_), channel_id=1, source_target_pairs={{0,8},{4,12},{8,0},{12,4},{16,24},{20,28},{24,16},{28,20},{1,9},{5... | collective-permute-start | bytes 208904 | tf_op jit(solution)/shard_map/ppermute | solution.py:23
  56.0 5.5 %collective-permute-start.5 = (bf16[16,2176]{1,0:T(8,128)(2,1)S(1)}, bf16[16,2176]{1,0:T(8,128)(2,1)S(1)}, u32[]{:S(2)}, u32[]{:S(2)}) collective-permute-start(bf16[16,2176]{1,0:T(8,128)(2,1)S(1)} %get-tuple-element.25.rest_7_), channel_id=1, source_target_pairs={{0,16},{4,20},{8,24},{12,28},{16,0},{20,4},{24,8},{28,12},{1,17},{... | collective-permute-start | bytes 208904 | tf_op jit(solution)/shard_map/ppermute | solution.py:23
  58.6 6.2 %collective-permute-start.3 = (bf16[16,2176]{1,0:T(8,128)(2,1)S(1)}, bf16[16,2176]{1,0:T(8,128)(2,1)S(1)}, u32[]{:S(2)}, u32[]{:S(2)}) collective-permute-start(bf16[16,2176]{1,0:T(8,128)(2,1)S(1)} %get-tuple-element.25.rest_7_), channel_id=1, source_target_pairs={{0,24},{4,28},{8,16},{12,20},{16,8},{20,12},{24,0},{28,4},{1,25},{... | collective-permute-start | bytes 208904 | tf_op jit(solution)/shard_map/ppermute | solution.py:23
  61.5 4.8 %collective-permute-start.8 = (bf16[16,2176]{1,0:T(8,128)(2,1)S(1)}, bf16[16,2176]{1,0:T(8,128)(2,1)S(1)}, u32[]{:S(2)}, u32[]{:S(2)}) collective-permute-start(bf16[16,2176]{1,0:T(8,128)(2,1)S(1)} %collective-permute-done.7.refs_2_.rest_5_), channel_id=1, source_target_pairs={{0,4},{4,0},{8,12},{12,8},{16,20},{20,16},{24,28},{28,24},{1,5},{5... | collective-permute-start | bytes 208904 | tf_op jit(solution)/shard_map/ppermute | solution.py:23
  64.8 4.3 %collective-permute-start.6 = (bf16[16,2176]{1,0:T(8,128)(2,1)S(1)}, bf16[16,2176]{1,0:T(8,128)(2,1)S(1)}, u32[]{:S(2)}, u32[]{:S(2)}) collective-permute-start(bf16[16,2176]{1,0:T(8,128)(2,1)S(1)} %collective-permute-done.5.refs_4_.rest_3_), channel_id=1, source_target_pairs={{0,4},{4,0},{8,12},{12,8},{16,20},{20,16},{24,28},{28,24},{1,5},{5... | collective-permute-start | bytes 208904 | tf_op jit(solution)/shard_map/ppermute | solution.py:23
  66.3 4.3 %collective-permute-start.4 = (bf16[16,2176]{1,0:T(8,128)(2,1)S(1)}, bf16[16,2176]{1,0:T(8,128)(2,1)S(1)}, u32[]{:S(2)}, u32[]{:S(2)}) collective-permute-start(bf16[16,2176]{1,0:T(8,128)(2,1)S(1)} %collective-permute-done.3.refs_6_.rest_1_), channel_id=1, source_target_pairs={{0,4},{4,0},{8,12},{12,8},{16,20},{20,16},{24,28},{28,24},{1,5},{5... | collective-permute-start | bytes 208904 | tf_op jit(solution)/shard_map/ppermute | solution.py:23
  70.6 0.6 copy-start.1
  71.2 0.6 copy-start.3
  71.8 1.9 %collective-permute-start.14 = (bf16[16,128,128]{2,1,0:T(8,128)(2,1)S(1)}, bf16[16,128,128]{2,1,0:T(8,128)(2,1)S(1)}, u32[]{:S(2)}, u32[]{:S(2)}) collective-permute-start(bf16[16,128,128]{2,1,0:T(8,128)(2,1)S(1)} %after.3.rest_11_), channel_id=1, source_target_pairs={{0,1},{1,0},{2,3},{3,2},{4,5},{5,4},{6,7},{7,6},{8,9},{9,8},{10,11... | collective-permute-start | bytes 1572872 | tf_op jit(solution)/shard_map/ppermute | solution.py:23
  73.8 0.9 copy-start.2
  74.6 0.9 copy-start.4
  75.5 0.9 copy-start.6
  76.4 0.9 copy-start.8
  83.2 7.9 %collective-permute-start.19 = (bf16[16,2048]{1,0:T(8,128)(2,1)S(1)}, bf16[16,2048]{1,0:T(8,128)(2,1)S(1)}, u32[]{:S(2)}, u32[]{:S(2)}) collective-permute-start(bf16[16,2048]{1,0:T(8,128)(2,1)S(1)} %get-tuple-element.29.rest_7_), channel_id=1, source_target_pairs={{0,8},{4,12},{8,0},{12,4},{16,24},{20,28},{24,16},{28,20},{1,9},{5... | collective-permute-start | bytes 196616 | tf_op jit(solution)/shard_map/ppermute | solution.py:23
  85.8 7.3 %collective-permute-start.17 = (bf16[16,2048]{1,0:T(8,128)(2,1)S(1)}, bf16[16,2048]{1,0:T(8,128)(2,1)S(1)}, u32[]{:S(2)}, u32[]{:S(2)}) collective-permute-start(bf16[16,2048]{1,0:T(8,128)(2,1)S(1)} %get-tuple-element.29.rest_7_), channel_id=1, source_target_pairs={{0,16},{4,20},{8,24},{12,28},{16,0},{20,4},{24,8},{28,12},{1,17},{... | collective-permute-start | bytes 196616 | tf_op jit(solution)/shard_map/ppermute | solution.py:23
  89.1 6.2 %collective-permute-start.15 = (bf16[16,2048]{1,0:T(8,128)(2,1)S(1)}, bf16[16,2048]{1,0:T(8,128)(2,1)S(1)}, u32[]{:S(2)}, u32[]{:S(2)}) collective-permute-start(bf16[16,2048]{1,0:T(8,128)(2,1)S(1)} %get-tuple-element.29.rest_7_), channel_id=1, source_target_pairs={{0,24},{4,28},{8,16},{12,20},{16,8},{20,12},{24,0},{28,4},{1,25},{... | collective-permute-start | bytes 196616 | tf_op jit(solution)/shard_map/ppermute | solution.py:23
  89.1 8.2 %collective-permute-start.21 = (bf16[16,2048]{1,0:T(8,128)(2,1)S(1)}, bf16[16,2048]{1,0:T(8,128)(2,1)S(1)}, u32[]{:S(2)}, u32[]{:S(2)}) collective-permute-start(bf16[16,2048]{1,0:T(8,128)(2,1)S(1)} %get-tuple-element.29.rest_7_), channel_id=1, source_target_pairs={{0,4},{4,0},{8,12},{12,8},{16,20},{20,16},{24,28},{28,24},{1,5},{5... | collective-permute-start | bytes 196616 | tf_op jit(solution)/shard_map/ppermute | solution.py:23
  91.1 6.2 %collective-permute-start.20 = (bf16[16,2048]{1,0:T(8,128)(2,1)S(1)}, bf16[16,2048]{1,0:T(8,128)(2,1)S(1)}, u32[]{:S(2)}, u32[]{:S(2)}) collective-permute-start(bf16[16,2048]{1,0:T(8,128)(2,1)S(1)} %collective-permute-done.19.rest_5_), channel_id=1, source_target_pairs={{0,4},{4,0},{8,12},{12,8},{16,20},{20,16},{24,28},{28,24},{1,5},{5... | collective-permute-start | bytes 196616 | tf_op jit(solution)/shard_map/ppermute | solution.py:23
  93.1 4.8 %collective-permute-start.18 = (bf16[16,2048]{1,0:T(8,128)(2,1)S(1)}, bf16[16,2048]{1,0:T(8,128)(2,1)S(1)}, u32[]{:S(2)}, u32[]{:S(2)}) collective-permute-start(bf16[16,2048]{1,0:T(8,128)(2,1)S(1)} %collective-permute-done.17.rest_3_), channel_id=1, source_target_pairs={{0,4},{4,0},{8,12},{12,8},{16,20},{20,16},{24,28},{28,24},{1,5},{5... | collective-permute-start | bytes 196616 | tf_op jit(solution)/shard_map/ppermute | solution.py:23
  95.2 4.3 %collective-permute-start.16 = (bf16[16,2048]{1,0:T(8,128)(2,1)S(1)}, bf16[16,2048]{1,0:T(8,128)(2,1)S(1)}, u32[]{:S(2)}, u32[]{:S(2)}) collective-permute-start(bf16[16,2048]{1,0:T(8,128)(2,1)S(1)} %collective-permute-done.15.rest_1_), channel_id=1, source_target_pairs={{0,4},{4,0},{8,12},{12,8},{16,20},{20,16},{24,28},{28,24},{1,5},{5... | collective-permute-start | bytes 196616 | tf_op jit(solution)/shard_map/ppermute | solution.py:23
  105.3 6.5 %collective-permute-start.26 = (bf16[16,2048]{1,0:T(8,128)(2,1)S(1)}, bf16[16,2048]{1,0:T(8,128)(2,1)S(1)}, u32[]{:S(2)}, u32[]{:S(2)}) collective-permute-start(bf16[16,2048]{1,0:T(8,128)(2,1)S(1)} %hop.4.rest_7_), channel_id=1, source_target_pairs={{0,8},{4,12},{8,0},{12,4},{16,24},{20,28},{24,16},{28,20},{1,9},{5... | collective-permute-start | bytes 196616 | tf_op jit(solution)/shard_map/ppermute | solution.py:23
  106.4 6.3 %collective-permute-start.24 = (bf16[16,2048]{1,0:T(8,128)(2,1)S(1)}, bf16[16,2048]{1,0:T(8,128)(2,1)S(1)}, u32[]{:S(2)}, u32[]{:S(2)}) collective-permute-start(bf16[16,2048]{1,0:T(8,128)(2,1)S(1)} %hop.4.rest_7_), channel_id=1, source_target_pairs={{0,16},{4,20},{8,24},{12,28},{16,0},{20,4},{24,8},{28,12},{1,17},{... | collective-permute-start | bytes 196616 | tf_op jit(solution)/shard_map/ppermute | solution.py:23
  109.8 6.1 %collective-permute-start.22 = (bf16[16,2048]{1,0:T(8,128)(2,1)S(1)}, bf16[16,2048]{1,0:T(8,128)(2,1)S(1)}, u32[]{:S(2)}, u32[]{:S(2)}) collective-permute-start(bf16[16,2048]{1,0:T(8,128)(2,1)S(1)} %hop.4.rest_7_), channel_id=1, source_target_pairs={{0,24},{4,28},{8,16},{12,20},{16,8},{20,12},{24,0},{28,4},{1,25},{... | collective-permute-start | bytes 196616 | tf_op jit(solution)/shard_map/ppermute | solution.py:23
  109.8 6.8 %collective-permute-start.28 = (bf16[16,2048]{1,0:T(8,128)(2,1)S(1)}, bf16[16,2048]{1,0:T(8,128)(2,1)S(1)}, u32[]{:S(2)}, u32[]{:S(2)}) collective-permute-start(bf16[16,2048]{1,0:T(8,128)(2,1)S(1)} %hop.4.rest_7_), channel_id=1, source_target_pairs={{0,4},{4,0},{8,12},{12,8},{16,20},{20,16},{24,28},{28,24},{1,5},{5... | collective-permute-start | bytes 196616 | tf_op jit(solution)/shard_map/ppermute | solution.py:23
  111.7 4.8 %collective-permute-start.27 = (bf16[16,2048]{1,0:T(8,128)(2,1)S(1)}, bf16[16,2048]{1,0:T(8,128)(2,1)S(1)}, u32[]{:S(2)}, u32[]{:S(2)}) collective-permute-start(bf16[16,2048]{1,0:T(8,128)(2,1)S(1)} %collective-permute-done.26.rest_5_), channel_id=1, source_target_pairs={{0,4},{4,0},{8,12},{12,8},{16,20},{20,16},{24,28},{28,24},{1,5},{5... | collective-permute-start | bytes 196616 | tf_op jit(solution)/shard_map/ppermute | solution.py:23
  112.8 4.3 %collective-permute-start.25 = (bf16[16,2048]{1,0:T(8,128)(2,1)S(1)}, bf16[16,2048]{1,0:T(8,128)(2,1)S(1)}, u32[]{:S(2)}, u32[]{:S(2)}) collective-permute-start(bf16[16,2048]{1,0:T(8,128)(2,1)S(1)} %collective-permute-done.24.rest_3_), channel_id=1, source_target_pairs={{0,4},{4,0},{8,12},{12,8},{16,20},{20,16},{24,28},{28,24},{1,5},{5... | collective-permute-start | bytes 196616 | tf_op jit(solution)/shard_map/ppermute | solution.py:23
  115.9 4.3 %collective-permute-start.23 = (bf16[16,2048]{1,0:T(8,128)(2,1)S(1)}, bf16[16,2048]{1,0:T(8,128)(2,1)S(1)}, u32[]{:S(2)}, u32[]{:S(2)}) collective-permute-start(bf16[16,2048]{1,0:T(8,128)(2,1)S(1)} %collective-permute-done.22.rest_1_), channel_id=1, source_target_pairs={{0,4},{4,0},{8,12},{12,8},{16,20},{20,16},{24,28},{28,24},{1,5},{5... | collective-permute-start | bytes 196616 | tf_op jit(solution)/shard_map/ppermute | solution.py:23
  125.9 1.9 %collective-permute-start.29 = (f32[16,512]{1,0:T(8,128)S(1)}, f32[16,512]{1,0:T(8,128)S(1)}, u32[]{:S(2)}, u32[]{:S(2)}) collective-permute-start(f32[16,512]{1,0:T(8,128)S(1)} %get-tuple-element.32), channel_id=1, source_target_pairs={{0,1},{1,0},{2,3},{3,2},{4,5},{5,4},{6,7},{7,6},{8,9},{9,8},{10,11... | collective-permute-start | bytes 98312 | tf_op jit(solution)/shard_map/ppermute | solution.py:23
  126.0 4.2 %collective-permute-start.30 = (f32[16,512]{1,0:T(8,128)S(1)}, f32[16,512]{1,0:T(8,128)S(1)}, u32[]{:S(2)}, u32[]{:S(2)}) collective-permute-start(f32[16,512]{1,0:T(8,128)S(1)} %get-tuple-element.33), channel_id=1, source_target_pairs={{0,2},{1,3},{2,0},{3,1},{4,6},{5,7},{6,4},{7,5},{8,10},{9,11},{10,... | collective-permute-start | bytes 98312 | tf_op jit(solution)/shard_map/ppermute | solution.py:23
  126.4 3.8 %collective-permute-start.31 = (f32[16,512]{1,0:T(8,128)S(1)}, f32[16,512]{1,0:T(8,128)S(1)}, u32[]{:S(2)}, u32[]{:S(2)}) collective-permute-start(f32[16,512]{1,0:T(8,128)S(1)} %get-tuple-element.34), channel_id=1, source_target_pairs={{0,3},{1,2},{2,1},{3,0},{4,7},{5,6},{6,5},{7,4},{8,11},{9,10},{10,... | collective-permute-start | bytes 98312 | tf_op jit(solution)/shard_map/ppermute | solution.py:23

commit v3 on v2

--- a/solution.py
+++ b/solution.py
@@ -83,7 +83,7 @@
     return lax.dot_general(left, right, NT, preferred_element_type=jnp.float32)
 
 
-def documents_kernel(place, docs, w_in, w_out_t, host, degrees, *rest):
+def documents_kernel(place, part, docs, w_in, w_out_t, host, degrees, *rest):
     labels, outs, total = rest[:LABELS], rest[LABELS:-1], rest[-1]
     step = pl.program_id(0)
     topics = w_out_t.shape[0]
@@ -119,7 +119,7 @@
                 out[r : r + 1, wide : wide + label.shape[1]] = label[...].astype(jnp.float32)
 
 
-def documents(docs, w_in, w_out, doc_host, hosts, split, place, degrees, labels):
+def documents(docs, w_in, w_out, doc_host, hosts, split, place, part, degrees, labels):
     count, depth = docs.shape
     hid, topics = w_out.shape
     per = topics // split
@@ -129,17 +129,17 @@
     return pl.pallas_call(
         documents_kernel,
         grid_spec=pltpu.PrefetchScalarGridSpec(
-            num_scalar_prefetch=1,
+            num_scalar_prefetch=2,
             grid=(steps,),
             in_specs=[
-                pl.BlockSpec((DOC_BLOCK, depth), lambda i, p: (i, 0)),
-                pl.BlockSpec((depth, hid), lambda i, p: (0, 0)),
-                pl.BlockSpec((topics, hid), lambda i, p: (0, 0)),
-                pl.BlockSpec((1, 1, DOC_BLOCK), lambda i, p: (i, 0, 0)),
-                pl.BlockSpec(degrees.shape, lambda i, p: (0, 0, 0)),
+                pl.BlockSpec((DOC_BLOCK, depth), lambda i, *p: (i, 0)),
+                pl.BlockSpec((depth, hid), lambda i, *p: (0, 0)),
+                pl.BlockSpec((topics, hid), lambda i, *p: (0, 0)),
+                pl.BlockSpec((1, 1, DOC_BLOCK), lambda i, *p: (i, 0, 0)),
+                pl.BlockSpec(degrees.shape, lambda i, *p: (0, 0, 0)),
             ]
-            + [pl.BlockSpec(label.shape, lambda i, p: (0, 0)) for label in labels],
-            out_specs=[pl.BlockSpec(shape, lambda i, p: (0, 0))] * split,
+            + [pl.BlockSpec(label.shape, lambda i, *p: (0, 0)) for label in labels],
+            out_specs=[pl.BlockSpec(shape, lambda i, *p: (0, 0))] * split,
             scratch_shapes=[pltpu.VMEM((2 * DIGITS * topics, width), jnp.float32)],
         ),
         out_shape=[jax.ShapeDtypeStruct(shape, jnp.float32)] * split,
@@ -150,7 +150,7 @@
             transcendentals=count * (hid + topics),
         ),
         name="documents",
-    )(place, docs, w_in, w_out.T, doc_host.reshape(steps, 1, DOC_BLOCK), degrees, *labels)
+    )(place, part, docs, w_in, w_out.T, doc_host.reshape(steps, 1, DOC_BLOCK), degrees, *labels)
 
 
 def start_kernel(held, teleport, *rest):
@@ -386,12 +386,12 @@
     far = {j: [xor_send(early, "doc", j)] for j in range(2, split, 2)}
     degrees = column_sums(src_block, tile_count, tiles, parts, blocks)
     degrees = lax.all_to_all(degrees, "hst", split_axis=0, concat_axis=0, tiled=True)
-    sums = documents(docs, w_in, w_out, doc_host, hosts, split, place, degrees, labels)
+    sums = documents(docs, w_in, w_out, doc_host, hosts, split, place, part, degrees, labels)
     sums = [sums[0]] + [xor_send(sums[j], "doc", j) for j in range(1, split)]
     for j in range(2, split, 2):
-        far[j][0] = after(far[j][0], [sums[1]])
+        far[j][0] = after(far[j][0], sums[1:])
         far[j + 1] = [xor_send(far[j][0], "doc", 1)]
-    sent, tele, inverse, meta, late = start_values(teleport, sums, block, [late])
+    sent, tele, inverse, meta, late, near = start_values(teleport, sums, block, [late, near])
     for j in range(2, split, 2):
         far[j].append(xor_send(late, "doc", j))
     for step in range(HOPS):

time: 131 us -> 116 us (0.89)
  Pallas kernels: 35 us -> 29 us
  local copies, waits for them, and re-layouts: 7.76 us -> 3.06 us
  waiting for transfers between devices: 39.1 us -> 36.6 us
  starting transfers between devices: 48.2 us -> 46.3 us
    pallas_call x3, Pallas kernels: 17.4 us -> 11.3 us  [hop(): pl.pallas_call(functools.partial(hop_kernel, first, last, parts, spans, f...]
    unnamed x30 -> x14, local copies, waits for them, and re-layouts: 4.84 us -> 0.03 us
    ppermute x32, waiting for transfers between devices: 32.2 us -> 29.7 us  [xor_send(): return lax.ppermute(value, axis, [(i, i ^ step) for i in range(size)])]
    ppermute x32, starting transfers between devices: 42.3 us -> 40.5 us  [xor_send(): return lax.ppermute(value, axis, [(i, i ^ step) for i in range(size)])]
  transfers between devices with their start and end apart: 33 -> 33, of which waited for: 20 -> 18; matrix products, arithmetic and copies ran while one was open for 0% -> 3% of each run, Pallas kernels for 13% -> 15%
where the time goes in v3:
time: 116 us
  starting transfers between devices  46.3 us (40%)
  waiting for transfers between devices  36.6 us (32%)
  Pallas kernels  29 us (25%)
  local copies, waits for them, and re-layouts  3.06 us (3%)
    ppermute x32, starting transfers between devices, xor_send(): return lax.ppermute(value, axis, [(i, i ^ step) for i in range(size)])  40.5 us
    ppermute x32, waiting for transfers between devices, xor_send(): return lax.ppermute(value, axis, [(i, i ^ step) for i in range(size)])  29.7 us
    pallas_call x1, Pallas kernels, documents(): pl.pallas_call(documents_kernel, grid_spec=pltpu.PrefetchScalarGridSpec(n...  15.1 us
    pallas_call x3, Pallas kernels, hop(): pl.pallas_call(functools.partial(hop_kernel, first, last, parts, spans, f...  11.3 us
    all_to_all x1, waiting for transfers between devices, body(): lax.all_to_all(degrees, 'hst', split_axis=0, concat_axis=0, tiled=True)  6.9 us
    all_to_all x1, starting transfers between devices, body(): lax.all_to_all(degrees, 'hst', split_axis=0, concat_axis=0, tiled=True)  5.76 us
    slice x2, local copies, waits for them, and re-layouts, body(): early, late = (tiles[:cut], tiles[cut:])  3.04 us
  transfers between devices with their start and end apart: 33, of which 18 were waited for; matrix products, arithmetic and copies ran while one was open for 3% of the time, Pallas kernels for 15%

profile of v3, /device:TPU:0, one launch (start us, length us, event | category | flops | bytes accessed | tf_op | source)
XLA Modules:
  0.0 115.7 jit_solution(12695711663552190310)
XLA Ops:
  0.0 0.5 collective-permute-start.3
  0.6 3.0 %slice.7 = bf16[48,128,128]{2,1,0:T(8,128)(2,1)} slice(bf16[64,128,128]{2,1,0:T(8,128)(2,1)} %rest_8_.5), slice={[0:48], [0:128], [0:128]} | slice | bytes 3145728 | tf_op jit(solution)/shard_map/slice | solution.py:385
  3.6 2.4 %collective-permute-start.11 = (bf16[48,128,128]{2,1,0:T(8,128)(2,1)}, bf16[48,128,128]{2,1,0:T(8,128)(2,1)}, u32[]{:S(2)}, u32[]{:S(2)}) collective-permute-start(bf16[48,128,128]{2,1,0:T(8,128)(2,1)} %slice.7), channel_id=1, source_target_pairs={{0,2},{1,3},{2,0},{3,1},{4,6},{5,7},{6,4},{7,5},{8,10},{9,11},{10,... | collective-permute-start | bytes 4718600 | tf_op jit(solution)/shard_map/ppermute | solution.py:23
  6.7 1.7 %column_sums.1 = f32[8,16,128]{2,1,0:T(8,128)} custom-call(s32[64]{0:T(128)S(1)} %copy-done.2, s32[1]{0:T(128)} %copy.18.count, bf16[64,128,128]{2,1,0:T(8,128)(2,1)S(1)} %copy-done), custom_call_target="tpu_custom_call" | custom-call | flops 1048576 | bytes 2097152 | tf_op jit(solution)/shard_map/column_sums/pallas_call | solution.py:49
  8.4 5.8 %all-to-all-start = ((f32[8,16,128]{2,1,0:T(8,128)}), f32[8,16,128]{2,1,0:T(8,128)S(1)}, u32[]{:S(2)}, u32[]{:S(2)}) async-start(f32[8,16,128]{2,1,0:T(8,128)} %column_sums.1), calls=%async_computation | async-start | bytes 131072 | tf_op jit(solution)/shard_map/all_to_all | solution.py:388
  14.1 6.9 %all-to-all-done.degrees = f32[8,16,128]{2,1,0:T(8,128)S(1)} async-done(((f32[8,16,128]{2,1,0:T(8,128)}), f32[8,16,128]{2,1,0:T(8,128)S(1)}, u32[]{:S(2)}, u32[]{:S(2)}) %all-to-all-start) | async-done | bytes 65568 | tf_op jit(solution)/shard_map/all_to_all | solution.py:388
  21.1 15.1 %documents.1 = (f32[16,2304]{1,0:T(8,128)S(1)}, f32[16,2304]{1,0:T(8,128)S(1)}, f32[16,2304]{1,0:T(8,128)S(1)}, f32[16,2304]{1,0:T(8,128)S(1)}) custom-call(s32[1]{0:T(128)} %bitcast.place, s32[1]{0:T(128)} %bitcast.2.part, bf16[8192,768]{1,0:T(8,128)(2,1)} %docs.1, bf16[768,256]{1,0:T(8,128)(2,1)S(1)} %copy-done.3, bf16[64,256]{1,0:T(8,128)(2,1)S(1)} %bitcast.12, ...), custom_call_target="tpu_custom_call" | custom-call | flops 7784628224 | bytes 12582912 | tf_op jit(solution)/shard_map/documents/pallas_call | solution.py:129
  36.2 0.1 collective-permute-start
  36.3 0.6 collective-permute-start.1
  36.9 1.2 %collective-permute-start.2 = (f32[16,2304]{1,0:T(8,128)S(1)}, f32[16,2304]{1,0:T(8,128)S(1)}, u32[]{:S(2)}, u32[]{:S(2)}) collective-permute-start(f32[16,2304]{1,0:T(8,128)S(1)} %get-tuple-element.24), channel_id=1, source_target_pairs={{0,3},{1,2},{2,1},{3,0},{4,7},{5,6},{6,5},{7,4},{8,11},{9,10},{10,... | collective-permute-start | bytes 442376 | tf_op jit(solution)/shard_map/ppermute | solution.py:23
  38.1 0.0 collective-permute-done.rest_1_.refs_1_
  38.1 6.5 %collective-permute-done.1.rest_2_.refs_2_ = f32[16,2304]{1,0:T(8,128)S(1)} collective-permute-done((f32[16,2304]{1,0:T(8,128)S(1)}, f32[16,2304]{1,0:T(8,128)S(1)}, u32[]{:S(2)}, u32[]{:S(2)}) %collective-permute-start.1) | collective-permute-done | bytes 147488 | tf_op jit(solution)/shard_map/ppermute | solution.py:23
  44.6 2.5 %collective-permute-done.2.rest_3_.refs_3_ = f32[16,2304]{1,0:T(8,128)S(1)} collective-permute-done((f32[16,2304]{1,0:T(8,128)S(1)}, f32[16,2304]{1,0:T(8,128)S(1)}, u32[]{:S(2)}, u32[]{:S(2)}) %collective-permute-start.2) | collective-permute-done | bytes 147488 | tf_op jit(solution)/shard_map/ppermute | solution.py:23
  47.1 0.1 collective-permute-start.13
  47.3 0.1 start_values.1
  47.5 1.8 %collective-permute-start.12 = (bf16[16,128,128]{2,1,0:T(8,128)(2,1)S(1)}, bf16[16,128,128]{2,1,0:T(8,128)(2,1)S(1)}, u32[]{:S(2)}, u32[]{:S(2)}) collective-permute-start(bf16[16,128,128]{2,1,0:T(8,128)(2,1)S(1)} %get-tuple-element.28), channel_id=1, source_target_pairs={{0,2},{1,3},{2,0},{3,1},{4,6},{5,7},{6,4},{7,5},{8,10},{9,11},{10,... | collective-permute-start | bytes 1572872 | tf_op jit(solution)/shard_map/ppermute | solution.py:23
  49.3 3.6 %collective-permute-start.4 = (bf16[16,2176]{1,0:T(8,128)(2,1)S(1)}, bf16[16,2176]{1,0:T(8,128)(2,1)S(1)}, u32[]{:S(2)}, u32[]{:S(2)}) collective-permute-start(bf16[16,2176]{1,0:T(8,128)(2,1)S(1)} %get-tuple-element.26.rest_7_), channel_id=1, source_target_pairs={{0,24},{4,28},{8,16},{12,20},{16,8},{20,12},{24,0},{28,4},{1,25},{... | collective-permute-start | bytes 208904 | tf_op jit(solution)/shard_map/ppermute | solution.py:23
  52.9 0.8 collective-permute-start.8
  53.7 2.2 %collective-permute-done.4.refs_6_.rest_1_ = bf16[16,2176]{1,0:T(8,128)(2,1)S(1)} collective-permute-done((bf16[16,2176]{1,0:T(8,128)(2,1)S(1)}, bf16[16,2176]{1,0:T(8,128)(2,1)S(1)}, u32[]{:S(2)}, u32[]{:S(2)}) %collective-permute-start.4) | collective-permute-done | bytes 69664 | tf_op jit(solution)/shard_map/ppermute | solution.py:23
  55.9 1.5 %collective-permute-start.10 = (bf16[16,2176]{1,0:T(8,128)(2,1)S(1)}, bf16[16,2176]{1,0:T(8,128)(2,1)S(1)}, u32[]{:S(2)}, u32[]{:S(2)}) collective-permute-start(bf16[16,2176]{1,0:T(8,128)(2,1)S(1)} %get-tuple-element.26.rest_7_), channel_id=1, source_target_pairs={{0,4},{4,0},{8,12},{12,8},{16,20},{20,16},{24,28},{28,24},{1,5},{5... | collective-permute-start | bytes 208904 | tf_op jit(solution)/shard_map/ppermute | solution.py:23
  57.4 1.4 %collective-permute-done.6.refs_4_.rest_3_ = bf16[16,2176]{1,0:T(8,128)(2,1)S(1)} collective-permute-done((bf16[16,2176]{1,0:T(8,128)(2,1)S(1)}, bf16[16,2176]{1,0:T(8,128)(2,1)S(1)}, u32[]{:S(2)}, u32[]{:S(2)}) %collective-permute-start.6) | collective-permute-done | bytes 69664 | tf_op jit(solution)/shard_map/ppermute | solution.py:23
  58.8 1.5 %collective-permute-start.5 = (bf16[16,2176]{1,0:T(8,128)(2,1)S(1)}, bf16[16,2176]{1,0:T(8,128)(2,1)S(1)}, u32[]{:S(2)}, u32[]{:S(2)}) collective-permute-start(bf16[16,2176]{1,0:T(8,128)(2,1)S(1)} %collective-permute-done.4.refs_6_.rest_1_), channel_id=1, source_target_pairs={{0,4},{4,0},{8,12},{12,8},{16,20},{20,16},{24,28},{28,24},{1,5},{5... | collective-permute-start | bytes 208904 | tf_op jit(solution)/shard_map/ppermute | solution.py:23
  60.3 0.5 collective-permute-start.7
  60.9 0.0 collective-permute-done.10.refs_1_.rest_6_
  60.9 1.5 %collective-permute-start.9 = (bf16[16,2176]{1,0:T(8,128)(2,1)S(1)}, bf16[16,2176]{1,0:T(8,128)(2,1)S(1)}, u32[]{:S(2)}, u32[]{:S(2)}) collective-permute-start(bf16[16,2176]{1,0:T(8,128)(2,1)S(1)} %collective-permute-done.8.refs_2_.rest_5_), channel_id=1, source_target_pairs={{0,4},{4,0},{8,12},{12,8},{16,20},{20,16},{24,28},{28,24},{1,5},{5... | collective-permute-start | bytes 208904 | tf_op jit(solution)/shard_map/ppermute | solution.py:23
  62.3 1.5 %collective-permute-done.5.refs_7_.rest_0_ = bf16[16,2176]{1,0:T(8,128)(2,1)S(1)} collective-permute-done((bf16[16,2176]{1,0:T(8,128)(2,1)S(1)}, bf16[16,2176]{1,0:T(8,128)(2,1)S(1)}, u32[]{:S(2)}, u32[]{:S(2)}) %collective-permute-start.5) | collective-permute-done | bytes 69664 | tf_op jit(solution)/shard_map/ppermute | solution.py:23
  63.8 1.5 %collective-permute-done.7.refs_5_.rest_2_ = bf16[16,2176]{1,0:T(8,128)(2,1)S(1)} collective-permute-done((bf16[16,2176]{1,0:T(8,128)(2,1)S(1)}, bf16[16,2176]{1,0:T(8,128)(2,1)S(1)}, u32[]{:S(2)}, u32[]{:S(2)}) %collective-permute-start.7) | collective-permute-done | bytes 69664 | tf_op jit(solution)/shard_map/ppermute | solution.py:23
  65.4 0.7 collective-permute-done.9.refs_3_.rest_4_
  66.1 0.0 collective-permute-done.12.refs_0_
  66.1 1.9 %collective-permute-done.14.rest_13_ = bf16[16,128,128]{2,1,0:T(8,128)(2,1)S(1)} collective-permute-done((bf16[16,128,128]{2,1,0:T(8,128)(2,1)S(1)}, bf16[16,128,128]{2,1,0:T(8,128)(2,1)S(1)}, u32[]{:S(2)}, u32[]{:S(2)}) %collective-permute-start.14) | collective-permute-done | bytes 524320 | tf_op jit(solution)/shard_map/ppermute | solution.py:23
  68.0 3.8 %hop.3 = (bf16[16,2048]{1,0:T(8,128)(2,1)S(1)}, f32[16,2048]{1,0:T(8,128)S(1)}) custom-call(s32[12,128]{1,0:T(8,128)S(1)} %get-tuple-element.25.meta, s32[1]{0:T(128)} %bitcast.2.part, s32[1]{0:T(128)} %bitcast.place, bf16[16,2176]{1,0:T(8,128)(2,1)S(1)} %collective-permute-done.5.refs_7_.rest_0_, ...), custom_call_target="tpu_custom_call" | custom-call | flops 134217728 | bytes 8388608 | tf_op jit(solution)/shard_map/hop/pallas_call | solution.py:323
  71.9 4.4 %collective-permute-start.15 = (bf16[16,2048]{1,0:T(8,128)(2,1)S(1)}, bf16[16,2048]{1,0:T(8,128)(2,1)S(1)}, u32[]{:S(2)}, u32[]{:S(2)}) collective-permute-start(bf16[16,2048]{1,0:T(8,128)(2,1)S(1)} %get-tuple-element.31.rest_7_), channel_id=1, source_target_pairs={{0,24},{4,28},{8,16},{12,20},{16,8},{20,12},{24,0},{28,4},{1,25},{... | collective-permute-start | bytes 196616 | tf_op jit(solution)/shard_map/ppermute | solution.py:23
  76.2 0.2 collective-permute-start.17
  76.4 0.5 collective-permute-start.19
  76.9 2.1 %collective-permute-start.21 = (bf16[16,2048]{1,0:T(8,128)(2,1)S(1)}, bf16[16,2048]{1,0:T(8,128)(2,1)S(1)}, u32[]{:S(2)}, u32[]{:S(2)}) collective-permute-start(bf16[16,2048]{1,0:T(8,128)(2,1)S(1)} %get-tuple-element.31.rest_7_), channel_id=1, source_target_pairs={{0,4},{4,0},{8,12},{12,8},{16,20},{20,16},{24,28},{28,24},{1,5},{5... | collective-permute-start | bytes 196616 | tf_op jit(solution)/shard_map/ppermute | solution.py:23
  79.0 0.0 collective-permute-done.15.rest_1_
  79.0 2.1 %collective-permute-start.16 = (bf16[16,2048]{1,0:T(8,128)(2,1)S(1)}, bf16[16,2048]{1,0:T(8,128)(2,1)S(1)}, u32[]{:S(2)}, u32[]{:S(2)}) collective-permute-start(bf16[16,2048]{1,0:T(8,128)(2,1)S(1)} %collective-permute-done.15.rest_1_), channel_id=1, source_target_pairs={{0,4},{4,0},{8,12},{12,8},{16,20},{20,16},{24,28},{28,24},{1,5},{5... | collective-permute-start | bytes 196616 | tf_op jit(solution)/shard_map/ppermute | solution.py:23
  81.0 1.7 %collective-permute-done.17.rest_3_ = bf16[16,2048]{1,0:T(8,128)(2,1)S(1)} collective-permute-done((bf16[16,2048]{1,0:T(8,128)(2,1)S(1)}, bf16[16,2048]{1,0:T(8,128)(2,1)S(1)}, u32[]{:S(2)}, u32[]{:S(2)}) %collective-permute-start.17) | collective-permute-done | bytes 65568 | tf_op jit(solution)/shard_map/ppermute | solution.py:23
  82.7 1.0 collective-permute-start.18
  83.7 0.0 collective-permute-done.19.rest_5_
  83.7 1.1 collective-permute-start.20
  84.7 0.0 collective-permute-done.21.rest_6_
  84.7 2.5 %collective-permute-done.18.rest_2_ = bf16[16,2048]{1,0:T(8,128)(2,1)S(1)} collective-permute-done((bf16[16,2048]{1,0:T(8,128)(2,1)S(1)}, bf16[16,2048]{1,0:T(8,128)(2,1)S(1)}, u32[]{:S(2)}, u32[]{:S(2)}) %collective-permute-start.18) | collective-permute-done | bytes 65568 | tf_op jit(solution)/shard_map/ppermute | solution.py:23
  87.3 0.7 collective-permute-done.20.rest_4_
  88.0 3.7 %hop.4.rest_7_ = bf16[16,2048]{1,0:T(8,128)(2,1)S(1)} custom-call(s32[12,128]{1,0:T(8,128)S(1)} %get-tuple-element.25.meta, s32[1]{0:T(128)} %bitcast.2.part, s32[1]{0:T(128)} %bitcast.place, bf16[16,2048]{1,0:T(8,128)(2,1)S(1)} %collective-permute-done.16.rest_0_, bf16[16,2048]{1,0:T(8,128)(2,1)S(1)} %collective-permute-done.15.rest_1_, ...), custom_call_target="tpu_custom_call" | custom-call | flops 134217728 | bytes 8388608 | tf_op jit(solution)/shard_map/hop/pallas_call | solution.py:323
  91.7 4.2 %collective-permute-start.22 = (bf16[16,2048]{1,0:T(8,128)(2,1)S(1)}, bf16[16,2048]{1,0:T(8,128)(2,1)S(1)}, u32[]{:S(2)}, u32[]{:S(2)}) collective-permute-start(bf16[16,2048]{1,0:T(8,128)(2,1)S(1)} %hop.4.rest_7_), channel_id=1, source_target_pairs={{0,24},{4,28},{8,16},{12,20},{16,8},{20,12},{24,0},{28,4},{1,25},{... | collective-permute-start | bytes 196616 | tf_op jit(solution)/shard_map/ppermute | solution.py:23
  95.9 0.6 collective-permute-start.26
  96.6 2.2 %collective-permute-start.28 = (bf16[16,2048]{1,0:T(8,128)(2,1)S(1)}, bf16[16,2048]{1,0:T(8,128)(2,1)S(1)}, u32[]{:S(2)}, u32[]{:S(2)}) collective-permute-start(bf16[16,2048]{1,0:T(8,128)(2,1)S(1)} %hop.4.rest_7_), channel_id=1, source_target_pairs={{0,4},{4,0},{8,12},{12,8},{16,20},{20,16},{24,28},{28,24},{1,5},{5... | collective-permute-start | bytes 196616 | tf_op jit(solution)/shard_map/ppermute | solution.py:23
  98.8 0.0 collective-permute-done.22.rest_1_
  98.8 2.1 %collective-permute-start.23 = (bf16[16,2048]{1,0:T(8,128)(2,1)S(1)}, bf16[16,2048]{1,0:T(8,128)(2,1)S(1)}, u32[]{:S(2)}, u32[]{:S(2)}) collective-permute-start(bf16[16,2048]{1,0:T(8,128)(2,1)S(1)} %collective-permute-done.22.rest_1_), channel_id=1, source_target_pairs={{0,4},{4,0},{8,12},{12,8},{16,20},{20,16},{24,28},{28,24},{1,5},{5... | collective-permute-start | bytes 196616 | tf_op jit(solution)/shard_map/ppermute | solution.py:23
  100.9 0.2 collective-permute-done.24.rest_3_
  101.1 1.4 %collective-permute-start.25 = (bf16[16,2048]{1,0:T(8,128)(2,1)S(1)}, bf16[16,2048]{1,0:T(8,128)(2,1)S(1)}, u32[]{:S(2)}, u32[]{:S(2)}) collective-permute-start(bf16[16,2048]{1,0:T(8,128)(2,1)S(1)} %collective-permute-done.24.rest_3_), channel_id=1, source_target_pairs={{0,4},{4,0},{8,12},{12,8},{16,20},{20,16},{24,28},{28,24},{1,5},{5... | collective-permute-start | bytes 196616 | tf_op jit(solution)/shard_map/ppermute | solution.py:23
  102.5 0.6 collective-permute-start.27
  103.1 0.0 collective-permute-done.28.rest_6_
  103.1 0.6 collective-permute-done.23.rest_0_
  103.7 1.6 %collective-permute-done.25.rest_2_ = bf16[16,2048]{1,0:T(8,128)(2,1)S(1)} collective-permute-done((bf16[16,2048]{1,0:T(8,128)(2,1)S(1)}, bf16[16,2048]{1,0:T(8,128)(2,1)S(1)}, u32[]{:S(2)}, u32[]{:S(2)}) %collective-permute-start.25) | collective-permute-done | bytes 65568 | tf_op jit(solution)/shard_map/ppermute | solution.py:23
  105.4 1.4 %collective-permute-done.27.rest_4_ = bf16[16,2048]{1,0:T(8,128)(2,1)S(1)} collective-permute-done((bf16[16,2048]{1,0:T(8,128)(2,1)S(1)}, bf16[16,2048]{1,0:T(8,128)(2,1)S(1)}, u32[]{:S(2)}, u32[]{:S(2)}) %collective-permute-start.27) | collective-permute-done | bytes 65568 | tf_op jit(solution)/shard_map/ppermute | solution.py:23
  106.8 3.8 %hop.5 = (f32[16,512]{1,0:T(8,128)S(1)}, f32[16,512]{1,0:T(8,128)S(1)}, f32[16,512]{1,0:T(8,128)S(1)}, f32[16,512]{1,0:T(8,128)S(1)}) custom-call(s32[12,128]{1,0:T(8,128)S(1)} %get-tuple-element.25.meta, s32[1]{0:T(128)} %bitcast.2.part, s32[1]{0:T(128)} %bitcast.place, bf16[16,2048]{1,0:T(8,128)(2,1)S(1)} %collective-permute-done.23.rest_0_, ...), custom_call_target="tpu_custom_call" | custom-call | flops 134217728 | bytes 8388608 | tf_op jit(solution)/shard_map/hop/pallas_call | solution.py:323
  110.5 0.1 collective-permute-start.29
  110.6 0.7 collective-permute-start.30
  111.3 1.2 %collective-permute-start.31 = (f32[16,512]{1,0:T(8,128)S(1)}, f32[16,512]{1,0:T(8,128)S(1)}, u32[]{:S(2)}, u32[]{:S(2)}) collective-permute-start(f32[16,512]{1,0:T(8,128)S(1)} %get-tuple-element.36), channel_id=1, source_target_pairs={{0,3},{1,2},{2,1},{3,0},{4,7},{5,6},{6,5},{7,4},{8,11},{9,10},{10,... | collective-permute-start | bytes 98312 | tf_op jit(solution)/shard_map/ppermute | solution.py:23
  112.5 2.4 %collective-permute-done.30.rest_2_ = f32[16,512]{1,0:T(8,128)S(1)} collective-permute-done((f32[16,512]{1,0:T(8,128)S(1)}, f32[16,512]{1,0:T(8,128)S(1)}, u32[]{:S(2)}, u32[]{:S(2)}) %collective-permute-start.30) | collective-permute-done | bytes 32800 | tf_op jit(solution)/shard_map/ppermute | solution.py:23
  114.9 0.1 collective-permute-done.31.rest_3_
  115.0 0.7 finish.1
  (27 shorter events, 0.1 us)
Async XLA Ops:
  0.0 6.7 %copy-start = (bf16[64,128,128]{2,1,0:T(8,128)(2,1)S(1)}, bf16[64,128,128]{2,1,0:T(8,128)(2,1)}, u32[]{:S(2)}) copy-start(bf16[64,128,128]{2,1,0:T(8,128)(2,1)} %rest_8_.5) | copy-start | bytes 6291460
  0.0 6.7 %copy-start.2 = (s32[64]{0:T(128)S(1)}, s32[64]{0:T(128)}, u32[]{:S(2)}) copy-start(s32[64]{0:T(128)} %source.1) | copy-start | bytes 772
  0.0 21.0 %copy-start.3 = (bf16[768,256]{1,0:T(8,128)(2,1)S(1)}, bf16[768,256]{1,0:T(8,128)(2,1)}, u32[]{:S(2)}) copy-start(bf16[768,256]{1,0:T(8,128)(2,1)} %w_in.1) | copy-start | bytes 1179652
  0.0 21.0 %copy-start.4 = (bf16[256,64]{0,1:T(8,128)(2,1)S(1)}, bf16[256,64]{0,1:T(8,128)(2,1)}, u32[]{:S(2)}) copy-start(bf16[256,64]{0,1:T(8,128)(2,1)} %param.11) | copy-start | bytes 98308
  0.0 21.0 %copy-start.5 = (s32[8192]{0:T(1024)S(1)}, s32[8192]{0:T(1024)}, u32[]{:S(2)}) copy-start(s32[8192]{0:T(1024)} %param.12) | copy-start | bytes 98308
  0.0 21.0 %copy-start.6 = (s32[64]{0:T(128)S(1)}, s32[64]{0:T(128)}, u32[]{:S(2)}) copy-start(s32[64]{0:T(128)} %param.14) | copy-start | bytes 772
  0.0 47.3 %collective-permute-start.3 = (bf16[64,128,128]{2,1,0:T(8,128)(2,1)}, bf16[64,128,128]{2,1,0:T(8,128)(2,1)}, u32[]{:S(2)}, u32[]{:S(2)}) collective-permute-start(bf16[64,128,128]{2,1,0:T(8,128)(2,1)} %rest_8_.5), channel_id=1, source_target_pairs={{0,1},{1,0},{2,3},{3,2},{4,5},{5,4},{6,7},{7,6},{8,9},{9,8},{10,11... | collective-permute-start | bytes 6291464 | tf_op jit(solution)/shard_map/ppermute | solution.py:23
  3.6 43.6 %collective-permute-start.11 = (bf16[48,128,128]{2,1,0:T(8,128)(2,1)}, bf16[48,128,128]{2,1,0:T(8,128)(2,1)}, u32[]{:S(2)}, u32[]{:S(2)}) collective-permute-start(bf16[48,128,128]{2,1,0:T(8,128)(2,1)} %slice.7), channel_id=1, source_target_pairs={{0,2},{1,3},{2,0},{3,1},{4,6},{5,7},{6,4},{7,5},{8,10},{9,11},{10,... | collective-permute-start | bytes 4718600 | tf_op jit(solution)/shard_map/ppermute | solution.py:23
  8.4 12.7 %all-to-all-start = ((f32[8,16,128]{2,1,0:T(8,128)}), f32[8,16,128]{2,1,0:T(8,128)S(1)}, u32[]{:S(2)}, u32[]{:S(2)}) async-start(f32[8,16,128]{2,1,0:T(8,128)} %column_sums.1), calls=%async_computation | async-start | bytes 131072 | tf_op jit(solution)/shard_map/all_to_all | solution.py:388
  36.2 1.9 %collective-permute-start = (f32[16,2304]{1,0:T(8,128)S(1)}, f32[16,2304]{1,0:T(8,128)S(1)}, u32[]{:S(2)}, u32[]{:S(2)}) collective-permute-start(f32[16,2304]{1,0:T(8,128)S(1)} %get-tuple-element.22), channel_id=1, source_target_pairs={{0,1},{1,0},{2,3},{3,2},{4,5},{5,4},{6,7},{7,6},{8,9},{9,8},{10,11... | collective-permute-start | bytes 442376 | tf_op jit(solution)/shard_map/ppermute | solution.py:23
  36.3 8.3 %collective-permute-start.1 = (f32[16,2304]{1,0:T(8,128)S(1)}, f32[16,2304]{1,0:T(8,128)S(1)}, u32[]{:S(2)}, u32[]{:S(2)}) collective-permute-start(f32[16,2304]{1,0:T(8,128)S(1)} %get-tuple-element.23), channel_id=1, source_target_pairs={{0,2},{1,3},{2,0},{3,1},{4,6},{5,7},{6,4},{7,5},{8,10},{9,11},{10,... | collective-permute-start | bytes 442376 | tf_op jit(solution)/shard_map/ppermute | solution.py:23
  36.9 10.4 %copy-start.1 = (s32[2048]{0:T(1024)S(1)}, s32[2048]{0:T(1024)}, u32[]{:S(2)}) copy-start(s32[2048]{0:T(1024)} %param.17) | copy-start | bytes 24580
  36.9 10.2 %collective-permute-start.2 = (f32[16,2304]{1,0:T(8,128)S(1)}, f32[16,2304]{1,0:T(8,128)S(1)}, u32[]{:S(2)}, u32[]{:S(2)}) collective-permute-start(f32[16,2304]{1,0:T(8,128)S(1)} %get-tuple-element.24), channel_id=1, source_target_pairs={{0,3},{1,2},{2,1},{3,0},{4,7},{5,6},{6,5},{7,4},{8,11},{9,10},{10,... | collective-permute-start | bytes 442376 | tf_op jit(solution)/shard_map/ppermute | solution.py:23
  47.1 19.0 %collective-permute-start.13 = (bf16[48,128,128]{2,1,0:T(8,128)(2,1)}, bf16[48,128,128]{2,1,0:T(8,128)(2,1)S(1)}, u32[]{:S(2)}, u32[]{:S(2)}) collective-permute-start(bf16[48,128,128]{2,1,0:T(8,128)(2,1)} %after.2.rest_10_), channel_id=1, source_target_pairs={{0,1},{1,0},{2,3},{3,2},{4,5},{5,4},{6,7},{7,6},{8,9},{9,8},{10,11... | collective-permute-start | bytes 4718600 | tf_op jit(solution)/shard_map/ppermute | solution.py:23
  47.5 18.6 %collective-permute-start.12 = (bf16[16,128,128]{2,1,0:T(8,128)(2,1)S(1)}, bf16[16,128,128]{2,1,0:T(8,128)(2,1)S(1)}, u32[]{:S(2)}, u32[]{:S(2)}) collective-permute-start(bf16[16,128,128]{2,1,0:T(8,128)(2,1)S(1)} %get-tuple-element.28), channel_id=1, source_target_pairs={{0,2},{1,3},{2,0},{3,1},{4,6},{5,7},{6,4},{7,5},{8,10},{9,11},{10,... | collective-permute-start | bytes 1572872 | tf_op jit(solution)/shard_map/ppermute | solution.py:23
  49.3 6.6 %collective-permute-start.4 = (bf16[16,2176]{1,0:T(8,128)(2,1)S(1)}, bf16[16,2176]{1,0:T(8,128)(2,1)S(1)}, u32[]{:S(2)}, u32[]{:S(2)}) collective-permute-start(bf16[16,2176]{1,0:T(8,128)(2,1)S(1)} %get-tuple-element.26.rest_7_), channel_id=1, source_target_pairs={{0,24},{4,28},{8,16},{12,20},{16,8},{20,12},{24,0},{28,4},{1,25},{... | collective-permute-start | bytes 208904 | tf_op jit(solution)/shard_map/ppermute | solution.py:23
  52.9 5.9 %collective-permute-start.6 = (bf16[16,2176]{1,0:T(8,128)(2,1)S(1)}, bf16[16,2176]{1,0:T(8,128)(2,1)S(1)}, u32[]{:S(2)}, u32[]{:S(2)}) collective-permute-start(bf16[16,2176]{1,0:T(8,128)(2,1)S(1)} %get-tuple-element.26.rest_7_), channel_id=1, source_target_pairs={{0,16},{4,20},{8,24},{12,28},{16,0},{20,4},{24,8},{28,12},{1,17},{... | collective-permute-start | bytes 208904 | tf_op jit(solution)/shard_map/ppermute | solution.py:23
  52.9 7.4 %collective-permute-start.8 = (bf16[16,2176]{1,0:T(8,128)(2,1)S(1)}, bf16[16,2176]{1,0:T(8,128)(2,1)S(1)}, u32[]{:S(2)}, u32[]{:S(2)}) collective-permute-start(bf16[16,2176]{1,0:T(8,128)(2,1)S(1)} %get-tuple-element.26.rest_7_), channel_id=1, source_target_pairs={{0,8},{4,12},{8,0},{12,4},{16,24},{20,28},{24,16},{28,20},{1,9},{5... | collective-permute-start | bytes 208904 | tf_op jit(solution)/shard_map/ppermute | solution.py:23
  55.9 5.0 %collective-permute-start.10 = (bf16[16,2176]{1,0:T(8,128)(2,1)S(1)}, bf16[16,2176]{1,0:T(8,128)(2,1)S(1)}, u32[]{:S(2)}, u32[]{:S(2)}) collective-permute-start(bf16[16,2176]{1,0:T(8,128)(2,1)S(1)} %get-tuple-element.26.rest_7_), channel_id=1, source_target_pairs={{0,4},{4,0},{8,12},{12,8},{16,20},{20,16},{24,28},{28,24},{1,5},{5... | collective-permute-start | bytes 208904 | tf_op jit(solution)/shard_map/ppermute | solution.py:23
  58.8 5.0 %collective-permute-start.5 = (bf16[16,2176]{1,0:T(8,128)(2,1)S(1)}, bf16[16,2176]{1,0:T(8,128)(2,1)S(1)}, u32[]{:S(2)}, u32[]{:S(2)}) collective-permute-start(bf16[16,2176]{1,0:T(8,128)(2,1)S(1)} %collective-permute-done.4.refs_6_.rest_1_), channel_id=1, source_target_pairs={{0,4},{4,0},{8,12},{12,8},{16,20},{20,16},{24,28},{28,24},{1,5},{5... | collective-permute-start | bytes 208904 | tf_op jit(solution)/shard_map/ppermute | solution.py:23
  60.3 5.1 %collective-permute-start.7 = (bf16[16,2176]{1,0:T(8,128)(2,1)S(1)}, bf16[16,2176]{1,0:T(8,128)(2,1)S(1)}, u32[]{:S(2)}, u32[]{:S(2)}) collective-permute-start(bf16[16,2176]{1,0:T(8,128)(2,1)S(1)} %collective-permute-done.6.refs_4_.rest_3_), channel_id=1, source_target_pairs={{0,4},{4,0},{8,12},{12,8},{16,20},{20,16},{24,28},{28,24},{1,5},{5... | collective-permute-start | bytes 208904 | tf_op jit(solution)/shard_map/ppermute | solution.py:23
  60.9 5.3 %collective-permute-start.9 = (bf16[16,2176]{1,0:T(8,128)(2,1)S(1)}, bf16[16,2176]{1,0:T(8,128)(2,1)S(1)}, u32[]{:S(2)}, u32[]{:S(2)}) collective-permute-start(bf16[16,2176]{1,0:T(8,128)(2,1)S(1)} %collective-permute-done.8.refs_2_.rest_5_), channel_id=1, source_target_pairs={{0,4},{4,0},{8,12},{12,8},{16,20},{20,16},{24,28},{28,24},{1,5},{5... | collective-permute-start | bytes 208904 | tf_op jit(solution)/shard_map/ppermute | solution.py:23
  66.1 1.9 %collective-permute-start.14 = (bf16[16,128,128]{2,1,0:T(8,128)(2,1)S(1)}, bf16[16,128,128]{2,1,0:T(8,128)(2,1)S(1)}, u32[]{:S(2)}, u32[]{:S(2)}) collective-permute-start(bf16[16,128,128]{2,1,0:T(8,128)(2,1)S(1)} %after.3.rest_11_), channel_id=1, source_target_pairs={{0,1},{1,0},{2,3},{3,2},{4,5},{5,4},{6,7},{7,6},{8,9},{9,8},{10,11... | collective-permute-start | bytes 1572872 | tf_op jit(solution)/shard_map/ppermute | solution.py:23
  71.9 7.1 %collective-permute-start.15 = (bf16[16,2048]{1,0:T(8,128)(2,1)S(1)}, bf16[16,2048]{1,0:T(8,128)(2,1)S(1)}, u32[]{:S(2)}, u32[]{:S(2)}) collective-permute-start(bf16[16,2048]{1,0:T(8,128)(2,1)S(1)} %get-tuple-element.31.rest_7_), channel_id=1, source_target_pairs={{0,24},{4,28},{8,16},{12,20},{16,8},{20,12},{24,0},{28,4},{1,25},{... | collective-permute-start | bytes 196616 | tf_op jit(solution)/shard_map/ppermute | solution.py:23
  76.2 6.5 %collective-permute-start.17 = (bf16[16,2048]{1,0:T(8,128)(2,1)S(1)}, bf16[16,2048]{1,0:T(8,128)(2,1)S(1)}, u32[]{:S(2)}, u32[]{:S(2)}) collective-permute-start(bf16[16,2048]{1,0:T(8,128)(2,1)S(1)} %get-tuple-element.31.rest_7_), channel_id=1, source_target_pairs={{0,16},{4,20},{8,24},{12,28},{16,0},{20,4},{24,8},{28,12},{1,17},{... | collective-permute-start | bytes 196616 | tf_op jit(solution)/shard_map/ppermute | solution.py:23
  76.4 7.3 %collective-permute-start.19 = (bf16[16,2048]{1,0:T(8,128)(2,1)S(1)}, bf16[16,2048]{1,0:T(8,128)(2,1)S(1)}, u32[]{:S(2)}, u32[]{:S(2)}) collective-permute-start(bf16[16,2048]{1,0:T(8,128)(2,1)S(1)} %get-tuple-element.31.rest_7_), channel_id=1, source_target_pairs={{0,8},{4,12},{8,0},{12,4},{16,24},{20,28},{24,16},{28,20},{1,9},{5... | collective-permute-start | bytes 196616 | tf_op jit(solution)/shard_map/ppermute | solution.py:23
  76.9 7.9 %collective-permute-start.21 = (bf16[16,2048]{1,0:T(8,128)(2,1)S(1)}, bf16[16,2048]{1,0:T(8,128)(2,1)S(1)}, u32[]{:S(2)}, u32[]{:S(2)}) collective-permute-start(bf16[16,2048]{1,0:T(8,128)(2,1)S(1)} %get-tuple-element.31.rest_7_), channel_id=1, source_target_pairs={{0,4},{4,0},{8,12},{12,8},{16,20},{20,16},{24,28},{28,24},{1,5},{5... | collective-permute-start | bytes 196616 | tf_op jit(solution)/shard_map/ppermute | solution.py:23
  79.0 5.8 %collective-permute-start.16 = (bf16[16,2048]{1,0:T(8,128)(2,1)S(1)}, bf16[16,2048]{1,0:T(8,128)(2,1)S(1)}, u32[]{:S(2)}, u32[]{:S(2)}) collective-permute-start(bf16[16,2048]{1,0:T(8,128)(2,1)S(1)} %collective-permute-done.15.rest_1_), channel_id=1, source_target_pairs={{0,4},{4,0},{8,12},{12,8},{16,20},{20,16},{24,28},{28,24},{1,5},{5... | collective-permute-start | bytes 196616 | tf_op jit(solution)/shard_map/ppermute | solution.py:23
  82.7 4.6 %collective-permute-start.18 = (bf16[16,2048]{1,0:T(8,128)(2,1)S(1)}, bf16[16,2048]{1,0:T(8,128)(2,1)S(1)}, u32[]{:S(2)}, u32[]{:S(2)}) collective-permute-start(bf16[16,2048]{1,0:T(8,128)(2,1)S(1)} %collective-permute-done.17.rest_3_), channel_id=1, source_target_pairs={{0,4},{4,0},{8,12},{12,8},{16,20},{20,16},{24,28},{28,24},{1,5},{5... | collective-permute-start | bytes 196616 | tf_op jit(solution)/shard_map/ppermute | solution.py:23
  83.7 4.3 %collective-permute-start.20 = (bf16[16,2048]{1,0:T(8,128)(2,1)S(1)}, bf16[16,2048]{1,0:T(8,128)(2,1)S(1)}, u32[]{:S(2)}, u32[]{:S(2)}) collective-permute-start(bf16[16,2048]{1,0:T(8,128)(2,1)S(1)} %collective-permute-done.19.rest_5_), channel_id=1, source_target_pairs={{0,4},{4,0},{8,12},{12,8},{16,20},{20,16},{24,28},{28,24},{1,5},{5... | collective-permute-start | bytes 196616 | tf_op jit(solution)/shard_map/ppermute | solution.py:23
  91.7 7.1 %collective-permute-start.22 = (bf16[16,2048]{1,0:T(8,128)(2,1)S(1)}, bf16[16,2048]{1,0:T(8,128)(2,1)S(1)}, u32[]{:S(2)}, u32[]{:S(2)}) collective-permute-start(bf16[16,2048]{1,0:T(8,128)(2,1)S(1)} %hop.4.rest_7_), channel_id=1, source_target_pairs={{0,24},{4,28},{8,16},{12,20},{16,8},{20,12},{24,0},{28,4},{1,25},{... | collective-permute-start | bytes 196616 | tf_op jit(solution)/shard_map/ppermute | solution.py:23
  95.9 5.2 %collective-permute-start.24 = (bf16[16,2048]{1,0:T(8,128)(2,1)S(1)}, bf16[16,2048]{1,0:T(8,128)(2,1)S(1)}, u32[]{:S(2)}, u32[]{:S(2)}) collective-permute-start(bf16[16,2048]{1,0:T(8,128)(2,1)S(1)} %hop.4.rest_7_), channel_id=1, source_target_pairs={{0,16},{4,20},{8,24},{12,28},{16,0},{20,4},{24,8},{28,12},{1,17},{... | collective-permute-start | bytes 196616 | tf_op jit(solution)/shard_map/ppermute | solution.py:23
  95.9 6.6 %collective-permute-start.26 = (bf16[16,2048]{1,0:T(8,128)(2,1)S(1)}, bf16[16,2048]{1,0:T(8,128)(2,1)S(1)}, u32[]{:S(2)}, u32[]{:S(2)}) collective-permute-start(bf16[16,2048]{1,0:T(8,128)(2,1)S(1)} %hop.4.rest_7_), channel_id=1, source_target_pairs={{0,8},{4,12},{8,0},{12,4},{16,24},{20,28},{24,16},{28,20},{1,9},{5... | collective-permute-start | bytes 196616 | tf_op jit(solution)/shard_map/ppermute | solution.py:23
  96.6 6.6 %collective-permute-start.28 = (bf16[16,2048]{1,0:T(8,128)(2,1)S(1)}, bf16[16,2048]{1,0:T(8,128)(2,1)S(1)}, u32[]{:S(2)}, u32[]{:S(2)}) collective-permute-start(bf16[16,2048]{1,0:T(8,128)(2,1)S(1)} %hop.4.rest_7_), channel_id=1, source_target_pairs={{0,4},{4,0},{8,12},{12,8},{16,20},{20,16},{24,28},{28,24},{1,5},{5... | collective-permute-start | bytes 196616 | tf_op jit(solution)/shard_map/ppermute | solution.py:23
  98.8 4.9 %collective-permute-start.23 = (bf16[16,2048]{1,0:T(8,128)(2,1)S(1)}, bf16[16,2048]{1,0:T(8,128)(2,1)S(1)}, u32[]{:S(2)}, u32[]{:S(2)}) collective-permute-start(bf16[16,2048]{1,0:T(8,128)(2,1)S(1)} %collective-permute-done.22.rest_1_), channel_id=1, source_target_pairs={{0,4},{4,0},{8,12},{12,8},{16,20},{20,16},{24,28},{28,24},{1,5},{5... | collective-permute-start | bytes 196616 | tf_op jit(solution)/shard_map/ppermute | solution.py:23
  101.1 4.3 %collective-permute-start.25 = (bf16[16,2048]{1,0:T(8,128)(2,1)S(1)}, bf16[16,2048]{1,0:T(8,128)(2,1)S(1)}, u32[]{:S(2)}, u32[]{:S(2)}) collective-permute-start(bf16[16,2048]{1,0:T(8,128)(2,1)S(1)} %collective-permute-done.24.rest_3_), channel_id=1, source_target_pairs={{0,4},{4,0},{8,12},{12,8},{16,20},{20,16},{24,28},{28,24},{1,5},{5... | collective-permute-start | bytes 196616 | tf_op jit(solution)/shard_map/ppermute | solution.py:23
  102.5 4.3 %collective-permute-start.27 = (bf16[16,2048]{1,0:T(8,128)(2,1)S(1)}, bf16[16,2048]{1,0:T(8,128)(2,1)S(1)}, u32[]{:S(2)}, u32[]{:S(2)}) collective-permute-start(bf16[16,2048]{1,0:T(8,128)(2,1)S(1)} %collective-permute-done.26.rest_5_), channel_id=1, source_target_pairs={{0,4},{4,0},{8,12},{12,8},{16,20},{20,16},{24,28},{28,24},{1,5},{5... | collective-permute-start | bytes 196616 | tf_op jit(solution)/shard_map/ppermute | solution.py:23
  110.5 1.9 %collective-permute-start.29 = (f32[16,512]{1,0:T(8,128)S(1)}, f32[16,512]{1,0:T(8,128)S(1)}, u32[]{:S(2)}, u32[]{:S(2)}) collective-permute-start(f32[16,512]{1,0:T(8,128)S(1)} %get-tuple-element.34), channel_id=1, source_target_pairs={{0,1},{1,0},{2,3},{3,2},{4,5},{5,4},{6,7},{7,6},{8,9},{9,8},{10,11... | collective-permute-start | bytes 98312 | tf_op jit(solution)/shard_map/ppermute | solution.py:23
  110.6 4.3 %collective-permute-start.30 = (f32[16,512]{1,0:T(8,128)S(1)}, f32[16,512]{1,0:T(8,128)S(1)}, u32[]{:S(2)}, u32[]{:S(2)}) collective-permute-start(f32[16,512]{1,0:T(8,128)S(1)} %get-tuple-element.35), channel_id=1, source_target_pairs={{0,2},{1,3},{2,0},{3,1},{4,6},{5,7},{6,4},{7,5},{8,10},{9,11},{10,... | collective-permute-start | bytes 98312 | tf_op jit(solution)/shard_map/ppermute | solution.py:23
  111.3 3.7 %collective-permute-start.31 = (f32[16,512]{1,0:T(8,128)S(1)}, f32[16,512]{1,0:T(8,128)S(1)}, u32[]{:S(2)}, u32[]{:S(2)}) collective-permute-start(f32[16,512]{1,0:T(8,128)S(1)} %get-tuple-element.36), channel_id=1, source_target_pairs={{0,3},{1,2},{2,1},{3,0},{4,7},{5,6},{6,5},{7,4},{8,11},{9,10},{10,... | collective-permute-start | bytes 98312 | tf_op jit(solution)/shard_map/ppermute | solution.py:23

commit v4 on v3

--- a/solution.py
+++ b/solution.py
@@ -205,6 +205,33 @@
     )(teleport.reshape(hosts // block, block), *sums, *held)
 
 
+def take_kernel(begin, source, out, sems):
+    size = out.shape[0] // sems.shape[0]
+    copies = []
+    for i in range(sems.shape[0]):
+        rows = pl.ds(begin + i * size, size)
+        copies.append(
+            pltpu.make_async_copy(source.at[rows], out.at[pl.ds(i * size, size)], sems.at[i])
+        )
+    for copy in copies:
+        copy.start()
+    for copy in copies:
+        copy.wait()
+
+
+def take(tiles, begin, end):
+    keep = pl.BlockSpec(memory_space=pl.ANY)
+    return pl.pallas_call(
+        functools.partial(take_kernel, begin),
+        in_specs=[keep],
+        out_specs=keep,
+        out_shape=jax.ShapeDtypeStruct((end - begin, *tiles.shape[1:]), tiles.dtype),
+        scratch_shapes=[pltpu.SemaphoreType.DMA((4,))],
+        compiler_params=pltpu.CompilerParams(vmem_limit_bytes=MIB),
+        name="take",
+    )(tiles)
+
+
 def after_kernel(*refs):
     del refs
 
@@ -223,7 +250,7 @@
 
 
 def hop_kernel(first, last, parts, spans, scale, meta, part, place, *rest):
-    shards, rest = rest[:parts][::-1], rest[parts:]
+    shards, rest = rest[:parts], rest[parts:]
     chunks, rest = rest[: len(spans)], rest[len(spans) :]
     (tele, inverse), outs, (slabs, inflow) = rest[:2], rest[2:-2], rest[-2:]
     blocks, per, block = inflow.shape
@@ -336,7 +363,7 @@
             transcendentals=0,
         ),
         name="hop",
-    )(meta, part, place, *reversed(shards), *chunks, tele, inverse)
+    )(meta, part, place, *shards, *chunks, tele, inverse)
 
 
 def finish_kernel(place, *rest):
@@ -362,11 +389,10 @@
 def spread(sent, axis):
     size = lax.axis_size(axis)
     held = {0: sent}
-    for j in range(size - 2, 2, -2):
+    for j in range(2, size, 2):
         held[j] = xor_send(sent, axis, j)
     held[1] = xor_send(sent, axis, 1)
-    held[2] = xor_send(sent, axis, 2)
-    for j in range(size - 2, 0, -2):
+    for j in range(2, size, 2):
         held[j + 1] = xor_send(held[j], axis, 1)
     return [held[j] for j in range(size)]
 
@@ -382,7 +408,7 @@
 
     near = xor_send(tiles, "doc", 1)
     cut = 3 * slots // 4
-    early, late = tiles[:cut], tiles[cut:]
+    early, late = take(tiles, 0, cut), take(tiles, cut, slots)
     far = {j: [xor_send(early, "doc", j)] for j in range(2, split, 2)}
     degrees = column_sums(src_block, tile_count, tiles, parts, blocks)
     degrees = lax.all_to_all(degrees, "hst", split_axis=0, concat_axis=0, tiled=True)

time: 116 us -> 116 us (level)
  Pallas kernels: 29 us -> 35.5 us
  starting transfers between devices: 46.3 us -> 40.3 us
  local copies, waits for them, and re-layouts: 3.06 us -> 1.62 us
    ppermute x32, starting transfers between devices: 40.5 us -> 34.6 us  [xor_send(): return lax.ppermute(value, axis, [(i, i ^ step) for i in range(size)])]
    pallas_call x3, Pallas kernels: 11.3 us -> 16 us  [hop(): pl.pallas_call(functools.partial(hop_kernel, first, last, parts, spans, f...]
    slice x2 -> x0, local copies, waits for them, and re-layouts: 3.04 us -> none  [body(): early, late = (tiles[:cut], tiles[cut:])]
    pallas_call x0 -> x2, Pallas kernels: none -> 1.9 us  [take(): pl.pallas_call(functools.partial(take_kernel, begin), in_specs=[keep], ou...]
    unnamed x14 -> x16, local copies, waits for them, and re-layouts: 0.03 us -> 1.62 us
  transfers between devices with their start and end apart: 33 -> 33, of which waited for: 18 -> 17; matrix products, arithmetic and copies ran while one was open for 3% -> 0% of each run, Pallas kernels for 15% -> 16%
where the time goes in v4:
time: 116 us
  starting transfers between devices  40.3 us (35%)
  waiting for transfers between devices  37.5 us (32%)
  Pallas kernels  35.5 us (31%)
  local copies, waits for them, and re-layouts  1.62 us (1%)
    ppermute x32, starting transfers between devices, xor_send(): return lax.ppermute(value, axis, [(i, i ^ step) for i in range(size)])  34.6 us
    ppermute x32, waiting for transfers between devices, xor_send(): return lax.ppermute(value, axis, [(i, i ^ step) for i in range(size)])  30.6 us
    pallas_call x3, Pallas kernels, hop(): pl.pallas_call(functools.partial(hop_kernel, first, last, parts, spans, f...  16 us
    pallas_call x1, Pallas kernels, documents(): pl.pallas_call(documents_kernel, grid_spec=pltpu.PrefetchScalarGridSpec(n...  15.1 us
    all_to_all x1, waiting for transfers between devices, body(): lax.all_to_all(degrees, 'hst', split_axis=0, concat_axis=0, tiled=True)  6.9 us
    all_to_all x1, starting transfers between devices, body(): lax.all_to_all(degrees, 'hst', split_axis=0, concat_axis=0, tiled=True)  5.76 us
  transfers between devices with their start and end apart: 33, of which 17 were waited for; matrix products, arithmetic and copies ran while one was open for 0% of the time, Pallas kernels for 16%

profile of v4, /device:TPU:0, one launch (start us, length us, event | category | flops | bytes accessed | tf_op | source)
XLA Modules:
  0.0 115.9 jit_solution(12395980221585017797)
XLA Ops:
  0.0 0.5 collective-permute-start.3
  0.5 1.6 %copy-done = bf16[64,128,128]{2,1,0:T(8,128)(2,1)S(1)} copy-done((bf16[64,128,128]{2,1,0:T(8,128)(2,1)S(1)}, bf16[64,128,128]{2,1,0:T(8,128)(2,1)}, u32[]{:S(2)}) %copy-start) | copy-done | bytes 2097176
  2.1 1.2 %take.3 = bf16[48,128,128]{2,1,0:T(8,128)(2,1)} custom-call(bf16[64,128,128]{2,1,0:T(8,128)(2,1)S(1)} %copy-done), custom_call_target="tpu_custom_call" | custom-call | tf_op jit(solution)/shard_map/take/pallas_call | solution.py:224
  3.3 2.6 %collective-permute-start.11 = (bf16[48,128,128]{2,1,0:T(8,128)(2,1)}, bf16[48,128,128]{2,1,0:T(8,128)(2,1)}, u32[]{:S(2)}, u32[]{:S(2)}) collective-permute-start(bf16[48,128,128]{2,1,0:T(8,128)(2,1)} %take.3), channel_id=1, source_target_pairs={{0,2},{1,3},{2,0},{3,1},{4,6},{5,7},{6,4},{7,5},{8,10},{9,11},{10,... | collective-permute-start | bytes 4718600 | tf_op jit(solution)/shard_map/ppermute | solution.py:23
  6.6 1.7 %column_sums.1 = f32[8,16,128]{2,1,0:T(8,128)} custom-call(s32[64]{0:T(128)S(1)} %copy-done.3, s32[1]{0:T(128)} %copy.18.count, bf16[64,128,128]{2,1,0:T(8,128)(2,1)S(1)} %copy-done.1), custom_call_target="tpu_custom_call" | custom-call | flops 1048576 | bytes 2097152 | tf_op jit(solution)/shard_map/column_sums/pallas_call | solution.py:49
  8.2 5.8 %all-to-all-start = ((f32[8,16,128]{2,1,0:T(8,128)}), f32[8,16,128]{2,1,0:T(8,128)S(1)}, u32[]{:S(2)}, u32[]{:S(2)}) async-start(f32[8,16,128]{2,1,0:T(8,128)} %column_sums.1), calls=%async_computation | async-start | bytes 131072 | tf_op jit(solution)/shard_map/all_to_all | solution.py:414
  14.0 6.9 %all-to-all-done.degrees = f32[8,16,128]{2,1,0:T(8,128)S(1)} async-done(((f32[8,16,128]{2,1,0:T(8,128)}), f32[8,16,128]{2,1,0:T(8,128)S(1)}, u32[]{:S(2)}, u32[]{:S(2)}) %all-to-all-start) | async-done | bytes 65568 | tf_op jit(solution)/shard_map/all_to_all | solution.py:414
  20.9 15.1 %documents.1 = (f32[16,2304]{1,0:T(8,128)S(1)}, f32[16,2304]{1,0:T(8,128)S(1)}, f32[16,2304]{1,0:T(8,128)S(1)}, f32[16,2304]{1,0:T(8,128)S(1)}) custom-call(s32[1]{0:T(128)} %bitcast.place, s32[1]{0:T(128)} %bitcast.2.part, bf16[8192,768]{1,0:T(8,128)(2,1)} %docs.1, bf16[768,256]{1,0:T(8,128)(2,1)S(1)} %copy-done.4, bf16[64,256]{1,0:T(8,128)(2,1)S(1)} %bitcast.12, ...), custom_call_target="tpu_custom_call" | custom-call | flops 7784628224 | bytes 12582912 | tf_op jit(solution)/shard_map/documents/pallas_call | solution.py:129
  36.1 0.1 collective-permute-start
  36.2 0.6 collective-permute-start.1
  36.7 1.3 %collective-permute-start.2 = (f32[16,2304]{1,0:T(8,128)S(1)}, f32[16,2304]{1,0:T(8,128)S(1)}, u32[]{:S(2)}, u32[]{:S(2)}) collective-permute-start(f32[16,2304]{1,0:T(8,128)S(1)} %get-tuple-element.24), channel_id=1, source_target_pairs={{0,3},{1,2},{2,1},{3,0},{4,7},{5,6},{6,5},{7,4},{8,11},{9,10},{10,... | collective-permute-start | bytes 442376 | tf_op jit(solution)/shard_map/ppermute | solution.py:23
  38.0 6.5 %collective-permute-done.1.rest_2_.refs_2_ = f32[16,2304]{1,0:T(8,128)S(1)} collective-permute-done((f32[16,2304]{1,0:T(8,128)S(1)}, f32[16,2304]{1,0:T(8,128)S(1)}, u32[]{:S(2)}, u32[]{:S(2)}) %collective-permute-start.1) | collective-permute-done | bytes 147488 | tf_op jit(solution)/shard_map/ppermute | solution.py:23
  44.5 2.8 %collective-permute-done.2.rest_3_.refs_3_ = f32[16,2304]{1,0:T(8,128)S(1)} collective-permute-done((f32[16,2304]{1,0:T(8,128)S(1)}, f32[16,2304]{1,0:T(8,128)S(1)}, u32[]{:S(2)}, u32[]{:S(2)}) %collective-permute-start.2) | collective-permute-done | bytes 147488 | tf_op jit(solution)/shard_map/ppermute | solution.py:23
  47.3 0.0 collective-permute-done.11.refs_0_
  47.3 0.1 collective-permute-start.13
  47.4 0.7 take.2.rest_4_
  48.1 0.1 start_values.1
  48.3 1.7 %collective-permute-start.12 = (bf16[16,128,128]{2,1,0:T(8,128)(2,1)S(1)}, bf16[16,128,128]{2,1,0:T(8,128)(2,1)S(1)}, u32[]{:S(2)}, u32[]{:S(2)}) collective-permute-start(bf16[16,128,128]{2,1,0:T(8,128)(2,1)S(1)} %get-tuple-element.28), channel_id=1, source_target_pairs={{0,2},{1,3},{2,0},{3,1},{4,6},{5,7},{6,4},{7,5},{8,10},{9,11},{10,... | collective-permute-start | bytes 1572872 | tf_op jit(solution)/shard_map/ppermute | solution.py:23
  50.0 1.5 %collective-permute-start.4 = (bf16[16,2176]{1,0:T(8,128)(2,1)S(1)}, bf16[16,2176]{1,0:T(8,128)(2,1)S(1)}, u32[]{:S(2)}, u32[]{:S(2)}) collective-permute-start(bf16[16,2176]{1,0:T(8,128)(2,1)S(1)} %get-tuple-element.26.rest_0_), channel_id=1, source_target_pairs={{0,4},{4,0},{8,12},{12,8},{16,20},{20,16},{24,28},{28,24},{1,5},{5... | collective-permute-start | bytes 208904 | tf_op jit(solution)/shard_map/ppermute | solution.py:23
  51.5 1.6 %collective-permute-start.5 = (bf16[16,2176]{1,0:T(8,128)(2,1)S(1)}, bf16[16,2176]{1,0:T(8,128)(2,1)S(1)}, u32[]{:S(2)}, u32[]{:S(2)}) collective-permute-start(bf16[16,2176]{1,0:T(8,128)(2,1)S(1)} %get-tuple-element.26.rest_0_), channel_id=1, source_target_pairs={{0,8},{4,12},{8,0},{12,4},{16,24},{20,28},{24,16},{28,20},{1,9},{5... | collective-permute-start | bytes 208904 | tf_op jit(solution)/shard_map/ppermute | solution.py:23
  53.0 2.6 %collective-permute-start.7 = (bf16[16,2176]{1,0:T(8,128)(2,1)S(1)}, bf16[16,2176]{1,0:T(8,128)(2,1)S(1)}, u32[]{:S(2)}, u32[]{:S(2)}) collective-permute-start(bf16[16,2176]{1,0:T(8,128)(2,1)S(1)} %get-tuple-element.26.rest_0_), channel_id=1, source_target_pairs={{0,16},{4,20},{8,24},{12,28},{16,0},{20,4},{24,8},{28,12},{1,17},{... | collective-permute-start | bytes 208904 | tf_op jit(solution)/shard_map/ppermute | solution.py:23
  55.6 0.0 collective-permute-done.4.refs_1_.rest_1_
  55.6 2.3 %collective-permute-start.9 = (bf16[16,2176]{1,0:T(8,128)(2,1)S(1)}, bf16[16,2176]{1,0:T(8,128)(2,1)S(1)}, u32[]{:S(2)}, u32[]{:S(2)}) collective-permute-start(bf16[16,2176]{1,0:T(8,128)(2,1)S(1)} %get-tuple-element.26.rest_0_), channel_id=1, source_target_pairs={{0,24},{4,28},{8,16},{12,20},{16,8},{20,12},{24,0},{28,4},{1,25},{... | collective-permute-start | bytes 208904 | tf_op jit(solution)/shard_map/ppermute | solution.py:23
  57.9 1.5 %collective-permute-start.6 = (bf16[16,2176]{1,0:T(8,128)(2,1)S(1)}, bf16[16,2176]{1,0:T(8,128)(2,1)S(1)}, u32[]{:S(2)}, u32[]{:S(2)}) collective-permute-start(bf16[16,2176]{1,0:T(8,128)(2,1)S(1)} %collective-permute-done.5.refs_2_.rest_2_), channel_id=1, source_target_pairs={{0,4},{4,0},{8,12},{12,8},{16,20},{20,16},{24,28},{28,24},{1,5},{5... | collective-permute-start | bytes 208904 | tf_op jit(solution)/shard_map/ppermute | solution.py:23
  59.4 1.1 collective-permute-done.7.refs_4_.rest_4_
  60.5 0.2 collective-permute-start.8
  60.6 1.2 %collective-permute-done.9.refs_6_.rest_6_ = bf16[16,2176]{1,0:T(8,128)(2,1)S(1)} collective-permute-done((bf16[16,2176]{1,0:T(8,128)(2,1)S(1)}, bf16[16,2176]{1,0:T(8,128)(2,1)S(1)}, u32[]{:S(2)}, u32[]{:S(2)}) %collective-permute-start.9) | collective-permute-done | bytes 69664 | tf_op jit(solution)/shard_map/ppermute | solution.py:23
  61.8 0.7 collective-permute-start.10
  62.5 2.3 %collective-permute-done.8.refs_5_.rest_5_ = bf16[16,2176]{1,0:T(8,128)(2,1)S(1)} collective-permute-done((bf16[16,2176]{1,0:T(8,128)(2,1)S(1)}, bf16[16,2176]{1,0:T(8,128)(2,1)S(1)}, u32[]{:S(2)}, u32[]{:S(2)}) %collective-permute-start.8) | collective-permute-done | bytes 69664 | tf_op jit(solution)/shard_map/ppermute | solution.py:23
  64.8 1.4 %collective-permute-done.10.refs_7_.rest_7_ = bf16[16,2176]{1,0:T(8,128)(2,1)S(1)} collective-permute-done((bf16[16,2176]{1,0:T(8,128)(2,1)S(1)}, bf16[16,2176]{1,0:T(8,128)(2,1)S(1)}, u32[]{:S(2)}, u32[]{:S(2)}) %collective-permute-start.10) | collective-permute-done | bytes 69664 | tf_op jit(solution)/shard_map/ppermute | solution.py:23
  66.2 0.0 collective-permute-done.12.refs_0_
  66.2 1.9 %collective-permute-done.14.rest_13_ = bf16[16,128,128]{2,1,0:T(8,128)(2,1)S(1)} collective-permute-done((bf16[16,128,128]{2,1,0:T(8,128)(2,1)S(1)}, bf16[16,128,128]{2,1,0:T(8,128)(2,1)S(1)}, u32[]{:S(2)}, u32[]{:S(2)}) %collective-permute-start.14) | collective-permute-done | bytes 524320 | tf_op jit(solution)/shard_map/ppermute | solution.py:23
  68.1 5.4 %hop.3 = (bf16[16,2048]{1,0:T(8,128)(2,1)S(1)}, f32[16,2048]{1,0:T(8,128)S(1)}) custom-call(s32[12,128]{1,0:T(8,128)S(1)} %get-tuple-element.25.meta, s32[1]{0:T(128)} %bitcast.2.part, s32[1]{0:T(128)} %bitcast.place, bf16[16,2176]{1,0:T(8,128)(2,1)S(1)} %get-tuple-element.26.rest_0_, bf16[16,2176]{1,0:T(8,128)(2,1)S(1)} %collective-permute-done.4.refs_1_.rest_1_, ...), custom_call_target="tpu_custom_call" | custom-call | flops 134217728 | bytes 8388608 | tf_op jit(solution)/shard_map/hop/pallas_call | solution.py:350
  73.5 0.1 collective-permute-start.16
  73.5 2.0 %collective-permute-start.18 = (bf16[16,2048]{1,0:T(8,128)(2,1)S(1)}, bf16[16,2048]{1,0:T(8,128)(2,1)S(1)}, u32[]{:S(2)}, u32[]{:S(2)}) collective-permute-start(bf16[16,2048]{1,0:T(8,128)(2,1)S(1)} %get-tuple-element.31.rest_0_), channel_id=1, source_target_pairs={{0,16},{4,20},{8,24},{12,28},{16,0},{20,4},{24,8},{28,12},{1,17},{... | collective-permute-start | bytes 196616 | tf_op jit(solution)/shard_map/ppermute | solution.py:23
  75.6 2.3 %collective-permute-start.20 = (bf16[16,2048]{1,0:T(8,128)(2,1)S(1)}, bf16[16,2048]{1,0:T(8,128)(2,1)S(1)}, u32[]{:S(2)}, u32[]{:S(2)}) collective-permute-start(bf16[16,2048]{1,0:T(8,128)(2,1)S(1)} %get-tuple-element.31.rest_0_), channel_id=1, source_target_pairs={{0,24},{4,28},{8,16},{12,20},{16,8},{20,12},{24,0},{28,4},{1,25},{... | collective-permute-start | bytes 196616 | tf_op jit(solution)/shard_map/ppermute | solution.py:23
  77.9 0.0 collective-permute-start.15
  77.9 0.8 collective-permute-done.16.rest_2_
  78.7 1.2 %collective-permute-start.17 = (bf16[16,2048]{1,0:T(8,128)(2,1)S(1)}, bf16[16,2048]{1,0:T(8,128)(2,1)S(1)}, u32[]{:S(2)}, u32[]{:S(2)}) collective-permute-start(bf16[16,2048]{1,0:T(8,128)(2,1)S(1)} %collective-permute-done.16.rest_2_), channel_id=1, source_target_pairs={{0,4},{4,0},{8,12},{12,8},{16,20},{20,16},{24,28},{28,24},{1,5},{5... | collective-permute-start | bytes 196616 | tf_op jit(solution)/shard_map/ppermute | solution.py:23
  80.0 2.2 %collective-permute-done.18.rest_4_ = bf16[16,2048]{1,0:T(8,128)(2,1)S(1)} collective-permute-done((bf16[16,2048]{1,0:T(8,128)(2,1)S(1)}, bf16[16,2048]{1,0:T(8,128)(2,1)S(1)}, u32[]{:S(2)}, u32[]{:S(2)}) %collective-permute-start.18) | collective-permute-done | bytes 65568 | tf_op jit(solution)/shard_map/ppermute | solution.py:23
  82.2 0.0 collective-permute-done.20.rest_6_
  82.2 2.0 %collective-permute-start.21 = (bf16[16,2048]{1,0:T(8,128)(2,1)S(1)}, bf16[16,2048]{1,0:T(8,128)(2,1)S(1)}, u32[]{:S(2)}, u32[]{:S(2)}) collective-permute-start(bf16[16,2048]{1,0:T(8,128)(2,1)S(1)} %collective-permute-done.20.rest_6_), channel_id=1, source_target_pairs={{0,4},{4,0},{8,12},{12,8},{16,20},{20,16},{24,28},{28,24},{1,5},{5... | collective-permute-start | bytes 196616 | tf_op jit(solution)/shard_map/ppermute | solution.py:23
  84.2 2.2 %collective-permute-done.19.rest_5_ = bf16[16,2048]{1,0:T(8,128)(2,1)S(1)} collective-permute-done((bf16[16,2048]{1,0:T(8,128)(2,1)S(1)}, bf16[16,2048]{1,0:T(8,128)(2,1)S(1)}, u32[]{:S(2)}, u32[]{:S(2)}) %collective-permute-start.19) | collective-permute-done | bytes 65568 | tf_op jit(solution)/shard_map/ppermute | solution.py:23
  86.4 0.7 collective-permute-done.21.rest_7_
  87.1 5.3 %hop.4.rest_0_ = bf16[16,2048]{1,0:T(8,128)(2,1)S(1)} custom-call(s32[12,128]{1,0:T(8,128)S(1)} %get-tuple-element.25.meta, s32[1]{0:T(128)} %bitcast.2.part, s32[1]{0:T(128)} %bitcast.place, bf16[16,2048]{1,0:T(8,128)(2,1)S(1)} %get-tuple-element.31.rest_0_, bf16[16,2048]{1,0:T(8,128)(2,1)S(1)} %collective-permute-done.15.rest_1_, ...), custom_call_target="tpu_custom_call" | custom-call | flops 134217728 | bytes 8388608 | tf_op jit(solution)/shard_map/hop/pallas_call | solution.py:350
  92.4 0.1 collective-permute-start.23
  92.5 2.7 %collective-permute-start.25 = (bf16[16,2048]{1,0:T(8,128)(2,1)S(1)}, bf16[16,2048]{1,0:T(8,128)(2,1)S(1)}, u32[]{:S(2)}, u32[]{:S(2)}) collective-permute-start(bf16[16,2048]{1,0:T(8,128)(2,1)S(1)} %hop.4.rest_0_), channel_id=1, source_target_pairs={{0,16},{4,20},{8,24},{12,28},{16,0},{20,4},{24,8},{28,12},{1,17},{... | collective-permute-start | bytes 196616 | tf_op jit(solution)/shard_map/ppermute | solution.py:23
  95.2 1.7 %collective-permute-start.27 = (bf16[16,2048]{1,0:T(8,128)(2,1)S(1)}, bf16[16,2048]{1,0:T(8,128)(2,1)S(1)}, u32[]{:S(2)}, u32[]{:S(2)}) collective-permute-start(bf16[16,2048]{1,0:T(8,128)(2,1)S(1)} %hop.4.rest_0_), channel_id=1, source_target_pairs={{0,24},{4,28},{8,16},{12,20},{16,8},{20,12},{24,0},{28,4},{1,25},{... | collective-permute-start | bytes 196616 | tf_op jit(solution)/shard_map/ppermute | solution.py:23
  96.9 0.0 collective-permute-start.22
  96.9 1.0 collective-permute-done.23.rest_2_
  97.9 1.0 collective-permute-start.24
  98.9 1.0 collective-permute-start.26
  99.9 1.3 %collective-permute-done.27.rest_6_ = bf16[16,2048]{1,0:T(8,128)(2,1)S(1)} collective-permute-done((bf16[16,2048]{1,0:T(8,128)(2,1)S(1)}, bf16[16,2048]{1,0:T(8,128)(2,1)S(1)}, u32[]{:S(2)}, u32[]{:S(2)}) %collective-permute-start.27) | collective-permute-done | bytes 65568 | tf_op jit(solution)/shard_map/ppermute | solution.py:23
  101.3 1.5 %collective-permute-start.28 = (bf16[16,2048]{1,0:T(8,128)(2,1)S(1)}, bf16[16,2048]{1,0:T(8,128)(2,1)S(1)}, u32[]{:S(2)}, u32[]{:S(2)}) collective-permute-start(bf16[16,2048]{1,0:T(8,128)(2,1)S(1)} %collective-permute-done.27.rest_6_), channel_id=1, source_target_pairs={{0,4},{4,0},{8,12},{12,8},{16,20},{20,16},{24,28},{28,24},{1,5},{5... | collective-permute-start | bytes 196616 | tf_op jit(solution)/shard_map/ppermute | solution.py:23
  102.7 0.0 collective-permute-done.22.rest_1_
  102.8 0.0 collective-permute-done.24.rest_3_
  102.8 0.4 collective-permute-done.26.rest_5_
  103.2 2.4 %collective-permute-done.28.rest_7_ = bf16[16,2048]{1,0:T(8,128)(2,1)S(1)} collective-permute-done((bf16[16,2048]{1,0:T(8,128)(2,1)S(1)}, bf16[16,2048]{1,0:T(8,128)(2,1)S(1)}, u32[]{:S(2)}, u32[]{:S(2)}) %collective-permute-start.28) | collective-permute-done | bytes 65568 | tf_op jit(solution)/shard_map/ppermute | solution.py:23
  105.5 5.3 %hop.5 = (f32[16,512]{1,0:T(8,128)S(1)}, f32[16,512]{1,0:T(8,128)S(1)}, f32[16,512]{1,0:T(8,128)S(1)}, f32[16,512]{1,0:T(8,128)S(1)}) custom-call(s32[12,128]{1,0:T(8,128)S(1)} %get-tuple-element.25.meta, s32[1]{0:T(128)} %bitcast.2.part, s32[1]{0:T(128)} %bitcast.place, bf16[16,2048]{1,0:T(8,128)(2,1)S(1)} %hop.4.rest_0_, ...), custom_call_target="tpu_custom_call" | custom-call | flops 134217728 | bytes 8388608 | tf_op jit(solution)/shard_map/hop/pallas_call | solution.py:350
  110.9 0.1 collective-permute-start.29
  111.0 0.6 collective-permute-start.30
  111.5 1.3 %collective-permute-start.31 = (f32[16,512]{1,0:T(8,128)S(1)}, f32[16,512]{1,0:T(8,128)S(1)}, u32[]{:S(2)}, u32[]{:S(2)}) collective-permute-start(f32[16,512]{1,0:T(8,128)S(1)} %get-tuple-element.36), channel_id=1, source_target_pairs={{0,3},{1,2},{2,1},{3,0},{4,7},{5,6},{6,5},{7,4},{8,11},{9,10},{10,... | collective-permute-start | bytes 98312 | tf_op jit(solution)/shard_map/ppermute | solution.py:23
  112.8 2.4 %collective-permute-done.30.rest_2_ = f32[16,512]{1,0:T(8,128)S(1)} collective-permute-done((f32[16,512]{1,0:T(8,128)S(1)}, f32[16,512]{1,0:T(8,128)S(1)}, u32[]{:S(2)}, u32[]{:S(2)}) %collective-permute-start.30) | collective-permute-done | bytes 32800 | tf_op jit(solution)/shard_map/ppermute | solution.py:23
  115.2 0.7 finish.1
  (29 shorter events, 0.1 us)
Async XLA Ops:
  0.0 48.1 %collective-permute-start.3 = (bf16[64,128,128]{2,1,0:T(8,128)(2,1)}, bf16[64,128,128]{2,1,0:T(8,128)(2,1)}, u32[]{:S(2)}, u32[]{:S(2)}) collective-permute-start(bf16[64,128,128]{2,1,0:T(8,128)(2,1)} %rest_8_.5), channel_id=1, source_target_pairs={{0,1},{1,0},{2,3},{3,2},{4,5},{5,4},{6,7},{7,6},{8,9},{9,8},{10,11... | collective-permute-start | bytes 6291464 | tf_op jit(solution)/shard_map/ppermute | solution.py:23
  0.5 1.6 %copy-start = (bf16[64,128,128]{2,1,0:T(8,128)(2,1)S(1)}, bf16[64,128,128]{2,1,0:T(8,128)(2,1)}, u32[]{:S(2)}) copy-start(bf16[64,128,128]{2,1,0:T(8,128)(2,1)} %rest_8_.5) | copy-start | bytes 6291460
  2.0 4.5 %copy-start.1 = (bf16[64,128,128]{2,1,0:T(8,128)(2,1)S(1)}, bf16[64,128,128]{2,1,0:T(8,128)(2,1)}, u32[]{:S(2)}) copy-start(bf16[64,128,128]{2,1,0:T(8,128)(2,1)} %rest_8_.5) | copy-start | bytes 6291460
  2.0 4.5 %copy-start.3 = (s32[64]{0:T(128)S(1)}, s32[64]{0:T(128)}, u32[]{:S(2)}) copy-start(s32[64]{0:T(128)} %source.3) | copy-start | bytes 772
  2.0 18.9 %copy-start.4 = (bf16[768,256]{1,0:T(8,128)(2,1)S(1)}, bf16[768,256]{1,0:T(8,128)(2,1)}, u32[]{:S(2)}) copy-start(bf16[768,256]{1,0:T(8,128)(2,1)} %w_in.1) | copy-start | bytes 1179652
  2.1 18.9 %copy-start.5 = (bf16[256,64]{0,1:T(8,128)(2,1)S(1)}, bf16[256,64]{0,1:T(8,128)(2,1)}, u32[]{:S(2)}) copy-start(bf16[256,64]{0,1:T(8,128)(2,1)} %param.11) | copy-start | bytes 98308
  2.1 18.9 %copy-start.6 = (s32[8192]{0:T(1024)S(1)}, s32[8192]{0:T(1024)}, u32[]{:S(2)}) copy-start(s32[8192]{0:T(1024)} %param.12) | copy-start | bytes 98308
  2.1 18.9 %copy-start.7 = (s32[64]{0:T(128)S(1)}, s32[64]{0:T(128)}, u32[]{:S(2)}) copy-start(s32[64]{0:T(128)} %param.14) | copy-start | bytes 772
  3.3 44.0 %collective-permute-start.11 = (bf16[48,128,128]{2,1,0:T(8,128)(2,1)}, bf16[48,128,128]{2,1,0:T(8,128)(2,1)}, u32[]{:S(2)}, u32[]{:S(2)}) collective-permute-start(bf16[48,128,128]{2,1,0:T(8,128)(2,1)} %take.3), channel_id=1, source_target_pairs={{0,2},{1,3},{2,0},{3,1},{4,6},{5,7},{6,4},{7,5},{8,10},{9,11},{10,... | collective-permute-start | bytes 4718600 | tf_op jit(solution)/shard_map/ppermute | solution.py:23
  8.2 12.7 %all-to-all-start = ((f32[8,16,128]{2,1,0:T(8,128)}), f32[8,16,128]{2,1,0:T(8,128)S(1)}, u32[]{:S(2)}, u32[]{:S(2)}) async-start(f32[8,16,128]{2,1,0:T(8,128)} %column_sums.1), calls=%async_computation | async-start | bytes 131072 | tf_op jit(solution)/shard_map/all_to_all | solution.py:414
  36.1 1.9 %collective-permute-start = (f32[16,2304]{1,0:T(8,128)S(1)}, f32[16,2304]{1,0:T(8,128)S(1)}, u32[]{:S(2)}, u32[]{:S(2)}) collective-permute-start(f32[16,2304]{1,0:T(8,128)S(1)} %get-tuple-element.22), channel_id=1, source_target_pairs={{0,1},{1,0},{2,3},{3,2},{4,5},{5,4},{6,7},{7,6},{8,9},{9,8},{10,11... | collective-permute-start | bytes 442376 | tf_op jit(solution)/shard_map/ppermute | solution.py:23
  36.2 8.3 %collective-permute-start.1 = (f32[16,2304]{1,0:T(8,128)S(1)}, f32[16,2304]{1,0:T(8,128)S(1)}, u32[]{:S(2)}, u32[]{:S(2)}) collective-permute-start(f32[16,2304]{1,0:T(8,128)S(1)} %get-tuple-element.23), channel_id=1, source_target_pairs={{0,2},{1,3},{2,0},{3,1},{4,6},{5,7},{6,4},{7,5},{8,10},{9,11},{10,... | collective-permute-start | bytes 442376 | tf_op jit(solution)/shard_map/ppermute | solution.py:23
  36.7 10.6 %collective-permute-start.2 = (f32[16,2304]{1,0:T(8,128)S(1)}, f32[16,2304]{1,0:T(8,128)S(1)}, u32[]{:S(2)}, u32[]{:S(2)}) collective-permute-start(f32[16,2304]{1,0:T(8,128)S(1)} %get-tuple-element.24), channel_id=1, source_target_pairs={{0,3},{1,2},{2,1},{3,0},{4,7},{5,6},{6,5},{7,4},{8,11},{9,10},{10,... | collective-permute-start | bytes 442376 | tf_op jit(solution)/shard_map/ppermute | solution.py:23
  47.3 0.8 copy-start.2
  47.3 18.9 %collective-permute-start.13 = (bf16[48,128,128]{2,1,0:T(8,128)(2,1)}, bf16[48,128,128]{2,1,0:T(8,128)(2,1)S(1)}, u32[]{:S(2)}, u32[]{:S(2)}) collective-permute-start(bf16[48,128,128]{2,1,0:T(8,128)(2,1)} %after.2.rest_10_), channel_id=1, source_target_pairs={{0,1},{1,0},{2,3},{3,2},{4,5},{5,4},{6,7},{7,6},{8,9},{9,8},{10,11... | collective-permute-start | bytes 4718600 | tf_op jit(solution)/shard_map/ppermute | solution.py:23
  48.3 17.9 %collective-permute-start.12 = (bf16[16,128,128]{2,1,0:T(8,128)(2,1)S(1)}, bf16[16,128,128]{2,1,0:T(8,128)(2,1)S(1)}, u32[]{:S(2)}, u32[]{:S(2)}) collective-permute-start(bf16[16,128,128]{2,1,0:T(8,128)(2,1)S(1)} %get-tuple-element.28), channel_id=1, source_target_pairs={{0,2},{1,3},{2,0},{3,1},{4,6},{5,7},{6,4},{7,5},{8,10},{9,11},{10,... | collective-permute-start | bytes 1572872 | tf_op jit(solution)/shard_map/ppermute | solution.py:23
  50.0 5.7 %collective-permute-start.4 = (bf16[16,2176]{1,0:T(8,128)(2,1)S(1)}, bf16[16,2176]{1,0:T(8,128)(2,1)S(1)}, u32[]{:S(2)}, u32[]{:S(2)}) collective-permute-start(bf16[16,2176]{1,0:T(8,128)(2,1)S(1)} %get-tuple-element.26.rest_0_), channel_id=1, source_target_pairs={{0,4},{4,0},{8,12},{12,8},{16,20},{20,16},{24,28},{28,24},{1,5},{5... | collective-permute-start | bytes 208904 | tf_op jit(solution)/shard_map/ppermute | solution.py:23
  51.5 6.4 %collective-permute-start.5 = (bf16[16,2176]{1,0:T(8,128)(2,1)S(1)}, bf16[16,2176]{1,0:T(8,128)(2,1)S(1)}, u32[]{:S(2)}, u32[]{:S(2)}) collective-permute-start(bf16[16,2176]{1,0:T(8,128)(2,1)S(1)} %get-tuple-element.26.rest_0_), channel_id=1, source_target_pairs={{0,8},{4,12},{8,0},{12,4},{16,24},{20,28},{24,16},{28,20},{1,9},{5... | collective-permute-start | bytes 208904 | tf_op jit(solution)/shard_map/ppermute | solution.py:23
  53.0 7.4 %collective-permute-start.7 = (bf16[16,2176]{1,0:T(8,128)(2,1)S(1)}, bf16[16,2176]{1,0:T(8,128)(2,1)S(1)}, u32[]{:S(2)}, u32[]{:S(2)}) collective-permute-start(bf16[16,2176]{1,0:T(8,128)(2,1)S(1)} %get-tuple-element.26.rest_0_), channel_id=1, source_target_pairs={{0,16},{4,20},{8,24},{12,28},{16,0},{20,4},{24,8},{28,12},{1,17},{... | collective-permute-start | bytes 208904 | tf_op jit(solution)/shard_map/ppermute | solution.py:23
  55.6 6.2 %collective-permute-start.9 = (bf16[16,2176]{1,0:T(8,128)(2,1)S(1)}, bf16[16,2176]{1,0:T(8,128)(2,1)S(1)}, u32[]{:S(2)}, u32[]{:S(2)}) collective-permute-start(bf16[16,2176]{1,0:T(8,128)(2,1)S(1)} %get-tuple-element.26.rest_0_), channel_id=1, source_target_pairs={{0,24},{4,28},{8,16},{12,20},{16,8},{20,12},{24,0},{28,4},{1,25},{... | collective-permute-start | bytes 208904 | tf_op jit(solution)/shard_map/ppermute | solution.py:23
  57.9 4.6 %collective-permute-start.6 = (bf16[16,2176]{1,0:T(8,128)(2,1)S(1)}, bf16[16,2176]{1,0:T(8,128)(2,1)S(1)}, u32[]{:S(2)}, u32[]{:S(2)}) collective-permute-start(bf16[16,2176]{1,0:T(8,128)(2,1)S(1)} %collective-permute-done.5.refs_2_.rest_2_), channel_id=1, source_target_pairs={{0,4},{4,0},{8,12},{12,8},{16,20},{20,16},{24,28},{28,24},{1,5},{5... | collective-permute-start | bytes 208904 | tf_op jit(solution)/shard_map/ppermute | solution.py:23
  60.5 4.3 %collective-permute-start.8 = (bf16[16,2176]{1,0:T(8,128)(2,1)S(1)}, bf16[16,2176]{1,0:T(8,128)(2,1)S(1)}, u32[]{:S(2)}, u32[]{:S(2)}) collective-permute-start(bf16[16,2176]{1,0:T(8,128)(2,1)S(1)} %collective-permute-done.7.refs_4_.rest_4_), channel_id=1, source_target_pairs={{0,4},{4,0},{8,12},{12,8},{16,20},{20,16},{24,28},{28,24},{1,5},{5... | collective-permute-start | bytes 208904 | tf_op jit(solution)/shard_map/ppermute | solution.py:23
  61.8 4.3 %collective-permute-start.10 = (bf16[16,2176]{1,0:T(8,128)(2,1)S(1)}, bf16[16,2176]{1,0:T(8,128)(2,1)S(1)}, u32[]{:S(2)}, u32[]{:S(2)}) collective-permute-start(bf16[16,2176]{1,0:T(8,128)(2,1)S(1)} %collective-permute-done.9.refs_6_.rest_6_), channel_id=1, source_target_pairs={{0,4},{4,0},{8,12},{12,8},{16,20},{20,16},{24,28},{28,24},{1,5},{5... | collective-permute-start | bytes 208904 | tf_op jit(solution)/shard_map/ppermute | solution.py:23
  66.2 1.9 %collective-permute-start.14 = (bf16[16,128,128]{2,1,0:T(8,128)(2,1)S(1)}, bf16[16,128,128]{2,1,0:T(8,128)(2,1)S(1)}, u32[]{:S(2)}, u32[]{:S(2)}) collective-permute-start(bf16[16,128,128]{2,1,0:T(8,128)(2,1)S(1)} %after.3.rest_11_), channel_id=1, source_target_pairs={{0,1},{1,0},{2,3},{3,2},{4,5},{5,4},{6,7},{7,6},{8,9},{9,8},{10,11... | collective-permute-start | bytes 1572872 | tf_op jit(solution)/shard_map/ppermute | solution.py:23
  73.5 5.2 %collective-permute-start.16 = (bf16[16,2048]{1,0:T(8,128)(2,1)S(1)}, bf16[16,2048]{1,0:T(8,128)(2,1)S(1)}, u32[]{:S(2)}, u32[]{:S(2)}) collective-permute-start(bf16[16,2048]{1,0:T(8,128)(2,1)S(1)} %get-tuple-element.31.rest_0_), channel_id=1, source_target_pairs={{0,8},{4,12},{8,0},{12,4},{16,24},{20,28},{24,16},{28,20},{1,9},{5... | collective-permute-start | bytes 196616 | tf_op jit(solution)/shard_map/ppermute | solution.py:23
  73.5 8.6 %collective-permute-start.18 = (bf16[16,2048]{1,0:T(8,128)(2,1)S(1)}, bf16[16,2048]{1,0:T(8,128)(2,1)S(1)}, u32[]{:S(2)}, u32[]{:S(2)}) collective-permute-start(bf16[16,2048]{1,0:T(8,128)(2,1)S(1)} %get-tuple-element.31.rest_0_), channel_id=1, source_target_pairs={{0,16},{4,20},{8,24},{12,28},{16,0},{20,4},{24,8},{28,12},{1,17},{... | collective-permute-start | bytes 196616 | tf_op jit(solution)/shard_map/ppermute | solution.py:23
  75.6 6.6 %collective-permute-start.20 = (bf16[16,2048]{1,0:T(8,128)(2,1)S(1)}, bf16[16,2048]{1,0:T(8,128)(2,1)S(1)}, u32[]{:S(2)}, u32[]{:S(2)}) collective-permute-start(bf16[16,2048]{1,0:T(8,128)(2,1)S(1)} %get-tuple-element.31.rest_0_), channel_id=1, source_target_pairs={{0,24},{4,28},{8,16},{12,20},{16,8},{20,12},{24,0},{28,4},{1,25},{... | collective-permute-start | bytes 196616 | tf_op jit(solution)/shard_map/ppermute | solution.py:23
  77.9 6.3 %collective-permute-start.15 = (bf16[16,2048]{1,0:T(8,128)(2,1)S(1)}, bf16[16,2048]{1,0:T(8,128)(2,1)S(1)}, u32[]{:S(2)}, u32[]{:S(2)}) collective-permute-start(bf16[16,2048]{1,0:T(8,128)(2,1)S(1)} %get-tuple-element.31.rest_0_), channel_id=1, source_target_pairs={{0,4},{4,0},{8,12},{12,8},{16,20},{20,16},{24,28},{28,24},{1,5},{5... | collective-permute-start | bytes 196616 | tf_op jit(solution)/shard_map/ppermute | solution.py:23
  78.7 5.5 %collective-permute-start.17 = (bf16[16,2048]{1,0:T(8,128)(2,1)S(1)}, bf16[16,2048]{1,0:T(8,128)(2,1)S(1)}, u32[]{:S(2)}, u32[]{:S(2)}) collective-permute-start(bf16[16,2048]{1,0:T(8,128)(2,1)S(1)} %collective-permute-done.16.rest_2_), channel_id=1, source_target_pairs={{0,4},{4,0},{8,12},{12,8},{16,20},{20,16},{24,28},{28,24},{1,5},{5... | collective-permute-start | bytes 196616 | tf_op jit(solution)/shard_map/ppermute | solution.py:23
  82.2 4.3 %collective-permute-start.19 = (bf16[16,2048]{1,0:T(8,128)(2,1)S(1)}, bf16[16,2048]{1,0:T(8,128)(2,1)S(1)}, u32[]{:S(2)}, u32[]{:S(2)}) collective-permute-start(bf16[16,2048]{1,0:T(8,128)(2,1)S(1)} %collective-permute-done.18.rest_4_), channel_id=1, source_target_pairs={{0,4},{4,0},{8,12},{12,8},{16,20},{20,16},{24,28},{28,24},{1,5},{5... | collective-permute-start | bytes 196616 | tf_op jit(solution)/shard_map/ppermute | solution.py:23
  82.2 5.0 %collective-permute-start.21 = (bf16[16,2048]{1,0:T(8,128)(2,1)S(1)}, bf16[16,2048]{1,0:T(8,128)(2,1)S(1)}, u32[]{:S(2)}, u32[]{:S(2)}) collective-permute-start(bf16[16,2048]{1,0:T(8,128)(2,1)S(1)} %collective-permute-done.20.rest_6_), channel_id=1, source_target_pairs={{0,4},{4,0},{8,12},{12,8},{16,20},{20,16},{24,28},{28,24},{1,5},{5... | collective-permute-start | bytes 196616 | tf_op jit(solution)/shard_map/ppermute | solution.py:23
  92.4 5.5 %collective-permute-start.23 = (bf16[16,2048]{1,0:T(8,128)(2,1)S(1)}, bf16[16,2048]{1,0:T(8,128)(2,1)S(1)}, u32[]{:S(2)}, u32[]{:S(2)}) collective-permute-start(bf16[16,2048]{1,0:T(8,128)(2,1)S(1)} %hop.4.rest_0_), channel_id=1, source_target_pairs={{0,8},{4,12},{8,0},{12,4},{16,24},{20,28},{24,16},{28,20},{1,9},{5... | collective-permute-start | bytes 196616 | tf_op jit(solution)/shard_map/ppermute | solution.py:23
  92.5 6.4 %collective-permute-start.25 = (bf16[16,2048]{1,0:T(8,128)(2,1)S(1)}, bf16[16,2048]{1,0:T(8,128)(2,1)S(1)}, u32[]{:S(2)}, u32[]{:S(2)}) collective-permute-start(bf16[16,2048]{1,0:T(8,128)(2,1)S(1)} %hop.4.rest_0_), channel_id=1, source_target_pairs={{0,16},{4,20},{8,24},{12,28},{16,0},{20,4},{24,8},{28,12},{1,17},{... | collective-permute-start | bytes 196616 | tf_op jit(solution)/shard_map/ppermute | solution.py:23
  95.2 6.1 %collective-permute-start.27 = (bf16[16,2048]{1,0:T(8,128)(2,1)S(1)}, bf16[16,2048]{1,0:T(8,128)(2,1)S(1)}, u32[]{:S(2)}, u32[]{:S(2)}) collective-permute-start(bf16[16,2048]{1,0:T(8,128)(2,1)S(1)} %hop.4.rest_0_), channel_id=1, source_target_pairs={{0,24},{4,28},{8,16},{12,20},{16,8},{20,12},{24,0},{28,4},{1,25},{... | collective-permute-start | bytes 196616 | tf_op jit(solution)/shard_map/ppermute | solution.py:23
  96.9 5.9 %collective-permute-start.22 = (bf16[16,2048]{1,0:T(8,128)(2,1)S(1)}, bf16[16,2048]{1,0:T(8,128)(2,1)S(1)}, u32[]{:S(2)}, u32[]{:S(2)}) collective-permute-start(bf16[16,2048]{1,0:T(8,128)(2,1)S(1)} %hop.4.rest_0_), channel_id=1, source_target_pairs={{0,4},{4,0},{8,12},{12,8},{16,20},{20,16},{24,28},{28,24},{1,5},{5... | collective-permute-start | bytes 196616 | tf_op jit(solution)/shard_map/ppermute | solution.py:23
  97.9 4.8 %collective-permute-start.24 = (bf16[16,2048]{1,0:T(8,128)(2,1)S(1)}, bf16[16,2048]{1,0:T(8,128)(2,1)S(1)}, u32[]{:S(2)}, u32[]{:S(2)}) collective-permute-start(bf16[16,2048]{1,0:T(8,128)(2,1)S(1)} %collective-permute-done.23.rest_2_), channel_id=1, source_target_pairs={{0,4},{4,0},{8,12},{12,8},{16,20},{20,16},{24,28},{28,24},{1,5},{5... | collective-permute-start | bytes 196616 | tf_op jit(solution)/shard_map/ppermute | solution.py:23
  98.9 4.3 %collective-permute-start.26 = (bf16[16,2048]{1,0:T(8,128)(2,1)S(1)}, bf16[16,2048]{1,0:T(8,128)(2,1)S(1)}, u32[]{:S(2)}, u32[]{:S(2)}) collective-permute-start(bf16[16,2048]{1,0:T(8,128)(2,1)S(1)} %collective-permute-done.25.rest_4_), channel_id=1, source_target_pairs={{0,4},{4,0},{8,12},{12,8},{16,20},{20,16},{24,28},{28,24},{1,5},{5... | collective-permute-start | bytes 196616 | tf_op jit(solution)/shard_map/ppermute | solution.py:23
  101.3 4.3 %collective-permute-start.28 = (bf16[16,2048]{1,0:T(8,128)(2,1)S(1)}, bf16[16,2048]{1,0:T(8,128)(2,1)S(1)}, u32[]{:S(2)}, u32[]{:S(2)}) collective-permute-start(bf16[16,2048]{1,0:T(8,128)(2,1)S(1)} %collective-permute-done.27.rest_6_), channel_id=1, source_target_pairs={{0,4},{4,0},{8,12},{12,8},{16,20},{20,16},{24,28},{28,24},{1,5},{5... | collective-permute-start | bytes 196616 | tf_op jit(solution)/shard_map/ppermute | solution.py:23
  110.9 1.9 %collective-permute-start.29 = (f32[16,512]{1,0:T(8,128)S(1)}, f32[16,512]{1,0:T(8,128)S(1)}, u32[]{:S(2)}, u32[]{:S(2)}) collective-permute-start(f32[16,512]{1,0:T(8,128)S(1)} %get-tuple-element.34), channel_id=1, source_target_pairs={{0,1},{1,0},{2,3},{3,2},{4,5},{5,4},{6,7},{7,6},{8,9},{9,8},{10,11... | collective-permute-start | bytes 98312 | tf_op jit(solution)/shard_map/ppermute | solution.py:23
  111.0 4.3 %collective-permute-start.30 = (f32[16,512]{1,0:T(8,128)S(1)}, f32[16,512]{1,0:T(8,128)S(1)}, u32[]{:S(2)}, u32[]{:S(2)}) collective-permute-start(f32[16,512]{1,0:T(8,128)S(1)} %get-tuple-element.35), channel_id=1, source_target_pairs={{0,2},{1,3},{2,0},{3,1},{4,6},{5,7},{6,4},{7,5},{8,10},{9,11},{10,... | collective-permute-start | bytes 98312 | tf_op jit(solution)/shard_map/ppermute | solution.py:23
  111.5 3.7 %collective-permute-start.31 = (f32[16,512]{1,0:T(8,128)S(1)}, f32[16,512]{1,0:T(8,128)S(1)}, u32[]{:S(2)}, u32[]{:S(2)}) collective-permute-start(f32[16,512]{1,0:T(8,128)S(1)} %get-tuple-element.36), channel_id=1, source_target_pairs={{0,3},{1,2},{2,1},{3,0},{4,7},{5,6},{6,5},{7,4},{8,11},{9,10},{10,... | collective-permute-start | bytes 98312 | tf_op jit(solution)/shard_map/ppermute | solution.py:23

commit v5 on v4

--- a/solution.py
+++ b/solution.py
@@ -11,7 +11,8 @@
 LABELS = 3
 DIGITS = 4
 DOC_BLOCK = 1024
-TILE_GROUP = 16
+TILE_GROUP = 8
+SUM_GROUP = 16
 HOP_MIB = 16
 LIFT = 2.0**64
 NT = (((1,), (1,)), ((), ()))
@@ -31,8 +32,8 @@
     def _():
         total[...] = jnp.zeros_like(total)
 
-    for i in range(TILE_GROUP):
-        k = step * TILE_GROUP + i
+    for i in range(SUM_GROUP):
+        k = step * SUM_GROUP + i
         row = jnp.where(k < count[0], source[k], parts * rows)
         part = jnp.sum(tiles[i].astype(jnp.float32), axis=0, keepdims=True)
         total[pl.ds(row, 1), :] += part
@@ -50,8 +51,8 @@
         column_sum_kernel,
         grid_spec=pltpu.PrefetchScalarGridSpec(
             num_scalar_prefetch=2,
-            grid=(slots // TILE_GROUP,),
-            in_specs=[pl.BlockSpec((TILE_GROUP, block, block), lambda i, s, c: (i, 0, 0))],
+            grid=(slots // SUM_GROUP,),
+            in_specs=[pl.BlockSpec((SUM_GROUP, block, block), lambda i, s, c: (i, 0, 0))],
             out_specs=pl.BlockSpec(shape, lambda i, s, c: (0, 0, 0)),
             scratch_shapes=[pltpu.VMEM((parts * rows + 8, block), jnp.float32)],
         ),
@@ -205,28 +206,36 @@
     )(teleport.reshape(hosts // block, block), *sums, *held)
 
 
-def take_kernel(begin, source, out, sems):
-    size = out.shape[0] // sems.shape[0]
+def take_kernel(source, early, late, sems):
     copies = []
-    for i in range(sems.shape[0]):
-        rows = pl.ds(begin + i * size, size)
-        copies.append(
-            pltpu.make_async_copy(source.at[rows], out.at[pl.ds(i * size, size)], sems.at[i])
-        )
+    begin = 0
+    for out in (early, late):
+        size = out.shape[0] // 4
+        for i in range(4):
+            rows = pl.ds(begin + i * size, size)
+            sem = sems.at[len(copies)]
+            copies.append(
+                pltpu.make_async_copy(source.at[rows], out.at[pl.ds(i * size, size)], sem)
+            )
+        begin += out.shape[0]
     for copy in copies:
         copy.start()
     for copy in copies:
         copy.wait()
 
 
-def take(tiles, begin, end):
+def take(tiles, cut):
+    slots, *tile = tiles.shape
     keep = pl.BlockSpec(memory_space=pl.ANY)
     return pl.pallas_call(
-        functools.partial(take_kernel, begin),
+        take_kernel,
         in_specs=[keep],
-        out_specs=keep,
-        out_shape=jax.ShapeDtypeStruct((end - begin, *tiles.shape[1:]), tiles.dtype),
-        scratch_shapes=[pltpu.SemaphoreType.DMA((4,))],
+        out_specs=[keep, keep],
+        out_shape=[
+            jax.ShapeDtypeStruct((cut, *tile), tiles.dtype),
+            jax.ShapeDtypeStruct((slots - cut, *tile), tiles.dtype),
+        ],
+        scratch_shapes=[pltpu.SemaphoreType.DMA((8,))],
         compiler_params=pltpu.CompilerParams(vmem_limit_bytes=MIB),
         name="take",
     )(tiles)
@@ -407,8 +416,8 @@
     labels = [label.reshape(1, -1) for label in (src_block, dst_block, tile_count)]
 
     near = xor_send(tiles, "doc", 1)
-    cut = 3 * slots // 4
-    early, late = take(tiles, 0, cut), take(tiles, cut, slots)
+    cut = 5 * slots // 8
+    early, late = take(tiles, cut)
     far = {j: [xor_send(early, "doc", j)] for j in range(2, split, 2)}
     degrees = column_sums(src_block, tile_count, tiles, parts, blocks)
     degrees = lax.all_to_all(degrees, "hst", split_axis=0, concat_axis=0, tiled=True)

time: 116 us -> 116 us (level)
  waiting for transfers between devices: 37.5 us -> 41.4 us
  starting transfers between devices: 40.3 us -> 36.5 us
  local copies, waits for them, and re-layouts: 1.62 us -> 3.49 us
  Pallas kernels: 35.5 us -> 33.7 us
    ppermute x32, starting transfers between devices: 34.6 us -> 30.6 us  [xor_send(): return lax.ppermute(value, axis, [(i, i ^ step) for i in range(size)])]
    ppermute x32, waiting for transfers between devices: 30.6 us -> 34.5 us  [xor_send(): return lax.ppermute(value, axis, [(i, i ^ step) for i in range(size)])]
    unnamed x16 -> x20, local copies, waits for them, and re-layouts: 1.62 us -> 3.49 us
  transfers between devices with their start and end apart: 33 -> 33, of which waited for: 17 -> 20; matrix products, arithmetic and copies ran while one was open for 0% -> 0% of each run, Pallas kernels for 16% -> 16%
where the time goes in v5:
time: 116 us
  waiting for transfers between devices  41.4 us (36%)
  starting transfers between devices  36.5 us (31%)
  Pallas kernels  33.7 us (29%)
  local copies, waits for them, and re-layouts  3.49 us (3%)
    ppermute x32, waiting for transfers between devices, xor_send(): return lax.ppermute(value, axis, [(i, i ^ step) for i in range(size)])  34.5 us
    ppermute x32, starting transfers between devices, xor_send(): return lax.ppermute(value, axis, [(i, i ^ step) for i in range(size)])  30.6 us
    pallas_call x1, Pallas kernels, documents(): pl.pallas_call(documents_kernel, grid_spec=pltpu.PrefetchScalarGridSpec(n...  15.2 us
    pallas_call x3, Pallas kernels, hop(): pl.pallas_call(functools.partial(hop_kernel, first, last, parts, spans, f...  14.9 us
    all_to_all x1, waiting for transfers between devices, body(): lax.all_to_all(degrees, 'hst', split_axis=0, concat_axis=0, tiled=True)  6.9 us
    all_to_all x1, starting transfers between devices, body(): lax.all_to_all(degrees, 'hst', split_axis=0, concat_axis=0, tiled=True)  5.84 us
    unnamed x20, local copies, waits for them, and re-layouts  3.49 us
  transfers between devices with their start and end apart: 33, of which 20 were waited for; matrix products, arithmetic and copies ran while one was open for 0% of the time, Pallas kernels for 16%

profile of v5, /device:TPU:0, one launch (start us, length us, event | category | flops | bytes accessed | tf_op | source)
XLA Modules:
  0.0 115.9 jit_solution(7260732550946507570)
XLA Ops:
  0.0 0.5 collective-permute-start.3
  0.5 1.6 %copy-done = bf16[64,128,128]{2,1,0:T(8,128)(2,1)S(1)} copy-done((bf16[64,128,128]{2,1,0:T(8,128)(2,1)S(1)}, bf16[64,128,128]{2,1,0:T(8,128)(2,1)}, u32[]{:S(2)}) %copy-start) | copy-done | bytes 2097176
  2.1 1.1 take.1
  3.2 0.9 copy-done.2
  4.1 2.5 %collective-permute-start.11 = (bf16[40,128,128]{2,1,0:T(8,128)(2,1)}, bf16[40,128,128]{2,1,0:T(8,128)(2,1)S(1)}, u32[]{:S(2)}, u32[]{:S(2)}) collective-permute-start(bf16[40,128,128]{2,1,0:T(8,128)(2,1)} %get-tuple-element.31), channel_id=1, source_target_pairs={{0,2},{1,3},{2,0},{3,1},{4,6},{5,7},{6,4},{7,5},{8,10},{9,11},{10,... | collective-permute-start | bytes 3932168 | tf_op jit(solution)/shard_map/ppermute | solution.py:24
  7.3 1.7 %column_sums.1 = f32[8,16,128]{2,1,0:T(8,128)} custom-call(s32[64]{0:T(128)S(1)} %copy-done.5, s32[1]{0:T(128)} %copy.18.count, bf16[64,128,128]{2,1,0:T(8,128)(2,1)S(1)} %copy-done.1), custom_call_target="tpu_custom_call" | custom-call | flops 1048576 | bytes 2097152 | tf_op jit(solution)/shard_map/column_sums/pallas_call | solution.py:50
  9.0 5.8 %all-to-all-start = ((f32[8,16,128]{2,1,0:T(8,128)}), f32[8,16,128]{2,1,0:T(8,128)S(1)}, u32[]{:S(2)}, u32[]{:S(2)}) async-start(f32[8,16,128]{2,1,0:T(8,128)} %column_sums.1), calls=%async_computation | async-start | bytes 131072 | tf_op jit(solution)/shard_map/all_to_all | solution.py:423
  14.8 6.9 %all-to-all-done.degrees = f32[8,16,128]{2,1,0:T(8,128)S(1)} async-done(((f32[8,16,128]{2,1,0:T(8,128)}), f32[8,16,128]{2,1,0:T(8,128)S(1)}, u32[]{:S(2)}, u32[]{:S(2)}) %all-to-all-start) | async-done | bytes 65568 | tf_op jit(solution)/shard_map/all_to_all | solution.py:423
  21.7 0.0 copy-start.6
  21.7 1.0 copy-done.6
  22.7 15.2 %documents.1 = (f32[16,2304]{1,0:T(8,128)S(1)}, f32[16,2304]{1,0:T(8,128)S(1)}, f32[16,2304]{1,0:T(8,128)S(1)}, f32[16,2304]{1,0:T(8,128)S(1)}) custom-call(s32[1]{0:T(128)} %bitcast.place, s32[1]{0:T(128)} %bitcast.2.part, bf16[8192,768]{1,0:T(8,128)(2,1)} %docs.1, bf16[768,256]{1,0:T(8,128)(2,1)S(1)} %copy-done.6, bf16[64,256]{1,0:T(8,128)(2,1)S(1)} %bitcast.12, ...), custom_call_target="tpu_custom_call" | custom-call | flops 7784628224 | bytes 12582912 | tf_op jit(solution)/shard_map/documents/pallas_call | solution.py:130
  37.9 0.1 collective-permute-start
  38.0 0.5 collective-permute-start.1
  38.5 1.3 %collective-permute-start.2 = (f32[16,2304]{1,0:T(8,128)S(1)}, f32[16,2304]{1,0:T(8,128)S(1)}, u32[]{:S(2)}, u32[]{:S(2)}) collective-permute-start(f32[16,2304]{1,0:T(8,128)S(1)} %get-tuple-element.26), channel_id=1, source_target_pairs={{0,3},{1,2},{2,1},{3,0},{4,7},{5,6},{6,5},{7,4},{8,11},{9,10},{10,... | collective-permute-start | bytes 442376 | tf_op jit(solution)/shard_map/ppermute | solution.py:24
  39.9 4.8 %collective-permute-done.1.rest_2_.refs_2_ = f32[16,2304]{1,0:T(8,128)S(1)} collective-permute-done((f32[16,2304]{1,0:T(8,128)S(1)}, f32[16,2304]{1,0:T(8,128)S(1)}, u32[]{:S(2)}, u32[]{:S(2)}) %collective-permute-start.1) | collective-permute-done | bytes 147488 | tf_op jit(solution)/shard_map/ppermute | solution.py:24
  44.7 2.3 %collective-permute-done.2.rest_3_.refs_3_ = f32[16,2304]{1,0:T(8,128)S(1)} collective-permute-done((f32[16,2304]{1,0:T(8,128)S(1)}, f32[16,2304]{1,0:T(8,128)S(1)}, u32[]{:S(2)}, u32[]{:S(2)}) %collective-permute-start.2) | collective-permute-done | bytes 147488 | tf_op jit(solution)/shard_map/ppermute | solution.py:24
  47.0 0.1 start_values.1
  47.1 0.5 collective-permute-start.12
  47.7 0.0 collective-permute-start.13
  47.7 0.6 collective-permute-start.9
  48.2 0.5 collective-permute-start.5
  48.7 3.3 %collective-permute-start.7 = (bf16[16,2176]{1,0:T(8,128)(2,1)S(1)}, bf16[16,2176]{1,0:T(8,128)(2,1)S(1)}, u32[]{:S(2)}, u32[]{:S(2)}) collective-permute-start(bf16[16,2176]{1,0:T(8,128)(2,1)S(1)} %get-tuple-element.29.rest_0_), channel_id=1, source_target_pairs={{0,16},{4,20},{8,24},{12,28},{16,0},{20,4},{24,8},{28,12},{1,17},{... | collective-permute-start | bytes 208904 | tf_op jit(solution)/shard_map/ppermute | solution.py:24
  52.1 2.4 %collective-permute-done.9.refs_6_.rest_6_ = bf16[16,2176]{1,0:T(8,128)(2,1)S(1)} collective-permute-done((bf16[16,2176]{1,0:T(8,128)(2,1)S(1)}, bf16[16,2176]{1,0:T(8,128)(2,1)S(1)}, u32[]{:S(2)}, u32[]{:S(2)}) %collective-permute-start.9) | collective-permute-done | bytes 69664 | tf_op jit(solution)/shard_map/ppermute | solution.py:24
  54.4 0.4 collective-permute-start.4
  54.9 1.8 %collective-permute-start.10 = (bf16[16,2176]{1,0:T(8,128)(2,1)S(1)}, bf16[16,2176]{1,0:T(8,128)(2,1)S(1)}, u32[]{:S(2)}, u32[]{:S(2)}) collective-permute-start(bf16[16,2176]{1,0:T(8,128)(2,1)S(1)} %collective-permute-done.9.refs_6_.rest_6_), channel_id=1, source_target_pairs={{0,4},{4,0},{8,12},{12,8},{16,20},{20,16},{24,28},{28,24},{1,5},{5... | collective-permute-start | bytes 208904 | tf_op jit(solution)/shard_map/ppermute | solution.py:24
  56.7 0.2 collective-permute-start.6
  56.9 2.1 %collective-permute-done.4.refs_1_.rest_1_ = bf16[16,2176]{1,0:T(8,128)(2,1)S(1)} collective-permute-done((bf16[16,2176]{1,0:T(8,128)(2,1)S(1)}, bf16[16,2176]{1,0:T(8,128)(2,1)S(1)}, u32[]{:S(2)}, u32[]{:S(2)}) %collective-permute-start.4) | collective-permute-done | bytes 69664 | tf_op jit(solution)/shard_map/ppermute | solution.py:24
  59.1 0.9 collective-permute-start.8
  59.9 0.6 collective-permute-done.10.refs_7_.rest_7_
  60.6 1.2 %collective-permute-done.6.refs_3_.rest_3_ = bf16[16,2176]{1,0:T(8,128)(2,1)S(1)} collective-permute-done((bf16[16,2176]{1,0:T(8,128)(2,1)S(1)}, bf16[16,2176]{1,0:T(8,128)(2,1)S(1)}, u32[]{:S(2)}, u32[]{:S(2)}) %collective-permute-start.6) | collective-permute-done | bytes 69664 | tf_op jit(solution)/shard_map/ppermute | solution.py:24
  61.7 1.6 %collective-permute-done.8.refs_5_.rest_5_ = bf16[16,2176]{1,0:T(8,128)(2,1)S(1)} collective-permute-done((bf16[16,2176]{1,0:T(8,128)(2,1)S(1)}, bf16[16,2176]{1,0:T(8,128)(2,1)S(1)}, u32[]{:S(2)}, u32[]{:S(2)}) %collective-permute-start.8) | collective-permute-done | bytes 69664 | tf_op jit(solution)/shard_map/ppermute | solution.py:24
  63.4 3.5 %collective-permute-done.12.refs_0_ = bf16[24,128,128]{2,1,0:T(8,128)(2,1)S(1)} collective-permute-done((bf16[24,128,128]{2,1,0:T(8,128)(2,1)S(1)}, bf16[24,128,128]{2,1,0:T(8,128)(2,1)S(1)}, u32[]{:S(2)}, u32[]{:S(2)}) %collective-permute-start.12) | collective-permute-done | bytes 786464 | tf_op jit(solution)/shard_map/ppermute | solution.py:24
  66.9 0.0 collective-permute-start.14
  66.9 0.0 collective-permute-done.13.rest_12_
  66.9 2.3 %collective-permute-done.14.rest_13_ = bf16[24,128,128]{2,1,0:T(8,128)(2,1)S(1)} collective-permute-done((bf16[24,128,128]{2,1,0:T(8,128)(2,1)S(1)}, bf16[24,128,128]{2,1,0:T(8,128)(2,1)S(1)}, u32[]{:S(2)}, u32[]{:S(2)}) %collective-permute-start.14) | collective-permute-done | bytes 786464 | tf_op jit(solution)/shard_map/ppermute | solution.py:24
  69.2 5.0 %hop.3 = (bf16[16,2048]{1,0:T(8,128)(2,1)S(1)}, f32[16,2048]{1,0:T(8,128)S(1)}) custom-call(s32[12,128]{1,0:T(8,128)S(1)} %get-tuple-element.28.meta, s32[1]{0:T(128)} %bitcast.2.part, s32[1]{0:T(128)} %bitcast.place, bf16[16,2176]{1,0:T(8,128)(2,1)S(1)} %get-tuple-element.29.rest_0_, bf16[16,2176]{1,0:T(8,128)(2,1)S(1)} %collective-permute-done.4.refs_1_.rest_1_, ...), custom_call_target="tpu_custom_call" | custom-call | flops 134217728 | bytes 8388608 | tf_op jit(solution)/shard_map/hop/pallas_call | solution.py:359
  74.2 0.7 collective-permute-start.16
  75.0 0.9 collective-permute-start.18
  75.9 2.8 %collective-permute-start.20 = (bf16[16,2048]{1,0:T(8,128)(2,1)S(1)}, bf16[16,2048]{1,0:T(8,128)(2,1)S(1)}, u32[]{:S(2)}, u32[]{:S(2)}) collective-permute-start(bf16[16,2048]{1,0:T(8,128)(2,1)S(1)} %get-tuple-element.35.rest_0_), channel_id=1, source_target_pairs={{0,24},{4,28},{8,16},{12,20},{16,8},{20,12},{24,0},{28,4},{1,25},{... | collective-permute-start | bytes 196616 | tf_op jit(solution)/shard_map/ppermute | solution.py:24
  78.7 0.6 collective-permute-done.16.rest_2_
  79.3 1.4 %collective-permute-start.17 = (bf16[16,2048]{1,0:T(8,128)(2,1)S(1)}, bf16[16,2048]{1,0:T(8,128)(2,1)S(1)}, u32[]{:S(2)}, u32[]{:S(2)}) collective-permute-start(bf16[16,2048]{1,0:T(8,128)(2,1)S(1)} %collective-permute-done.16.rest_2_), channel_id=1, source_target_pairs={{0,4},{4,0},{8,12},{12,8},{16,20},{20,16},{24,28},{28,24},{1,5},{5... | collective-permute-start | bytes 196616 | tf_op jit(solution)/shard_map/ppermute | solution.py:24
  80.7 2.5 %collective-permute-done.18.rest_4_ = bf16[16,2048]{1,0:T(8,128)(2,1)S(1)} collective-permute-done((bf16[16,2048]{1,0:T(8,128)(2,1)S(1)}, bf16[16,2048]{1,0:T(8,128)(2,1)S(1)}, u32[]{:S(2)}, u32[]{:S(2)}) %collective-permute-start.18) | collective-permute-done | bytes 65568 | tf_op jit(solution)/shard_map/ppermute | solution.py:24
  83.2 2.0 %collective-permute-start.21 = (bf16[16,2048]{1,0:T(8,128)(2,1)S(1)}, bf16[16,2048]{1,0:T(8,128)(2,1)S(1)}, u32[]{:S(2)}, u32[]{:S(2)}) collective-permute-start(bf16[16,2048]{1,0:T(8,128)(2,1)S(1)} %collective-permute-done.20.rest_6_), channel_id=1, source_target_pairs={{0,4},{4,0},{8,12},{12,8},{16,20},{20,16},{24,28},{28,24},{1,5},{5... | collective-permute-start | bytes 196616 | tf_op jit(solution)/shard_map/ppermute | solution.py:24
  85.3 2.2 %collective-permute-done.19.rest_5_ = bf16[16,2048]{1,0:T(8,128)(2,1)S(1)} collective-permute-done((bf16[16,2048]{1,0:T(8,128)(2,1)S(1)}, bf16[16,2048]{1,0:T(8,128)(2,1)S(1)}, u32[]{:S(2)}, u32[]{:S(2)}) %collective-permute-start.19) | collective-permute-done | bytes 65568 | tf_op jit(solution)/shard_map/ppermute | solution.py:24
  87.5 0.7 collective-permute-done.21.rest_7_
  88.2 4.9 %hop.4.rest_0_ = bf16[16,2048]{1,0:T(8,128)(2,1)S(1)} custom-call(s32[12,128]{1,0:T(8,128)S(1)} %get-tuple-element.28.meta, s32[1]{0:T(128)} %bitcast.2.part, s32[1]{0:T(128)} %bitcast.place, bf16[16,2048]{1,0:T(8,128)(2,1)S(1)} %get-tuple-element.35.rest_0_, bf16[16,2048]{1,0:T(8,128)(2,1)S(1)} %collective-permute-done.15.rest_1_, ...), custom_call_target="tpu_custom_call" | custom-call | flops 134217728 | bytes 8388608 | tf_op jit(solution)/shard_map/hop/pallas_call | solution.py:359
  93.2 1.1 collective-permute-start.23
  94.2 1.3 %collective-permute-start.25 = (bf16[16,2048]{1,0:T(8,128)(2,1)S(1)}, bf16[16,2048]{1,0:T(8,128)(2,1)S(1)}, u32[]{:S(2)}, u32[]{:S(2)}) collective-permute-start(bf16[16,2048]{1,0:T(8,128)(2,1)S(1)} %hop.4.rest_0_), channel_id=1, source_target_pairs={{0,16},{4,20},{8,24},{12,28},{16,0},{20,4},{24,8},{28,12},{1,17},{... | collective-permute-start | bytes 196616 | tf_op jit(solution)/shard_map/ppermute | solution.py:24
  95.6 2.0 %collective-permute-start.27 = (bf16[16,2048]{1,0:T(8,128)(2,1)S(1)}, bf16[16,2048]{1,0:T(8,128)(2,1)S(1)}, u32[]{:S(2)}, u32[]{:S(2)}) collective-permute-start(bf16[16,2048]{1,0:T(8,128)(2,1)S(1)} %hop.4.rest_0_), channel_id=1, source_target_pairs={{0,24},{4,28},{8,16},{12,20},{16,8},{20,12},{24,0},{28,4},{1,25},{... | collective-permute-start | bytes 196616 | tf_op jit(solution)/shard_map/ppermute | solution.py:24
  97.6 0.9 collective-permute-start.22
  98.5 1.2 collective-permute-start.24
  99.6 0.5 collective-permute-done.25.rest_4_
  100.1 0.4 collective-permute-start.26
  100.5 1.1 collective-permute-done.27.rest_6_
  101.6 0.7 collective-permute-start.28
  102.4 0.4 collective-permute-done.24.rest_3_
  102.7 1.6 %collective-permute-done.26.rest_5_ = bf16[16,2048]{1,0:T(8,128)(2,1)S(1)} collective-permute-done((bf16[16,2048]{1,0:T(8,128)(2,1)S(1)}, bf16[16,2048]{1,0:T(8,128)(2,1)S(1)}, u32[]{:S(2)}, u32[]{:S(2)}) %collective-permute-start.26) | collective-permute-done | bytes 65568 | tf_op jit(solution)/shard_map/ppermute | solution.py:24
  104.4 1.5 %collective-permute-done.28.rest_7_ = bf16[16,2048]{1,0:T(8,128)(2,1)S(1)} collective-permute-done((bf16[16,2048]{1,0:T(8,128)(2,1)S(1)}, bf16[16,2048]{1,0:T(8,128)(2,1)S(1)}, u32[]{:S(2)}, u32[]{:S(2)}) %collective-permute-start.28) | collective-permute-done | bytes 65568 | tf_op jit(solution)/shard_map/ppermute | solution.py:24
  105.9 5.0 %hop.5 = (f32[16,512]{1,0:T(8,128)S(1)}, f32[16,512]{1,0:T(8,128)S(1)}, f32[16,512]{1,0:T(8,128)S(1)}, f32[16,512]{1,0:T(8,128)S(1)}) custom-call(s32[12,128]{1,0:T(8,128)S(1)} %get-tuple-element.28.meta, s32[1]{0:T(128)} %bitcast.2.part, s32[1]{0:T(128)} %bitcast.place, bf16[16,2048]{1,0:T(8,128)(2,1)S(1)} %hop.4.rest_0_, ...), custom_call_target="tpu_custom_call" | custom-call | flops 134217728 | bytes 8388608 | tf_op jit(solution)/shard_map/hop/pallas_call | solution.py:359
  110.9 0.1 collective-permute-start.29
  110.9 0.6 collective-permute-start.30
  111.6 1.2 %collective-permute-start.31 = (f32[16,512]{1,0:T(8,128)S(1)}, f32[16,512]{1,0:T(8,128)S(1)}, u32[]{:S(2)}, u32[]{:S(2)}) collective-permute-start(f32[16,512]{1,0:T(8,128)S(1)} %get-tuple-element.40), channel_id=1, source_target_pairs={{0,3},{1,2},{2,1},{3,0},{4,7},{5,6},{6,5},{7,4},{8,11},{9,10},{10,... | collective-permute-start | bytes 98312 | tf_op jit(solution)/shard_map/ppermute | solution.py:24
  112.8 2.4 %collective-permute-done.30.rest_2_ = f32[16,512]{1,0:T(8,128)S(1)} collective-permute-done((f32[16,512]{1,0:T(8,128)S(1)}, f32[16,512]{1,0:T(8,128)S(1)}, u32[]{:S(2)}, u32[]{:S(2)}) %collective-permute-start.30) | collective-permute-done | bytes 32800 | tf_op jit(solution)/shard_map/ppermute | solution.py:24
  115.2 0.7 finish.1
  (32 shorter events, 0.1 us)
Async XLA Ops:
  0.0 47.0 %collective-permute-start.3 = (bf16[64,128,128]{2,1,0:T(8,128)(2,1)}, bf16[64,128,128]{2,1,0:T(8,128)(2,1)}, u32[]{:S(2)}, u32[]{:S(2)}) collective-permute-start(bf16[64,128,128]{2,1,0:T(8,128)(2,1)} %rest_8_.5), channel_id=1, source_target_pairs={{0,1},{1,0},{2,3},{3,2},{4,5},{5,4},{6,7},{7,6},{8,9},{9,8},{10,11... | collective-permute-start | bytes 6291464 | tf_op jit(solution)/shard_map/ppermute | solution.py:24
  0.5 1.6 %copy-start = (bf16[64,128,128]{2,1,0:T(8,128)(2,1)S(1)}, bf16[64,128,128]{2,1,0:T(8,128)(2,1)}, u32[]{:S(2)}) copy-start(bf16[64,128,128]{2,1,0:T(8,128)(2,1)} %rest_8_.5) | copy-start | bytes 6291460
  2.0 5.2 %copy-start.1 = (bf16[64,128,128]{2,1,0:T(8,128)(2,1)S(1)}, bf16[64,128,128]{2,1,0:T(8,128)(2,1)}, u32[]{:S(2)}) copy-start(bf16[64,128,128]{2,1,0:T(8,128)(2,1)} %rest_8_.5) | copy-start | bytes 6291460
  2.0 5.2 %copy-start.5 = (s32[64]{0:T(128)S(1)}, s32[64]{0:T(128)}, u32[]{:S(2)}) copy-start(s32[64]{0:T(128)} %source.2) | copy-start | bytes 772
  2.0 19.7 %copy-start.7 = (bf16[256,64]{0,1:T(8,128)(2,1)S(1)}, bf16[256,64]{0,1:T(8,128)(2,1)}, u32[]{:S(2)}) copy-start(bf16[256,64]{0,1:T(8,128)(2,1)} %param.11) | copy-start | bytes 98308
  2.1 19.7 %copy-start.8 = (s32[8192]{0:T(1024)S(1)}, s32[8192]{0:T(1024)}, u32[]{:S(2)}) copy-start(s32[8192]{0:T(1024)} %param.12) | copy-start | bytes 98308
  2.1 19.7 %copy-start.9 = (s32[64]{0:T(128)S(1)}, s32[64]{0:T(128)}, u32[]{:S(2)}) copy-start(s32[64]{0:T(128)} %param.14) | copy-start | bytes 772
  3.2 0.9 copy-start.2
  4.1 43.5 %collective-permute-start.11 = (bf16[40,128,128]{2,1,0:T(8,128)(2,1)}, bf16[40,128,128]{2,1,0:T(8,128)(2,1)S(1)}, u32[]{:S(2)}, u32[]{:S(2)}) collective-permute-start(bf16[40,128,128]{2,1,0:T(8,128)(2,1)} %get-tuple-element.31), channel_id=1, source_target_pairs={{0,2},{1,3},{2,0},{3,1},{4,6},{5,7},{6,4},{7,5},{8,10},{9,11},{10,... | collective-permute-start | bytes 3932168 | tf_op jit(solution)/shard_map/ppermute | solution.py:24
  9.0 12.7 %all-to-all-start = ((f32[8,16,128]{2,1,0:T(8,128)}), f32[8,16,128]{2,1,0:T(8,128)S(1)}, u32[]{:S(2)}, u32[]{:S(2)}) async-start(f32[8,16,128]{2,1,0:T(8,128)} %column_sums.1), calls=%async_computation | async-start | bytes 131072 | tf_op jit(solution)/shard_map/all_to_all | solution.py:423
  21.7 1.0 copy-start.6
  22.7 24.3 %copy-start.3 = (bf16[24,128,128]{2,1,0:T(8,128)(2,1)S(1)}, bf16[24,128,128]{2,1,0:T(8,128)(2,1)}, u32[]{:S(2)}) copy-start(bf16[24,128,128]{2,1,0:T(8,128)(2,1)} %copy-done.2) | copy-start | bytes 2359300
  22.7 24.3 %copy-start.4 = (s32[2048]{0:T(1024)S(1)}, s32[2048]{0:T(1024)}, u32[]{:S(2)}) copy-start(s32[2048]{0:T(1024)} %param.17) | copy-start | bytes 24580
  37.9 1.9 %collective-permute-start = (f32[16,2304]{1,0:T(8,128)S(1)}, f32[16,2304]{1,0:T(8,128)S(1)}, u32[]{:S(2)}, u32[]{:S(2)}) collective-permute-start(f32[16,2304]{1,0:T(8,128)S(1)} %get-tuple-element.24), channel_id=1, source_target_pairs={{0,1},{1,0},{2,3},{3,2},{4,5},{5,4},{6,7},{7,6},{8,9},{9,8},{10,11... | collective-permute-start | bytes 442376 | tf_op jit(solution)/shard_map/ppermute | solution.py:24
  38.0 6.7 %collective-permute-start.1 = (f32[16,2304]{1,0:T(8,128)S(1)}, f32[16,2304]{1,0:T(8,128)S(1)}, u32[]{:S(2)}, u32[]{:S(2)}) collective-permute-start(f32[16,2304]{1,0:T(8,128)S(1)} %get-tuple-element.25), channel_id=1, source_target_pairs={{0,2},{1,3},{2,0},{3,1},{4,6},{5,7},{6,4},{7,5},{8,10},{9,11},{10,... | collective-permute-start | bytes 442376 | tf_op jit(solution)/shard_map/ppermute | solution.py:24
  38.5 8.4 %collective-permute-start.2 = (f32[16,2304]{1,0:T(8,128)S(1)}, f32[16,2304]{1,0:T(8,128)S(1)}, u32[]{:S(2)}, u32[]{:S(2)}) collective-permute-start(f32[16,2304]{1,0:T(8,128)S(1)} %get-tuple-element.26), channel_id=1, source_target_pairs={{0,3},{1,2},{2,1},{3,0},{4,7},{5,6},{6,5},{7,4},{8,11},{9,10},{10,... | collective-permute-start | bytes 442376 | tf_op jit(solution)/shard_map/ppermute | solution.py:24
  47.1 19.8 %collective-permute-start.12 = (bf16[24,128,128]{2,1,0:T(8,128)(2,1)S(1)}, bf16[24,128,128]{2,1,0:T(8,128)(2,1)S(1)}, u32[]{:S(2)}, u32[]{:S(2)}) collective-permute-start(bf16[24,128,128]{2,1,0:T(8,128)(2,1)S(1)} %get-tuple-element.32), channel_id=1, source_target_pairs={{0,2},{1,3},{2,0},{3,1},{4,6},{5,7},{6,4},{7,5},{8,10},{9,11},{10,... | collective-permute-start | bytes 2359304 | tf_op jit(solution)/shard_map/ppermute | solution.py:24
  47.7 19.3 %collective-permute-start.13 = (bf16[40,128,128]{2,1,0:T(8,128)(2,1)S(1)}, bf16[40,128,128]{2,1,0:T(8,128)(2,1)S(1)}, u32[]{:S(2)}, u32[]{:S(2)}) collective-permute-start(bf16[40,128,128]{2,1,0:T(8,128)(2,1)S(1)} %after.2.rest_10_), channel_id=1, source_target_pairs={{0,1},{1,0},{2,3},{3,2},{4,5},{5,4},{6,7},{7,6},{8,9},{9,8},{10,11... | collective-permute-start | bytes 3932168 | tf_op jit(solution)/shard_map/ppermute | solution.py:24
  47.7 6.8 %collective-permute-start.9 = (bf16[16,2176]{1,0:T(8,128)(2,1)S(1)}, bf16[16,2176]{1,0:T(8,128)(2,1)S(1)}, u32[]{:S(2)}, u32[]{:S(2)}) collective-permute-start(bf16[16,2176]{1,0:T(8,128)(2,1)S(1)} %get-tuple-element.29.rest_0_), channel_id=1, source_target_pairs={{0,24},{4,28},{8,16},{12,20},{16,8},{20,12},{24,0},{28,4},{1,25},{... | collective-permute-start | bytes 208904 | tf_op jit(solution)/shard_map/ppermute | solution.py:24
  48.2 6.7 %collective-permute-start.5 = (bf16[16,2176]{1,0:T(8,128)(2,1)S(1)}, bf16[16,2176]{1,0:T(8,128)(2,1)S(1)}, u32[]{:S(2)}, u32[]{:S(2)}) collective-permute-start(bf16[16,2176]{1,0:T(8,128)(2,1)S(1)} %get-tuple-element.29.rest_0_), channel_id=1, source_target_pairs={{0,8},{4,12},{8,0},{12,4},{16,24},{20,28},{24,16},{28,20},{1,9},{5... | collective-permute-start | bytes 208904 | tf_op jit(solution)/shard_map/ppermute | solution.py:24
  48.7 8.0 %collective-permute-start.7 = (bf16[16,2176]{1,0:T(8,128)(2,1)S(1)}, bf16[16,2176]{1,0:T(8,128)(2,1)S(1)}, u32[]{:S(2)}, u32[]{:S(2)}) collective-permute-start(bf16[16,2176]{1,0:T(8,128)(2,1)S(1)} %get-tuple-element.29.rest_0_), channel_id=1, source_target_pairs={{0,16},{4,20},{8,24},{12,28},{16,0},{20,4},{24,8},{28,12},{1,17},{... | collective-permute-start | bytes 208904 | tf_op jit(solution)/shard_map/ppermute | solution.py:24
  54.4 4.6 %collective-permute-start.4 = (bf16[16,2176]{1,0:T(8,128)(2,1)S(1)}, bf16[16,2176]{1,0:T(8,128)(2,1)S(1)}, u32[]{:S(2)}, u32[]{:S(2)}) collective-permute-start(bf16[16,2176]{1,0:T(8,128)(2,1)S(1)} %get-tuple-element.29.rest_0_), channel_id=1, source_target_pairs={{0,4},{4,0},{8,12},{12,8},{16,20},{20,16},{24,28},{28,24},{1,5},{5... | collective-permute-start | bytes 208904 | tf_op jit(solution)/shard_map/ppermute | solution.py:24
  54.9 5.7 %collective-permute-start.10 = (bf16[16,2176]{1,0:T(8,128)(2,1)S(1)}, bf16[16,2176]{1,0:T(8,128)(2,1)S(1)}, u32[]{:S(2)}, u32[]{:S(2)}) collective-permute-start(bf16[16,2176]{1,0:T(8,128)(2,1)S(1)} %collective-permute-done.9.refs_6_.rest_6_), channel_id=1, source_target_pairs={{0,4},{4,0},{8,12},{12,8},{16,20},{20,16},{24,28},{28,24},{1,5},{5... | collective-permute-start | bytes 208904 | tf_op jit(solution)/shard_map/ppermute | solution.py:24
  56.7 5.1 %collective-permute-start.6 = (bf16[16,2176]{1,0:T(8,128)(2,1)S(1)}, bf16[16,2176]{1,0:T(8,128)(2,1)S(1)}, u32[]{:S(2)}, u32[]{:S(2)}) collective-permute-start(bf16[16,2176]{1,0:T(8,128)(2,1)S(1)} %collective-permute-done.5.refs_2_.rest_2_), channel_id=1, source_target_pairs={{0,4},{4,0},{8,12},{12,8},{16,20},{20,16},{24,28},{28,24},{1,5},{5... | collective-permute-start | bytes 208904 | tf_op jit(solution)/shard_map/ppermute | solution.py:24
  59.1 4.3 %collective-permute-start.8 = (bf16[16,2176]{1,0:T(8,128)(2,1)S(1)}, bf16[16,2176]{1,0:T(8,128)(2,1)S(1)}, u32[]{:S(2)}, u32[]{:S(2)}) collective-permute-start(bf16[16,2176]{1,0:T(8,128)(2,1)S(1)} %collective-permute-done.7.refs_4_.rest_4_), channel_id=1, source_target_pairs={{0,4},{4,0},{8,12},{12,8},{16,20},{20,16},{24,28},{28,24},{1,5},{5... | collective-permute-start | bytes 208904 | tf_op jit(solution)/shard_map/ppermute | solution.py:24
  66.9 2.3 %collective-permute-start.14 = (bf16[24,128,128]{2,1,0:T(8,128)(2,1)S(1)}, bf16[24,128,128]{2,1,0:T(8,128)(2,1)S(1)}, u32[]{:S(2)}, u32[]{:S(2)}) collective-permute-start(bf16[24,128,128]{2,1,0:T(8,128)(2,1)S(1)} %after.3.rest_11_), channel_id=1, source_target_pairs={{0,1},{1,0},{2,3},{3,2},{4,5},{5,4},{6,7},{7,6},{8,9},{9,8},{10,11... | collective-permute-start | bytes 2359304 | tf_op jit(solution)/shard_map/ppermute | solution.py:24
  74.2 5.0 %collective-permute-start.16 = (bf16[16,2048]{1,0:T(8,128)(2,1)S(1)}, bf16[16,2048]{1,0:T(8,128)(2,1)S(1)}, u32[]{:S(2)}, u32[]{:S(2)}) collective-permute-start(bf16[16,2048]{1,0:T(8,128)(2,1)S(1)} %get-tuple-element.35.rest_0_), channel_id=1, source_target_pairs={{0,8},{4,12},{8,0},{12,4},{16,24},{20,28},{24,16},{28,20},{1,9},{5... | collective-permute-start | bytes 196616 | tf_op jit(solution)/shard_map/ppermute | solution.py:24
  75.0 8.3 %collective-permute-start.18 = (bf16[16,2048]{1,0:T(8,128)(2,1)S(1)}, bf16[16,2048]{1,0:T(8,128)(2,1)S(1)}, u32[]{:S(2)}, u32[]{:S(2)}) collective-permute-start(bf16[16,2048]{1,0:T(8,128)(2,1)S(1)} %get-tuple-element.35.rest_0_), channel_id=1, source_target_pairs={{0,16},{4,20},{8,24},{12,28},{16,0},{20,4},{24,8},{28,12},{1,17},{... | collective-permute-start | bytes 196616 | tf_op jit(solution)/shard_map/ppermute | solution.py:24
  75.9 7.4 %collective-permute-start.20 = (bf16[16,2048]{1,0:T(8,128)(2,1)S(1)}, bf16[16,2048]{1,0:T(8,128)(2,1)S(1)}, u32[]{:S(2)}, u32[]{:S(2)}) collective-permute-start(bf16[16,2048]{1,0:T(8,128)(2,1)S(1)} %get-tuple-element.35.rest_0_), channel_id=1, source_target_pairs={{0,24},{4,28},{8,16},{12,20},{16,8},{20,12},{24,0},{28,4},{1,25},{... | collective-permute-start | bytes 196616 | tf_op jit(solution)/shard_map/ppermute | solution.py:24
  78.7 6.6 %collective-permute-start.15 = (bf16[16,2048]{1,0:T(8,128)(2,1)S(1)}, bf16[16,2048]{1,0:T(8,128)(2,1)S(1)}, u32[]{:S(2)}, u32[]{:S(2)}) collective-permute-start(bf16[16,2048]{1,0:T(8,128)(2,1)S(1)} %get-tuple-element.35.rest_0_), channel_id=1, source_target_pairs={{0,4},{4,0},{8,12},{12,8},{16,20},{20,16},{24,28},{28,24},{1,5},{5... | collective-permute-start | bytes 196616 | tf_op jit(solution)/shard_map/ppermute | solution.py:24
  79.3 6.0 %collective-permute-start.17 = (bf16[16,2048]{1,0:T(8,128)(2,1)S(1)}, bf16[16,2048]{1,0:T(8,128)(2,1)S(1)}, u32[]{:S(2)}, u32[]{:S(2)}) collective-permute-start(bf16[16,2048]{1,0:T(8,128)(2,1)S(1)} %collective-permute-done.16.rest_2_), channel_id=1, source_target_pairs={{0,4},{4,0},{8,12},{12,8},{16,20},{20,16},{24,28},{28,24},{1,5},{5... | collective-permute-start | bytes 196616 | tf_op jit(solution)/shard_map/ppermute | solution.py:24
  83.2 4.3 %collective-permute-start.19 = (bf16[16,2048]{1,0:T(8,128)(2,1)S(1)}, bf16[16,2048]{1,0:T(8,128)(2,1)S(1)}, u32[]{:S(2)}, u32[]{:S(2)}) collective-permute-start(bf16[16,2048]{1,0:T(8,128)(2,1)S(1)} %collective-permute-done.18.rest_4_), channel_id=1, source_target_pairs={{0,4},{4,0},{8,12},{12,8},{16,20},{20,16},{24,28},{28,24},{1,5},{5... | collective-permute-start | bytes 196616 | tf_op jit(solution)/shard_map/ppermute | solution.py:24
  83.2 5.0 %collective-permute-start.21 = (bf16[16,2048]{1,0:T(8,128)(2,1)S(1)}, bf16[16,2048]{1,0:T(8,128)(2,1)S(1)}, u32[]{:S(2)}, u32[]{:S(2)}) collective-permute-start(bf16[16,2048]{1,0:T(8,128)(2,1)S(1)} %collective-permute-done.20.rest_6_), channel_id=1, source_target_pairs={{0,4},{4,0},{8,12},{12,8},{16,20},{20,16},{24,28},{28,24},{1,5},{5... | collective-permute-start | bytes 196616 | tf_op jit(solution)/shard_map/ppermute | solution.py:24
  93.2 5.3 %collective-permute-start.23 = (bf16[16,2048]{1,0:T(8,128)(2,1)S(1)}, bf16[16,2048]{1,0:T(8,128)(2,1)S(1)}, u32[]{:S(2)}, u32[]{:S(2)}) collective-permute-start(bf16[16,2048]{1,0:T(8,128)(2,1)S(1)} %hop.4.rest_0_), channel_id=1, source_target_pairs={{0,8},{4,12},{8,0},{12,4},{16,24},{20,28},{24,16},{28,20},{1,9},{5... | collective-permute-start | bytes 196616 | tf_op jit(solution)/shard_map/ppermute | solution.py:24
  94.2 5.9 %collective-permute-start.25 = (bf16[16,2048]{1,0:T(8,128)(2,1)S(1)}, bf16[16,2048]{1,0:T(8,128)(2,1)S(1)}, u32[]{:S(2)}, u32[]{:S(2)}) collective-permute-start(bf16[16,2048]{1,0:T(8,128)(2,1)S(1)} %hop.4.rest_0_), channel_id=1, source_target_pairs={{0,16},{4,20},{8,24},{12,28},{16,0},{20,4},{24,8},{28,12},{1,17},{... | collective-permute-start | bytes 196616 | tf_op jit(solution)/shard_map/ppermute | solution.py:24
  95.6 6.1 %collective-permute-start.27 = (bf16[16,2048]{1,0:T(8,128)(2,1)S(1)}, bf16[16,2048]{1,0:T(8,128)(2,1)S(1)}, u32[]{:S(2)}, u32[]{:S(2)}) collective-permute-start(bf16[16,2048]{1,0:T(8,128)(2,1)S(1)} %hop.4.rest_0_), channel_id=1, source_target_pairs={{0,24},{4,28},{8,16},{12,20},{16,8},{20,12},{24,0},{28,4},{1,25},{... | collective-permute-start | bytes 196616 | tf_op jit(solution)/shard_map/ppermute | solution.py:24
  97.6 4.8 %collective-permute-start.22 = (bf16[16,2048]{1,0:T(8,128)(2,1)S(1)}, bf16[16,2048]{1,0:T(8,128)(2,1)S(1)}, u32[]{:S(2)}, u32[]{:S(2)}) collective-permute-start(bf16[16,2048]{1,0:T(8,128)(2,1)S(1)} %hop.4.rest_0_), channel_id=1, source_target_pairs={{0,4},{4,0},{8,12},{12,8},{16,20},{20,16},{24,28},{28,24},{1,5},{5... | collective-permute-start | bytes 196616 | tf_op jit(solution)/shard_map/ppermute | solution.py:24
  98.5 4.3 %collective-permute-start.24 = (bf16[16,2048]{1,0:T(8,128)(2,1)S(1)}, bf16[16,2048]{1,0:T(8,128)(2,1)S(1)}, u32[]{:S(2)}, u32[]{:S(2)}) collective-permute-start(bf16[16,2048]{1,0:T(8,128)(2,1)S(1)} %collective-permute-done.23.rest_2_), channel_id=1, source_target_pairs={{0,4},{4,0},{8,12},{12,8},{16,20},{20,16},{24,28},{28,24},{1,5},{5... | collective-permute-start | bytes 196616 | tf_op jit(solution)/shard_map/ppermute | solution.py:24
  100.1 4.3 %collective-permute-start.26 = (bf16[16,2048]{1,0:T(8,128)(2,1)S(1)}, bf16[16,2048]{1,0:T(8,128)(2,1)S(1)}, u32[]{:S(2)}, u32[]{:S(2)}) collective-permute-start(bf16[16,2048]{1,0:T(8,128)(2,1)S(1)} %collective-permute-done.25.rest_4_), channel_id=1, source_target_pairs={{0,4},{4,0},{8,12},{12,8},{16,20},{20,16},{24,28},{28,24},{1,5},{5... | collective-permute-start | bytes 196616 | tf_op jit(solution)/shard_map/ppermute | solution.py:24
  101.6 4.3 %collective-permute-start.28 = (bf16[16,2048]{1,0:T(8,128)(2,1)S(1)}, bf16[16,2048]{1,0:T(8,128)(2,1)S(1)}, u32[]{:S(2)}, u32[]{:S(2)}) collective-permute-start(bf16[16,2048]{1,0:T(8,128)(2,1)S(1)} %collective-permute-done.27.rest_6_), channel_id=1, source_target_pairs={{0,4},{4,0},{8,12},{12,8},{16,20},{20,16},{24,28},{28,24},{1,5},{5... | collective-permute-start | bytes 196616 | tf_op jit(solution)/shard_map/ppermute | solution.py:24
  110.9 1.9 %collective-permute-start.29 = (f32[16,512]{1,0:T(8,128)S(1)}, f32[16,512]{1,0:T(8,128)S(1)}, u32[]{:S(2)}, u32[]{:S(2)}) collective-permute-start(f32[16,512]{1,0:T(8,128)S(1)} %get-tuple-element.38), channel_id=1, source_target_pairs={{0,1},{1,0},{2,3},{3,2},{4,5},{5,4},{6,7},{7,6},{8,9},{9,8},{10,11... | collective-permute-start | bytes 98312 | tf_op jit(solution)/shard_map/ppermute | solution.py:24
  110.9 4.3 %collective-permute-start.30 = (f32[16,512]{1,0:T(8,128)S(1)}, f32[16,512]{1,0:T(8,128)S(1)}, u32[]{:S(2)}, u32[]{:S(2)}) collective-permute-start(f32[16,512]{1,0:T(8,128)S(1)} %get-tuple-element.39), channel_id=1, source_target_pairs={{0,2},{1,3},{2,0},{3,1},{4,6},{5,7},{6,4},{7,5},{8,10},{9,11},{10,... | collective-permute-start | bytes 98312 | tf_op jit(solution)/shard_map/ppermute | solution.py:24
  111.6 3.7 %collective-permute-start.31 = (f32[16,512]{1,0:T(8,128)S(1)}, f32[16,512]{1,0:T(8,128)S(1)}, u32[]{:S(2)}, u32[]{:S(2)}) collective-permute-start(f32[16,512]{1,0:T(8,128)S(1)} %get-tuple-element.40), channel_id=1, source_target_pairs={{0,3},{1,2},{2,1},{3,0},{4,7},{5,6},{6,5},{7,4},{8,11},{9,10},{10,... | collective-permute-start | bytes 98312 | tf_op jit(solution)/shard_map/ppermute | solution.py:24
